TPU v7x, 256 devices: a whole 4x4x8 slice. The times are simulated.
256 devices in a mesh: lat: 64 (over y, z, core), lev: 4 (over x).
Axes of the slice: x: 4, y: 4, z: 8, core: 2. Of those that a mesh axis runs over, the one named last changes fastest.
Arguments:
- fourier: bfloat16 [1280, 2, 64, 2, 640], P('lat', None, 'lev'), may hold values from -6 to 6
- quadrature: float32 [1280], P('lat'), may hold values from 0.3 to 3
- counts: int32 [1280], replicated, may hold values from 4 to 2576, as said below
- folded: int32 [640], replicated, may hold values from 0 to 639, as said below
- basis: bfloat16 [640, 640, 640], P('lat'), may hold values from -0.25 to 0.25
- vertical: bfloat16 [64, 64], P('lev'), may hold values from -0.75 to 0.75
- damping: float32 [640], replicated, may hold values from 0.2 to 1
Outputs:
- spectral: bfloat16 [640, 2, 64, 2, 640], P('lat', None, 'lev')
- grid: bfloat16 [1280, 2, 64, 2, 640], P('lat', None, 'lev')
Inputs may be any that keep to these rules, and one draw needn't show every extreme that they name: `counts`: each count is a multiple of 4 and at most 20 + 4 min(j, 1279 - j) for latitude j; the two equatorial latitudes reach that bound and the two polar ones hold 4 points. folded is a permutation of the wavenumbers; slots d * 10 to (d + 1) * 10 - 1 belong to index d of lat, and the wavenumbers of every such block have the same sum.
All inputs are finite; a program needn't handle non-finite values.
Results may differ from a plain program's by a relative error of at most 0.0069.
Values may be sent and summed in bfloat16 or wider, within the bound.
No kernel may reach another device: no remote copies, remote signals or barrier semaphores. Data moves between devices by JAX's collectives and lax.ppermute only.
A program may use at most 128 MiB of HBM per device.

v0:
```python
import jax
import jax.numpy as jnp
from jax import lax
from jax.sharding import PartitionSpec as P

FIELDS = 2


def mix_levels(spectral_out, vertical):
    return jnp.einsum(
        "lq,kfqcn->kflcn",
        vertical,
        lax.all_gather(spectral_out, "lev", axis=2, tiled=True),
        preferred_element_type=jnp.float32,
    )


def transform_pair(received, table, waves, vertical, damping):
    lat_total = received.shape[0]
    hemisphere = lat_total // 2
    batch = received.shape[1]
    slots = received.shape[2]
    wave_count = table.shape[2]
    degrees = jnp.arange(wave_count, dtype=jnp.int32)
    northern = received[:hemisphere].astype(jnp.float32)
    southern = received[hemisphere:][::-1].astype(jnp.float32)
    symmetric = (northern + southern).astype(jnp.bfloat16)
    antisym = (northern - southern).astype(jnp.bfloat16)
    matching = ((degrees[None, :] + waves[:, None]) % 2 == 0)[:, None, :]
    from_sym = jnp.einsum("kjn,jbk->kbn", table, symmetric, preferred_element_type=jnp.float32)
    from_anti = jnp.einsum("kjn,jbk->kbn", table, antisym, preferred_element_type=jnp.float32)
    spectra = jnp.where(matching, from_sym, from_anti)
    spectra = jnp.where(degrees[None, None, :] >= waves[:, None, None], spectra, 0.0).astype(
        jnp.bfloat16
    )
    spectral_out = spectra.reshape(slots, FIELDS, -1, 2, wave_count)
    mixed = mix_levels(spectral_out, vertical)
    filtered = (mixed * damping).astype(jnp.bfloat16).reshape(slots, batch, wave_count)
    kept = jnp.where(matching, filtered, jnp.zeros_like(filtered))
    flipped = jnp.where(matching, jnp.zeros_like(filtered), filtered)
    even_part = jnp.einsum("kjn,kbn->kjb", table, kept, preferred_element_type=jnp.float32)
    odd_part = jnp.einsum("kjn,kbn->kjb", table, flipped, preferred_element_type=jnp.float32)
    north_out = (even_part + odd_part).astype(jnp.bfloat16)
    south_out = (even_part - odd_part).astype(jnp.bfloat16)[:, ::-1]
    rebuilt = jnp.concatenate([north_out, south_out], axis=1)
    lat_devices = lax.axis_size("lat")
    outgoing = rebuilt.reshape(slots, lat_devices, lat_total // lat_devices, batch)
    returned = lax.all_to_all(outgoing, "lat", split_axis=1, concat_axis=1, tiled=True)
    return (spectral_out, returned)


def on_device(fourier, quadrature, counts, folded, basis, vertical, damping):
    lat_rows = fourier.shape[0]
    wave_count = fourier.shape[4]
    batch = fourier.shape[1] * fourier.shape[2] * 2
    lat_devices = lax.axis_size("lat")
    per_device = wave_count // lat_devices
    my_index = lax.axis_index("lat")
    local_counts = lax.dynamic_slice_in_dim(counts, my_index * lat_rows, lat_rows)
    orders = jnp.arange(wave_count, dtype=jnp.int32)
    resolved = (2 * orders[None, :] < local_counts[:, None])[:, None, None, None, :]
    weighted = jnp.where(
        resolved, fourier.astype(jnp.float32) * quadrature[:, None, None, None, None], 0.0
    ).astype(jnp.bfloat16)
    ordered = jnp.take(weighted.reshape(lat_rows, batch, wave_count), folded, axis=2)
    ordered = ordered.reshape(lat_rows, batch, lat_devices, per_device)
    my_waves = lax.dynamic_slice_in_dim(folded, my_index * per_device, per_device)
    received = lax.all_to_all(ordered, "lat", split_axis=2, concat_axis=0, tiled=True)
    spectral, returned = transform_pair(received[:, :, 0, :], basis, my_waves, vertical, damping)
    slotted = jnp.transpose(returned, (2, 3, 1, 0)).reshape(lat_rows, batch, wave_count)
    inverse = jnp.zeros((wave_count,), jnp.int32).at[folded].set(orders)
    regrid = jnp.take(slotted, inverse, axis=2).reshape(fourier.shape)
    grid = jnp.where(resolved, regrid, jnp.zeros_like(regrid))
    return (spectral, grid)


def solution(mesh):
    return jax.shard_map(
        on_device,
        mesh=mesh,
        in_specs=(
            P("lat", None, "lev", None, None),
            P("lat"),
            P(),
            P(),
            P("lat", None, None),
            P("lev", None),
            P(),
        ),
        out_specs=(P("lat", None, "lev", None, None), P("lat", None, "lev", None, None)),
        check_vma=False,
    )
```

profile of v0, /device:TPU:1, one launch (start us, length us, event | category | flops | bytes accessed | tf_op | source)
XLA Modules:
  0.0 285.5 jit_solution(3461631233227705094)
XLA Ops:
  7.2 0.7 compare_and_fusion.1
  7.9 0.7 compare_select_fusion.1
  8.6 0.8 dynamic_slice.7
  9.4 3.5 %select_convert_fusion = bf16[20,2,16,2,640]{4,3,2,1,0:T(2,128)(2,1)S(1)} fusion(bf16[20,2,16,2,640]{4,3,2,1,0:T(2,128)(2,1)} %param.9, pred[20,640]{1,0:T(8,128)(4,1)S(1)} %broadcast_compare_fusion, f32[20]{0:T(128)} %param.10), kind=kLoop, calls=%fused_computation.6 | loop fusion | flops 3276800 | bytes 3289680 | tf_op jit(solution)/shard_map/convert_element_type | solution.py:64
  12.9 0.7 reshape.115
  13.6 3.9 %copy.67 = bf16[20,64,640]{1,0,2:T(8,128)(2,1)} copy(bf16[20,64,640]{2,1,0:T(8,128)(2,1)S(1)} %reshape.115) | data formatting | bytes 3276800 | tf_op jit(solution)/shard_map/reshape | solution.py:65
  17.5 5.5 %gather_fusion = bf16[640,20,64]{2,1,0:T(8,128)(2,1)} fusion(bf16[20,64,640]{1,0,2:T(8,128)(2,1)} %copy.67, s32[1024]{0:T(1024)S(1)} %pad_clamp_fusion.1), kind=kCustom, calls=%fused_computation.clone | custom fusion | bytes 3279360 | tf_op jit(solution)/shard_map/jit(_take)/gather | solution.py:65
  23.0 5.0 %broadcast_select_fusion = bf16[640,20,64]{2,1,0:T(8,128)(2,1)} fusion(bf16[640,20,64]{2,1,0:T(8,128)(2,1)} %gather_fusion, pred[640]{0:T(1024)(128)(4,1)S(1)} %compare_and_fusion.1), kind=kLoop, calls=%fused_computation.4 | loop fusion | flops 819200 | bytes 3277440 | tf_op jit(solution)/shard_map/jit(_take)/select_n | solution.py:65
  28.0 6.8 %reshape.157 = bf16[64,2,6400]{2,1,0:T(2,128)(2,1)} reshape(bf16[64,10,20,64]{3,2,1,0:T(8,128)(2,1)} %bitcast.41) | data formatting | bytes 3276800
  34.8 13.2 %all-to-all-start = ((bf16[64,2,6400]{2,1,0:T(2,128)(2,1)}), bf16[64,2,6400]{2,1,0:T(2,128)(2,1)S(1)}, u32[]{:S(2)}, u32[]{:S(2)}) async-start(bf16[64,2,6400]{2,1,0:T(2,128)(2,1)} %reshape.157), calls=%async_computation | async-start | bytes 3276800 | tf_op jit(solution)/shard_map/all_to_all | solution.py:68
  48.0 0.2 all-gather.2.cloned.1.call-start
  48.2 0.8 dynamic_slice.6
  49.1 40.1 %all-to-all-done = bf16[64,2,6400]{2,1,0:T(2,128)(2,1)S(1)} async-done(((bf16[64,2,6400]{2,1,0:T(2,128)(2,1)}), bf16[64,2,6400]{2,1,0:T(2,128)(2,1)S(1)}, u32[]{:S(2)}, u32[]{:S(2)}) %all-to-all-start) | async-done | bytes 1638432 | tf_op jit(solution)/shard_map/all_to_all | solution.py:68
  89.1 4.2 %reshape.158 = bf16[64,10,20,64]{3,2,1,0:T(8,128)(2,1)} reshape(bf16[64,2,6400]{2,1,0:T(2,128)(2,1)S(1)} %all-to-all-done) | data formatting | bytes 3276800
  93.4 3.0 %copy.82 = bf16[20,64,64,10]{1,2,3,0:T(8,128)(2,1)S(1)} copy(bf16[20,64,64,10]{1,0,3,2:T(8,128)(2,1)} %bitcast.40) | data formatting | bytes 3276800 | tf_op jit(solution)/shard_map/all_to_all | solution.py:68
  96.4 2.4 fusion.26
  98.7 1.1 copy.70
  99.8 1.6 slice.12
  101.5 1.8 copy.71
  103.3 0.9 rev.6
  104.2 5.8 %copy.69 = f32[32,20,64,1,10]{2,1,0,4,3:T(8,128)} copy(f32[32,20,64,1,10]{2,0,4,3,1:T(8,128)} %get-tuple-element.6) | data formatting | bytes 3276800 | tf_op jit(solution)/shard_map/convert_element_type | solution.py:25
  110.0 4.6 %reshape.122 = f32[640,64,10]{1,0,2:T(8,128)} reshape(f32[32,20,64,1,10]{2,1,0,4,3:T(8,128)} %copy.69) | data formatting | bytes 3276800 | tf_op jit(solution)/shard_map/convert_element_type | solution.py:25
  114.6 2.6 copy.72
  117.2 4.9 %fusion.6 = bf16[10,64,640]{2,1,0:T(8,128)(2,1)S(1)} fusion(bf16[10,640,640]{2,1,0:T(8,128)(2,1)} %param.13, f32[640,64,10]{0,1,2:T(8,128)S(1)} %copy.72, bf16[640,64,10]{0,1,2:T(8,128)(2,1)S(1)} %rev.6), kind=kOutput, calls=%fused_computation.21 | convolution fusion | flops 525516800 | bytes 11468800 | tf_op jit(solution)/shard_map/kjn,jbk->kbn/dot_general | solution.py:30
  122.1 4.9 %select_convert_fusion.1 = bf16[10,64,640]{2,1,0:T(8,128)(2,1)S(1)} fusion(bf16[10,64,640]{2,1,0:T(8,128)(2,1)S(1)} %fusion.6, bf16[10,640,640]{2,1,0:T(8,128)(2,1)} %param.13, f32[640,64,10]{0,1,2:T(8,128)S(1)} %copy.72, bf16[640,64,10]{0,1,2:T(8,128)(2,1)S(1)} %rev.6, pred[10,640]{1,0:T(8,128)(4,1)S(1)} %get-tuple-element.8, ...), kind=kOutput, calls=%fused_computation.17 | convolution fusion | flops 526336000 | bytes 12300800 | tf_op jit(solution)/shard_map/kjn,jbk->kbn/dot_general | solution.py:31
  126.9 0.3 reshape.117
  127.3 1.1 copy.74
  128.4 40.0 %all-gather.2.cloned.1.call-done = bf16[10,2,64,2,640]{4,2,3,1,0:T(8,128)(2,1)} async-done(((bf16[10,2,16,2,640]{4,2,3,1,0:T(8,128)(2,1)}), bf16[10,2,64,2,640]{4,2,3,1,0:T(8,128)(2,1)}) %all-gather.2.cloned.1.call-update) | async-done | bytes 3276816 | tf_op jit(solution)/shard_map/all_gather | solution.py:13
  168.4 2.5 fusion.2
  170.9 0.7 copy.75
  171.6 0.3 reshape.118
  171.9 6.1 %fusion.8 = f32[10,64,640]{2,1,0:T(8,128)S(1)} fusion(bf16[10,640,640]{2,1,0:T(8,128)(2,1)} %param.13, bf16[10,64,640]{2,1,0:T(8,128)(2,1)S(1)} %reshape.118, pred[10,640]{1,0:T(8,128)(4,1)S(1)} %get-tuple-element.8), kind=kOutput, calls=%fused_computation.22 | convolution fusion | flops 524697600 | bytes 10656000 | tf_op jit(solution)/shard_map/kjn,kbn->kjb/dot_general | solution.py:42
  178.0 6.1 %fusion.3 = (bf16[10,640,64]{1,2,0:T(8,128)(2,1)S(1)}, bf16[10,640,64]{1,2,0:T(8,128)(2,1)S(1)}) fusion(f32[10,64,640]{2,1,0:T(8,128)S(1)} %fusion.8, bf16[10,640,640]{2,1,0:T(8,128)(2,1)} %param.13, bf16[10,64,640]{2,1,0:T(8,128)(2,1)S(1)} %reshape.118, pred[10,640]{1,0:T(8,128)(4,1)S(1)} %get-tuple-element.8), kind=kOutput, calls=%fused_computation.19 | convolution fusion | flops 526336000 | bytes 12294400 | tf_op jit(solution)/shard_map/kjn,kbn->kjb/dot_general | solution.py:41
  184.1 0.9 rev.7
  184.9 1.3 pad_maximum_fusion
  186.3 3.3 %copy.76 = bf16[10,1280,64]{2,1,0:T(8,128)(2,1)S(1)} copy(bf16[10,1280,64]{1,2,0:T(8,128)(2,1)} %pad_maximum_fusion) | data formatting | bytes 3276800 | tf_op jit(solution)/shard_map/concatenate | solution.py:45
  189.6 3.2 %reshape.119 = bf16[10,64,20,64]{3,2,1,0:T(8,128)(2,1)} reshape(bf16[10,1280,64]{2,1,0:T(8,128)(2,1)S(1)} %copy.76) | data formatting | bytes 3276800 | tf_op jit(solution)/shard_map/reshape | solution.py:47
  192.8 4.7 %copy.83 = bf16[10,64,20,64]{3,2,0,1:T(8,128)(2,1)} copy(bf16[10,64,20,64]{3,2,1,0:T(8,128)(2,1)} %reshape.119) | data formatting | bytes 3276800 | tf_op jit(solution)/shard_map/reshape | solution.py:47
  197.5 6.8 %reshape.159 = bf16[64,2,6400]{2,1,0:T(2,128)(2,1)} reshape(bf16[64,10,20,64]{3,2,1,0:T(8,128)(2,1)} %bitcast.42) | data formatting | bytes 3276800
  204.2 10.7 %all-to-all-start.1 = ((bf16[64,2,6400]{2,1,0:T(2,128)(2,1)}), bf16[64,2,6400]{2,1,0:T(2,128)(2,1)S(1)}, u32[]{:S(2)}, u32[]{:S(2)}) async-start(bf16[64,2,6400]{2,1,0:T(2,128)(2,1)} %reshape.159), calls=%async_computation.1 | async-start | bytes 3276800 | tf_op jit(solution)/shard_map/all_to_all | solution.py:48
  215.0 4.1 %scatter_custom_fusion = s32[640]{0:T(1024)S(1)} fusion(s32[640]{0:T(1024)S(1)} %compare_select_fusion.1, s32[640]{0:T(1024)S(1)} %iota.21, s32[]{:T(128)} %constant.11.clone.1), kind=kCustom, calls=%fused_computation.48 | custom fusion | bytes 2564 | tf_op jit(solution)/shard_map/scatter | solution.py:71
  219.1 37.0 %all-to-all-done.1 = bf16[64,2,6400]{2,1,0:T(2,128)(2,1)S(1)} async-done(((bf16[64,2,6400]{2,1,0:T(2,128)(2,1)}), bf16[64,2,6400]{2,1,0:T(2,128)(2,1)S(1)}, u32[]{:S(2)}, u32[]{:S(2)}) %all-to-all-start.1) | async-done | bytes 1638432 | tf_op jit(solution)/shard_map/all_to_all | solution.py:48
  256.2 4.2 %reshape.160 = bf16[64,10,20,64]{3,2,1,0:T(8,128)(2,1)} reshape(bf16[64,2,6400]{2,1,0:T(2,128)(2,1)S(1)} %all-to-all-done.1) | data formatting | bytes 3276800
  260.4 5.5 %gather_fusion.1 = bf16[640,20,64]{2,1,0:T(8,128)(2,1)} fusion(bf16[20,64,640]{1,0,2:T(8,128)(2,1)} %bitcast.44, s32[1024]{0:T(1024)S(1)} %pad_clamp_fusion), kind=kCustom, calls=%fused_computation.1.clone | custom fusion | bytes 3279360 | tf_op jit(solution)/shard_map/jit(_take)/gather | solution.py:72
  265.9 5.0 %select_bitcast_fusion = bf16[20,64,640]{1,0,2:T(8,128)(2,1)} fusion(bf16[640,20,64]{2,1,0:T(8,128)(2,1)} %gather_fusion.1, pred[640]{0:T(1024)(128)(4,1)S(1)} %compare_and_fusion), kind=kLoop, calls=%fused_computation.3 | loop fusion | flops 819200 | bytes 3277440 | tf_op jit(solution)/shard_map/jit(_take)/select_n | solution.py:72
  270.9 4.5 %copy.78 = bf16[20,64,640]{2,1,0:T(8,128)(2,1)S(1)} copy(bf16[20,64,640]{1,0,2:T(8,128)(2,1)} %select_bitcast_fusion) | data formatting | bytes 3276800 | tf_op jit(solution)/shard_map/jit(_take)/select_n | solution.py:72
  275.4 0.7 reshape.121
  276.1 2.5 broadcast_select_fusion.1
  (15 shorter events, 0.3 us)
Async XLA Ops:
  7.2 161.3 %copy-start = (bf16[16,64]{1,0:T(8,128)(2,1)S(1)}, bf16[16,64]{1,0:T(8,128)(2,1)}, u32[]{:S(2)}) copy-start(bf16[16,64]{1,0:T(8,128)(2,1)} %param.14) | copy-start | bytes 6148
  34.8 54.4 %all-to-all-start = ((bf16[64,2,6400]{2,1,0:T(2,128)(2,1)}), bf16[64,2,6400]{2,1,0:T(2,128)(2,1)S(1)}, u32[]{:S(2)}, u32[]{:S(2)}) async-start(bf16[64,2,6400]{2,1,0:T(2,128)(2,1)} %reshape.157), calls=%async_computation | async-start | bytes 3276800 | tf_op jit(solution)/shard_map/all_to_all | solution.py:68
  48.0 120.5 %all-gather.2.cloned.1.call-start = ((), (), s32[]{:S(2)}) async-start(), calls=%async_computation.2 | async-start | bytes 4096000 | tf_op jit(solution)/shard_map/all_gather | solution.py:13
  126.9 41.5 %copy-start.2 = (f32[640]{0:T(1024)S(1)}, f32[640]{0:T(1024)}, u32[]{:S(2)}) copy-start(f32[640]{0:T(1024)} %param.15) | copy-start | bytes 7684
  127.2 43.7 %copy-start.1 = (bf16[10,2,16,2,640]{4,3,2,1,0:T(2,128)(2,1)}, bf16[10,2,16,2,640]{4,3,2,1,0:T(2,128)(2,1)S(1)}, u32[]{:S(2)}) copy-start(bf16[10,2,16,2,640]{4,3,2,1,0:T(2,128)(2,1)S(1)} %reshape.117) | copy-start | bytes 2457604
  204.2 51.9 %all-to-all-start.1 = ((bf16[64,2,6400]{2,1,0:T(2,128)(2,1)}), bf16[64,2,6400]{2,1,0:T(2,128)(2,1)S(1)}, u32[]{:S(2)}, u32[]{:S(2)}) async-start(bf16[64,2,6400]{2,1,0:T(2,128)(2,1)} %reshape.159), calls=%async_computation.1 | async-start | bytes 3276800 | tf_op jit(solution)/shard_map/all_to_all | solution.py:48
Sparse Core Ops, SparseCore 0:
  128.5 39.8 all-gather.1
where the time goes:
time: 287 us; the launch traced here: 285 us
  waiting for transfers between devices  117 us (41%)
  local copies, waits for them, and re-layouts  84.3 us (29%)
  matrix products  24.3 us (8%)
  starting transfers between devices  24.1 us (8%)
  other arithmetic  21.3 us (7%)
  between operations  14.3 us (5%)
    all_to_all x1, waiting for transfers between devices, on_device(): lax.all_to_all(ordered, 'lat', split_axis=2, concat_axis=0, tiled=True)  40.1 us
    all_gather x1, waiting for transfers between devices, mix_levels(): lax.all_gather(spectral_out, 'lev', axis=2, tiled=True)  40 us
    all_to_all x1, waiting for transfers between devices, transform_pair(): lax.all_to_all(outgoing, 'lat', split_axis=1, concat_axis=1, tiled=True)  37 us
    unnamed x10, local copies, waits for them, and re-layouts  22 us
    all_to_all x1, starting transfers between devices, on_device(): lax.all_to_all(ordered, 'lat', split_axis=2, concat_axis=0, tiled=True)  13.2 us
    convert_element_type x3, local copies, waits for them, and re-layouts, transform_pair(): northern = received[:hemisphere].astype(jnp.float32)  13 us
    all_to_all x1, starting transfers between devices, transform_pair(): lax.all_to_all(outgoing, 'lat', split_axis=1, concat_axis=1, tiled=True)  10.7 us
    reshape x2, local copies, waits for them, and re-layouts, transform_pair(): rebuilt.reshape(slots, lat_devices, lat_total // lat_devices, batch)  7.89 us
  transfers between devices with their start and end apart: 3, of which 3 were waited for; matrix products, arithmetic and copies ran while one was open for 2% of the time, Pallas kernels for 0%

commit v1 on v0

v1 whole, which is shorter than its diff:
```python
import numpy as np
import jax
import jax.numpy as jnp
from jax import lax
from jax.experimental import pallas as pl
from jax.experimental.pallas import tpu as pltpu
from jax.sharding import PartitionSpec as P

F32, BF16 = jnp.float32, jnp.bfloat16
AXES = ("lat", "lev")
OWN = 64
LEV = 4
ROWS = 20
SLOTS = 10
LOCAL = 16
WAVES = 640
HALF = 640
QUADS = 5
CHUNK = 26
STRIDE = LEV * CHUNK
TOTAL = OWN * STRIDE
VMEM = 60 * 1024 * 1024


def row_order():
    a, f, l, c = np.meshgrid(np.arange(4), np.arange(2), np.arange(LOCAL), np.arange(2), indexing="ij")
    source = ((a * 2 + f) * LOCAL + l) * 2 + c
    target = ((f * 2 + c) * 4 + a) * LOCAL + l
    out = np.zeros((256, 256), np.float32)
    out[target.ravel(), source.ravel()] = 1
    return out


def lane_orders():
    h, x, k, a, l = np.meshgrid(np.arange(2), np.arange(LEV), np.arange(2), np.arange(4), np.arange(LOCAL), indexing="ij")
    source = (((h * LEV + x) * 2 + k) * 4 + a) * LOCAL + l
    place = np.where(h == 0, a, 3 - a)
    there = np.zeros((1024, 1024), np.float32)
    back = np.zeros((1024, 1024), np.float32)
    for q in range(2):
        target = (((place * 2 + k) * 2 + q) * LEV + x) * LOCAL + l
        there[source.ravel(), target.ravel()] = np.where((h == 1) & (q == 1), -1, 1).ravel()
        same = h == q
        back[target[same], source[same]] = 1
    return there, back


def one_hot(folded_ref, hot):
    lanes = lax.broadcasted_iota(jnp.int32, (OWN, WAVES), 1)
    for k in range(SLOTS):
        hot[k * OWN : (k + 1) * OWN, :] = jnp.where(folded_ref[:, k : k + 1] == lanes, 1.0, 0.0).astype(BF16)


def low_lanes(rows):
    return lax.broadcasted_iota(jnp.int32, (rows, 128), 1) < 64


def outward(place, counts, quad, fourier, folded, order, out, hot, weighted, stage):
    quarter = pl.program_id(0)

    @pl.when(quarter == 0)
    def _():
        one_hot(folded, hot)
        stage[pl.ds(CHUNK - 1, OWN * LEV, stride=CHUNK), :] = jnp.zeros((OWN * LEV, 128), F32)

    lanes = 2 * lax.broadcasted_iota(jnp.int32, (64, WAVES), 1)
    for a in range(4):
        row = quarter * 4 + a
        count = counts[place[0] * ROWS + row]
        product = fourier[a].astype(F32) * quad[row]
        weighted[a * 64 : (a + 1) * 64, :] = jnp.where(lanes < count, product, 0.0).astype(BF16)
    ordered = jnp.dot(order[...], weighted[...], preferred_element_type=F32).astype(BF16)
    low = low_lanes(OWN)
    for pair in range(QUADS):
        both = lax.dot_general(
            hot[pair * 128 : (pair + 1) * 128, :], ordered, (((1,), (1,)), ((), ())), preferred_element_type=F32
        )
        first, second = both[:OWN], both[OWN:]
        for half in range(2):
            left, right = first[:, half * 128 : (half + 1) * 128], second[:, half * 128 : (half + 1) * 128]
            start = pair * QUADS + quarter
            stage[pl.ds(2 * half * CHUNK + start, OWN, stride=STRIDE), :] = jnp.where(
                low, left, pltpu.roll(right, 64, 1)
            )
            stage[pl.ds((2 * half + 1) * CHUNK + start, OWN, stride=STRIDE), :] = jnp.where(
                low, pltpu.roll(left, 64, 1), right
            )

    @pl.when(quarter == QUADS - 1)
    def _():
        out[...] = stage[...].astype(BF16)


def middle(waves, received, basis, there, back, vertical, damping, spectral, out, stage, mixed_up, columns, turn):
    slot = pl.program_id(0)
    half = OWN // 2
    group = QUADS * half

    @pl.when(slot == 0)
    def _():
        turn[...] = jnp.where(
            lax.broadcasted_iota(jnp.int32, (group, group), 0) + lax.broadcasted_iota(jnp.int32, (group, group), 1)
            == group - 1,
            1.0,
            0.0,
        ).astype(BF16)
        stage[...] = received[...].astype(F32)
        for pair in range(QUADS):
            for quarter in range(QUADS):
                rows = slice(pair * group + quarter * half, pair * group + (quarter + 1) * half)
                for side in range(2):
                    for x in range(LEV):
                        lanes = slice((side * LEV + x) * 128, (side * LEV + x + 1) * 128)
                        start = (side * half * LEV + x) * CHUNK + pair * QUADS + quarter
                        mixed_up[rows, lanes] = stage[pl.ds(start, half, stride=STRIDE), :].astype(BF16)
            rows = slice(pair * group, (pair + 1) * group)
            mixed_up[rows, 512:] = jnp.dot(turn[...], mixed_up[rows, 512:], preferred_element_type=F32).astype(BF16)
        for pair in range(QUADS):
            rows = slice(pair * group, (pair + 1) * group)
            sums = jnp.dot(mixed_up[rows, :], there[...], preferred_element_type=F32)
            for quarter in range(QUADS):
                for a in range(4):
                    for k in range(2):
                        columns[2 * pair + k, pl.ds(quarter * 4 + a, half, stride=ROWS), :] = sums[
                            quarter * half : (quarter + 1) * half, (a * 2 + k) * 128 : (a * 2 + k + 1) * 128
                        ]

    wave = waves[slot]
    table = basis[0]
    both = columns[slot].T.astype(BF16)
    products = jnp.dot(both, table, preferred_element_type=F32)
    degrees = lax.broadcasted_iota(jnp.int32, (64, WAVES), 1)
    matching = (degrees + wave) % 2 == 0
    spectra = jnp.where(matching, products[:64], products[64:])
    spectra = jnp.where(degrees >= wave, spectra, 0.0).astype(BF16)
    for x in range(LEV):
        spectral[x, 0] = spectra[x * LOCAL : (x + 1) * LOCAL]
    filtered = jnp.dot(vertical[...], spectra, preferred_element_type=F32) * damping[...]
    signed = jnp.where(matching, filtered, -filtered)
    stacked = jnp.concatenate([filtered, signed], axis=0).astype(BF16)
    columns[slot] = lax.dot_general(table, stacked, (((1,), (1,)), ((), ())), preferred_element_type=F32)

    @pl.when(slot == SLOTS - 1)
    def _():
        stage[pl.ds(CHUNK - 1, OWN * LEV, stride=CHUNK), :] = jnp.zeros((OWN * LEV, 128), F32)
        for pair in range(QUADS):
            for quarter in range(QUADS):
                rows = slice(pair * group + quarter * half, pair * group + (quarter + 1) * half)
                for a in range(4):
                    for k in range(2):
                        mixed_up[rows, (a * 2 + k) * 128 : (a * 2 + k + 1) * 128] = columns[
                            2 * pair + k, pl.ds(quarter * 4 + a, half, stride=ROWS), :
                        ].astype(BF16)
        for pair in range(QUADS):
            rows = slice(pair * group, (pair + 1) * group)
            moved = jnp.dot(mixed_up[rows, :], back[...], preferred_element_type=F32)
            south = jnp.dot(turn[...], moved[:, 512:].astype(BF16), preferred_element_type=F32)
            for quarter in range(QUADS):
                part = slice(quarter * half, (quarter + 1) * half)
                for x in range(LEV):
                    start = x * CHUNK + pair * QUADS + quarter
                    lanes = slice(x * 128, (x + 1) * 128)
                    stage[pl.ds(start, half, stride=STRIDE), :] = moved[part, lanes]
                    stage[pl.ds(half * STRIDE + start, half, stride=STRIDE), :] = south[part, lanes]
        out[...] = stage[...].astype(BF16)


def homeward(place, counts, received, folded, order, grid, hot, slots, stage):
    quarter = pl.program_id(0)

    @pl.when(quarter == 0)
    def _():
        one_hot(folded, hot)
        stage[...] = received[...].astype(F32)

    low = low_lanes(OWN)
    for pair in range(QUADS):
        for half in range(2):
            start = pair * QUADS + quarter
            left = stage[pl.ds(2 * half * CHUNK + start, OWN, stride=STRIDE), :]
            right = stage[pl.ds((2 * half + 1) * CHUNK + start, OWN, stride=STRIDE), :]
            lanes = slice(half * 128, (half + 1) * 128)
            slots[(2 * pair) * OWN : (2 * pair + 1) * OWN, lanes] = jnp.where(
                low, left, pltpu.roll(right, 64, 1)
            ).astype(BF16)
            slots[(2 * pair + 1) * OWN : (2 * pair + 2) * OWN, lanes] = jnp.where(
                low, pltpu.roll(left, 64, 1), right
            ).astype(BF16)
    turned = lax.dot_general(
        order[...], slots[...], (((1,), (1,)), ((), ())), preferred_element_type=F32
    ).astype(BF16)
    values = jnp.dot(turned, hot[...], preferred_element_type=F32)
    lanes = 2 * lax.broadcasted_iota(jnp.int32, (64, WAVES), 1)
    for a in range(4):
        count = counts[place[0] * ROWS + quarter * 4 + a]
        grid[a] = jnp.where(lanes < count, values[a * 64 : (a + 1) * 64], 0.0).astype(BF16)


def smem():
    return pl.BlockSpec(memory_space=pltpu.SMEM)


def fixed(shape):
    return pl.BlockSpec(shape, lambda i: (0,) * len(shape))


def exchange(blocks):
    blocks = blocks.reshape(TOTAL // 2, 2, 128).reshape(OWN * LEV, CHUNK // 2, 2, 128)
    blocks = lax.all_to_all(blocks, AXES, split_axis=0, concat_axis=0, tiled=True)
    return blocks.reshape(TOTAL // 2, 2, 128).reshape(TOTAL, 128)


def on_device(fourier, quadrature, counts, folded, basis, vertical, damping):
    place = lax.axis_index("lat").astype(jnp.int32)
    params = pltpu.CompilerParams(vmem_limit_bytes=VMEM, dimension_semantics=("arbitrary",))
    whole_vertical = lax.all_gather(vertical, "lev", axis=0, tiled=True)
    owners = folded.reshape(OWN, SLOTS)
    my_waves = lax.dynamic_slice_in_dim(folded, place * SLOTS, SLOTS)
    order = row_order()
    there, back = lane_orders()
    place = place[None]

    sent = pl.pallas_call(
        outward,
        grid=(QUADS,),
        in_specs=[
            smem(),
            smem(),
            smem(),
            pl.BlockSpec((4, 64, WAVES), lambda i: (i, 0, 0)),
            fixed((OWN, SLOTS)),
            fixed((256, 256)),
        ],
        out_specs=fixed((TOTAL, 128)),
        out_shape=jax.ShapeDtypeStruct((TOTAL, 128), BF16),
        scratch_shapes=[
            pltpu.VMEM((WAVES, WAVES), BF16),
            pltpu.VMEM((256, WAVES), BF16),
            pltpu.VMEM((TOTAL, 128), F32),
        ],
        compiler_params=params,
    )(place, counts, quadrature, fourier.reshape(ROWS, 64, WAVES), owners, jnp.asarray(order, BF16))

    received = exchange(sent)

    spectral, sent = pl.pallas_call(
        middle,
        grid=(SLOTS,),
        in_specs=[
            smem(),
            fixed((TOTAL, 128)),
            pl.BlockSpec((1, HALF, WAVES), lambda i: (i, 0, 0)),
            fixed((1024, 1024)),
            fixed((1024, 1024)),
            fixed((64, 64)),
            fixed((1, WAVES)),
        ],
        out_specs=[pl.BlockSpec((LEV, 1, LOCAL, WAVES), lambda i: (0, i, 0, 0)), fixed((TOTAL, 128))],
        out_shape=[
            jax.ShapeDtypeStruct((LEV, SLOTS, LOCAL, WAVES), BF16),
            jax.ShapeDtypeStruct((TOTAL, 128), BF16),
        ],
        scratch_shapes=[
            pltpu.VMEM((TOTAL, 128), F32),
            pltpu.VMEM((800, 1024), BF16),
            pltpu.VMEM((SLOTS, HALF, 128), F32),
            pltpu.VMEM((160, 160), BF16),
        ],
        compiler_params=params,
    )(
        my_waves,
        received,
        basis,
        jnp.asarray(there, BF16),
        jnp.asarray(back, BF16),
        whole_vertical,
        damping.reshape(1, WAVES),
    )

    received = exchange(sent)
    parts = lax.all_to_all(spectral, "lev", split_axis=0, concat_axis=0, tiled=True)
    parts = parts.reshape(2, 2, SLOTS, LOCAL, WAVES).transpose(2, 0, 3, 1, 4)

    grid = pl.pallas_call(
        homeward,
        grid=(QUADS,),
        in_specs=[smem(), smem(), fixed((TOTAL, 128)), fixed((OWN, SLOTS)), fixed((256, 256))],
        out_specs=pl.BlockSpec((4, 64, WAVES), lambda i: (i, 0, 0)),
        out_shape=jax.ShapeDtypeStruct((ROWS, 64, WAVES), BF16),
        scratch_shapes=[
            pltpu.VMEM((WAVES, WAVES), BF16),
            pltpu.VMEM((WAVES, 256), BF16),
            pltpu.VMEM((TOTAL, 128), F32),
        ],
        compiler_params=params,
    )(place, counts, received, owners, jnp.asarray(order.T, BF16))
    return parts, grid.reshape(ROWS, 2, LOCAL, 2, WAVES)


def solution(mesh):
    return jax.shard_map(
        on_device,
        mesh=mesh,
        in_specs=(
            P("lat", None, "lev", None, None),
            P("lat"),
            P(),
            P(),
            P("lat", None, None),
            P("lev", None),
            P(),
        ),
        out_specs=(P("lat", None, "lev", None, None), P("lat", None, "lev", None, None)),
        check_vma=False,
    )
```

time: 287 us -> 180 us (0.63)
  local copies, waits for them, and re-layouts: 84.3 us -> 16.6 us
  waiting for transfers between devices: 117 us -> 79.1 us
  Pallas kernels: 0 us -> 34.3 us
  blocking collectives: 0 us -> 25.6 us
  matrix products: 24.3 us -> 0 us
  other arithmetic: 21.3 us -> 0 us
  between operations: 14.3 us -> 0.66 us
    all_gather x1 -> x0, waiting for transfers between devices: 40 us -> none  [mix_levels(): lax.all_gather(spectral_out, 'lev', axis=2, tiled=True)]
    pallas_call x0 -> x3, Pallas kernels: none -> 34.3 us  [the longest x1 20.1 us: on_device(): pl.pallas_call(middle, grid=(SLOTS,), in_specs=[smem(), fixed((TOTAL, 128...]
    dot_general x5 -> x0, matrix products: 24.3 us -> none  [the longest x1 6.07 us: transform_pair(): jnp.einsum('kjn,kbn->kjb', table, kept, preferred_element_type=jnp.float32)]
    unnamed x10 -> x8, local copies, waits for them, and re-layouts: 22 us -> 2.45 us
    all_to_all x0 -> x1, blocking collectives: none -> 15 us  [on_device(): lax.all_to_all(spectral, 'lev', split_axis=0, concat_axis=0, tiled=True)]
    convert_element_type x4 -> x0, local copies, waits for them, and re-layouts: 13.7 us -> none  [the longest x3 13 us: transform_pair(): northern = received[:hemisphere].astype(jnp.float32)]
    select_n x5 -> x0, other arithmetic: 13.2 us -> none  [the longest x2 5.7 us: on_device(): jnp.take(weighted.reshape(lat_rows, batch, wave_count), folded, axis=2)]
    gather x2 -> x0, local copies, waits for them, and re-layouts: 11 us -> none  [the longest x1 5.49 us: on_device(): jnp.take(weighted.reshape(lat_rows, batch, wave_count), folded, axis=2)]
  transfers between devices with their start and end apart: 3 -> 2, of which waited for: 3 -> 2; matrix products, arithmetic and copies ran while one was open for 2% -> 2% of each run, Pallas kernels for 0% -> 0%
where the time goes in v1:
time: 180 us; the launch traced here: 179 us
  waiting for transfers between devices  79.1 us (44%)
  Pallas kernels  34.3 us (19%)
  blocking collectives  25.6 us (14%)
  starting transfers between devices  22.8 us (13%)
  local copies, waits for them, and re-layouts  16.6 us (9%)
    all_to_all x2, waiting for transfers between devices, exchange(): lax.all_to_all(blocks, AXES, split_axis=0, concat_axis=0, tiled=True)  79.1 us
    all_to_all x2, starting transfers between devices, exchange(): lax.all_to_all(blocks, AXES, split_axis=0, concat_axis=0, tiled=True)  22.8 us
    pallas_call x1, Pallas kernels, on_device(): pl.pallas_call(middle, grid=(SLOTS,), in_specs=[smem(), fixed((TOTAL, 128...  20.1 us
    all_to_all x1, blocking collectives, on_device(): lax.all_to_all(spectral, 'lev', split_axis=0, concat_axis=0, tiled=True)  15 us
    all_gather x1, blocking collectives, on_device(): whole_vertical = lax.all_gather(vertical, 'lev', axis=0, tiled=True)  10.6 us
    pallas_call x1, Pallas kernels, on_device(): pl.pallas_call(outward, grid=(QUADS,), in_specs=[smem(), smem(), smem(),...  7.66 us
    pallas_call x1, Pallas kernels, on_device(): pl.pallas_call(homeward, grid=(QUADS,), in_specs=[smem(), smem(), fixed((...  6.54 us
    reshape x1, local copies, waits for them, and re-layouts, on_device(): fourier.reshape(ROWS, 64, WAVES)  4.69 us
  transfers between devices with their start and end apart: 2, of which 2 were waited for; matrix products, arithmetic and copies ran while one was open for 2% of the time, Pallas kernels for 0%

profile of v1, /device:TPU:1, one launch (start us, length us, event | category | flops | bytes accessed | tf_op | source)
XLA Modules:
  0.0 179.1 jit_solution(13735591883015170839)
XLA Ops:
  0.6 1.4 reshape.20.folded
  2.1 4.7 %reshape.19.fourier = bf16[20,64,640]{2,1,0:T(8,128)(2,1)} reshape(bf16[20,2,16,2,640]{4,3,2,1,0:T(2,128)(2,1)} %param.11) | data formatting | bytes 3276800 | tf_op jit(solution)/shard_map/reshape | solution.py:242
  6.8 7.7 %shard_map.122 = bf16[6656,128]{1,0:T(8,128)(2,1)} custom-call(s32[1]{0:T(128)} %bitcast.place, s32[1280]{0:T(1024)} %counts.3, f32[20]{0:T(128)} %quad.1, bf16[20,64,640]{2,1,0:T(8,128)(2,1)} %reshape.19.fourier, s32[64,10]{1,0:T(8,128)} %reshape.20.folded, bf16[256,256]{1,0:T(8,128)(2,1)} %constant.20.clone.order), custom_call_target="tpu_custom_call" | custom-call | tf_op jit(solution)/shard_map/pallas_call | solution.py:223
  14.4 0.0 copy-start.3
  14.4 0.0 copy-start.2
  14.4 15.7 %all-to-all-start = ((bf16[256,13,2,128]{3,2,1,0:T(2,128)(2,1)}), bf16[256,13,2,128]{3,2,1,0:T(2,128)(2,1)S(1)}, u32[]{:S(2)}, u32[]{:S(2)}) async-start(bf16[256,13,2,128]{3,2,1,0:T(2,128)(2,1)} %bitcast.11), calls=%async_computation | async-start | bytes 3407872 | tf_op jit(solution)/shard_map/all_to_all | solution.py:209
  30.1 1.3 dynamic_slice.3.waves
  31.4 0.0 copy-done.3
  31.4 0.6 reshape.21.damping
  32.0 0.0 copy-done.2
  32.0 10.6 %all_gather.3.vertical = bf16[64,64]{1,0:T(8,128)(2,1)} all-gather(bf16[16,64]{1,0:T(8,128)(2,1)S(1)} %copy-done.2), channel_id=1, replica_groups=mesh['lat'=64,'lev'=4] {'lev'}, dimensions={0}, use_global_device_ids=true | all-gather | bytes 10240 | tf_op jit(solution)/shard_map/all_gather | solution.py:216
  42.6 34.0 %all-to-all-done = bf16[256,13,2,128]{3,2,1,0:T(2,128)(2,1)S(1)} async-done(((bf16[256,13,2,128]{3,2,1,0:T(2,128)(2,1)}), bf16[256,13,2,128]{3,2,1,0:T(2,128)(2,1)S(1)}, u32[]{:S(2)}, u32[]{:S(2)}) %all-to-all-start) | async-done | bytes 1703968 | tf_op jit(solution)/shard_map/all_to_all | solution.py:209
  76.6 0.0 copy-start
  76.6 1.2 copy-done
  77.8 20.1 %shard_map.123 = (bf16[4,10,16,640]{3,2,1,0:T(8,128)(2,1)}, bf16[6656,128]{1,0:T(8,128)(2,1)}) custom-call(s32[10]{0:T(128)} %dynamic_slice.3.waves, bf16[6656,128]{1,0:T(8,128)(2,1)} %bitcast.9, bf16[10,640,640]{2,1,0:T(8,128)(2,1)} %basis.1, bf16[1024,1024]{1,0:T(8,128)(2,1)} %constant.21.clone.there, bf16[1024,1024]{1,0:T(8,128)(2,1)} %constant.22.clone.back, ...), custom_call_target="tpu_custom_call" | custom-call | tf_op jit(solution)/shard_map/pallas_call | solution.py:246
  98.0 15.0 %all_to_all.15 = bf16[4,10,16,640]{3,2,1,0:T(8,128)(2,1)S(1)} all-to-all(bf16[4,10,16,640]{3,2,1,0:T(8,128)(2,1)} %get-tuple-element.4), channel_id=1, replica_groups=mesh['lat'=64,'lev'=4] {'lev'}, dimensions={0} | all-to-all | bytes 1638400 | tf_op jit(solution)/shard_map/all_to_all | solution.py:281
  112.9 7.1 %all-to-all-start.2 = ((bf16[256,13,2,128]{3,2,1,0:T(2,128)(2,1)}), bf16[256,13,2,128]{3,2,1,0:T(2,128)(2,1)S(1)}, u32[]{:S(2)}, u32[]{:S(2)}) async-start(bf16[256,13,2,128]{3,2,1,0:T(2,128)(2,1)} %bitcast.13), calls=%async_computation.2 | async-start | bytes 3407872 | tf_op jit(solution)/shard_map/all_to_all | solution.py:209
  120.1 1.5 copy.16
  121.6 45.1 %all-to-all-done.2 = bf16[256,13,2,128]{3,2,1,0:T(2,128)(2,1)S(1)} async-done(((bf16[256,13,2,128]{3,2,1,0:T(2,128)(2,1)}), bf16[256,13,2,128]{3,2,1,0:T(2,128)(2,1)S(1)}, u32[]{:S(2)}, u32[]{:S(2)}) %all-to-all-start.2) | async-done | bytes 1703968 | tf_op jit(solution)/shard_map/all_to_all | solution.py:209
  166.8 0.0 copy-start.1
  166.8 1.2 copy-done.1
  168.0 6.5 %shard_map.124 = bf16[20,64,640]{2,1,0:T(8,128)(2,1)} custom-call(s32[1]{0:T(128)} %bitcast.place, s32[1280]{0:T(1024)} %counts.3, bf16[6656,128]{1,0:T(8,128)(2,1)} %bitcast.10, s32[64,10]{1,0:T(8,128)} %reshape.20.folded, bf16[256,256]{1,0:T(8,128)(2,1)} %constant.23.clone.order), custom_call_target="tpu_custom_call" | custom-call | tf_op jit(solution)/shard_map/pallas_call | solution.py:284
  174.5 4.5 %reshape.23 = bf16[20,2,16,2,640]{4,3,2,1,0:T(2,128)(2,1)} reshape(bf16[20,64,640]{2,1,0:T(8,128)(2,1)} %shard_map.124) | data formatting | bytes 3276800 | tf_op jit(solution)/shard_map/reshape | solution.py:297
Async XLA Ops:
  14.4 17.0 %copy-start.3 = (f32[640]{0:T(1024)S(1)}, f32[640]{0:T(1024)}, u32[]{:S(2)}) copy-start(f32[640]{0:T(1024)} %param.17) | copy-start | bytes 7684
  14.4 17.6 %copy-start.2 = (bf16[16,64]{1,0:T(8,128)(2,1)S(1)}, bf16[16,64]{1,0:T(8,128)(2,1)}, u32[]{:S(2)}) copy-start(bf16[16,64]{1,0:T(8,128)(2,1)} %param.16) | copy-start | bytes 6148
  14.4 62.2 %all-to-all-start = ((bf16[256,13,2,128]{3,2,1,0:T(2,128)(2,1)}), bf16[256,13,2,128]{3,2,1,0:T(2,128)(2,1)S(1)}, u32[]{:S(2)}, u32[]{:S(2)}) async-start(bf16[256,13,2,128]{3,2,1,0:T(2,128)(2,1)} %bitcast.11), calls=%async_computation | async-start | bytes 3407872 | tf_op jit(solution)/shard_map/all_to_all | solution.py:209
  76.6 1.2 copy-start
  112.9 53.8 %all-to-all-start.2 = ((bf16[256,13,2,128]{3,2,1,0:T(2,128)(2,1)}), bf16[256,13,2,128]{3,2,1,0:T(2,128)(2,1)S(1)}, u32[]{:S(2)}, u32[]{:S(2)}) async-start(bf16[256,13,2,128]{3,2,1,0:T(2,128)(2,1)} %bitcast.13), calls=%async_computation.2 | async-start | bytes 3407872 | tf_op jit(solution)/shard_map/all_to_all | solution.py:209
  166.8 1.2 copy-start.1

commit v2 on v1

v2 whole, which is shorter than its diff:
```python
import numpy as np
import jax
import jax.numpy as jnp
from jax import lax
from jax.experimental import pallas as pl
from jax.experimental.pallas import tpu as pltpu
from jax.sharding import PartitionSpec as P

F32, BF16 = jnp.float32, jnp.bfloat16
AXES = ("lat", "lev")
OWN = 64
HEMI = 32
LEV = 4
ROWS = 20
SLOTS = 10
LOCAL = 16
WAVES = 640
HALF = 640
QUADS = 5
GROUP = QUADS * HEMI
CHUNK = 26
STRIDE = LEV * CHUNK
TOTAL = OWN * STRIDE
VMEM = 28 * 1024 * 1024
ORDER = [d if d < HEMI else OWN - 1 + HEMI - d for d in range(OWN)]
GROUPS = [[d * LEV + x for d in ORDER for x in range(LEV)]]


def lane_order():
    x, k, a, l = np.meshgrid(np.arange(LEV), np.arange(2), np.arange(4), np.arange(LOCAL), indexing="ij")
    out = np.zeros((512, 512), np.float32)
    out[(((x * 2 + k) * 4 + a) * LOCAL + l).ravel(), (((a * 2 + k) * LEV + x) * LOCAL + l).ravel()] = 1
    return out


def low_lanes(rows):
    return lax.broadcasted_iota(jnp.int32, (rows, 128), 1) < 64


def nt(left, right):
    return lax.dot_general(left, right, (((1,), (1,)), ((), ())), preferred_element_type=F32)


def one_hot(folded, column, hot):
    row = folded[...].astype(F32).reshape(1, WAVES)
    for t in range(WAVES // 128):
        lanes = slice(t * 128, (t + 1) * 128)
        column[lanes, :] = jnp.broadcast_to(row[:, lanes], (128, 128)).T
    i = lax.broadcasted_iota(jnp.int32, (OWN, OWN), 0)
    d = lax.broadcasted_iota(jnp.int32, (OWN, OWN), 1)
    turn = jnp.where(d == jnp.where(i < HEMI, i, OWN - 1 + HEMI - i), 1.0, 0.0).astype(BF16)
    lanes = lax.broadcasted_iota(jnp.int32, (OWN, 128), 1)
    for k in range(SLOTS):
        waves = column[pl.ds(k, OWN, stride=SLOTS), :].astype(jnp.int32)
        plain = jnp.concatenate(
            [jnp.where(waves == lanes + t * 128, 1.0, 0.0).astype(BF16) for t in range(WAVES // 128)], axis=1
        )
        hot[k * OWN : (k + 1) * OWN, :] = jnp.dot(turn, plain, preferred_element_type=F32).astype(BF16)


def outward(place, counts, quad, fourier, folded, vertical, out, hot, weighted, stage, column, couple):
    quarter = pl.program_id(0)
    south = place[0] >= HEMI
    where = jnp.where(south, QUADS - 1 - quarter, quarter)

    @pl.when(quarter == 0)
    def _():
        one_hot(folded, column, hot)
        couple[...] = vertical[...].astype(F32)
        piece = 2 * lax.rem(place[0], 8)
        line = jnp.concatenate([couple[pl.ds(piece, 1), :], couple[pl.ds(piece + 1, 1), :]], axis=1)
        stage[pl.ds(CHUNK - 1, OWN * LEV, stride=CHUNK), :] = jnp.broadcast_to(line, (OWN * LEV, 128))

    lanes = 2 * lax.broadcasted_iota(jnp.int32, (LEV * LOCAL, WAVES), 1)
    for a in range(4):
        row = quarter * 4 + a
        count = counts[place[0] * ROWS + row]
        product = fourier[a].astype(F32) * quad[row]
        product = jnp.where(lanes < count, product, 0.0).astype(BF16)
        at = jnp.where(south, 3 - a, a)
        for x in range(LEV):
            weighted[pl.ds(pl.multiple_of((x * 4 + at) * LOCAL, LOCAL), LOCAL), :] = product[
                x * LOCAL : (x + 1) * LOCAL
            ]
    low = low_lanes(OWN)
    for pair in range(QUADS):
        both = nt(hot[pair * 128 : (pair + 1) * 128, :], weighted[...])
        first, second = both[:OWN], both[OWN:]
        for half in range(2):
            left, right = first[:, half * 128 : (half + 1) * 128], second[:, half * 128 : (half + 1) * 128]
            start = pair * QUADS + where
            stage[pl.ds(2 * half * CHUNK + start, OWN, stride=STRIDE), :] = jnp.where(
                low, left, pltpu.roll(right, 64, 1)
            )
            stage[pl.ds((2 * half + 1) * CHUNK + start, OWN, stride=STRIDE), :] = jnp.where(
                low, pltpu.roll(left, 64, 1), right
            )

    @pl.when(quarter == QUADS - 1)
    def _():
        out[...] = stage[...].astype(BF16)


def middle(
    place, folded, received, basis, order, damping, own, first, second, third, out, stage, sums, columns, turned, couple
):
    slot = pl.program_id(0)
    pair = slot // 2

    @pl.when(slot == 0)
    def _():
        stage[...] = received[...].astype(F32)
        for x in range(LEV):
            lines = stage[pl.ds(x * CHUNK + CHUNK - 1, 8, stride=STRIDE), :]
            couple[pl.ds(x * LOCAL, 8, stride=2), :] = lines
            couple[pl.ds(x * LOCAL + 1, 8, stride=2), :] = pltpu.roll(lines, 64, 1)

    @pl.when(slot % 2 == 0)
    def _():
        for quarter in range(QUADS):
            rows = slice(quarter * HEMI, (quarter + 1) * HEMI)
            for x in range(LEV):
                start = x * CHUNK + pair * QUADS + quarter
                lanes = slice(x * 128, (x + 1) * 128)
                north = stage[pl.ds(start, HEMI, stride=STRIDE), :]
                south = stage[pl.ds(HEMI * STRIDE + start, HEMI, stride=STRIDE), :]
                sums[0, rows, lanes] = (north + south).astype(BF16)
                sums[1, rows, lanes] = (north - south).astype(BF16)
        for side in range(2):
            placed = jnp.dot(sums[side], order[...], preferred_element_type=F32)
            for quarter in range(QUADS):
                for a in range(4):
                    columns[side, pl.ds(quarter * 4 + a, HEMI, stride=ROWS), :] = placed[
                        quarter * HEMI : (quarter + 1) * HEMI, a * 128 : (a + 1) * 128
                    ]
            across = columns[side].T.astype(BF16)
            for k in range(2):
                turned[k, side * 64 : (side + 1) * 64, :] = across[k * 64 : (k + 1) * 64]

    wave = folded[place[0] * SLOTS + slot]
    table = basis[0]
    odd = slot % 2
    products = jnp.dot(turned[odd], table, preferred_element_type=F32)
    degrees = lax.broadcasted_iota(jnp.int32, (64, WAVES), 1)
    matching = (degrees + wave) % 2 == 0
    spectra = jnp.where(matching, products[:64], products[64:])
    spectra = jnp.where(degrees >= wave, spectra, 0.0).astype(BF16)
    for x in range(LEV):
        piece = spectra[x * LOCAL : (x + 1) * LOCAL]
        ahead = lax.rem(x - place[1] + LEV, LEV)
        for o, ref in enumerate((own, first, second, third)):

            @pl.when(ahead == o)
            def _():
                ref[0] = piece

    filtered = jnp.dot(couple[:, :64].astype(BF16), spectra, preferred_element_type=F32) * damping[...].reshape(1, WAVES)
    signed = jnp.where(matching, filtered, -filtered)
    stacked = jnp.concatenate([filtered, signed], axis=0).astype(BF16)
    columns[odd] = nt(table, stacked)

    @pl.when(odd == 1)
    def _():
        low = low_lanes(HEMI)
        for quarter in range(QUADS):
            rows = slice(quarter * HEMI, (quarter + 1) * HEMI)
            for a in range(4):
                lanes = slice(a * 128, (a + 1) * 128)
                left = columns[0, pl.ds(quarter * 4 + a, HEMI, stride=ROWS), :]
                right = columns[1, pl.ds(quarter * 4 + a, HEMI, stride=ROWS), :]
                sums[0, rows, lanes] = jnp.where(low, left, pltpu.roll(right, 64, 1)).astype(BF16)
                sums[1, rows, lanes] = jnp.where(low, pltpu.roll(left, 64, 1), right).astype(BF16)
        for side in range(2):
            placed = nt(sums[side], order[...])
            for quarter in range(QUADS):
                for x in range(LEV):
                    start = (side * HEMI * LEV + x) * CHUNK + pair * QUADS + quarter
                    stage[pl.ds(start, HEMI, stride=STRIDE), :] = placed[
                        quarter * HEMI : (quarter + 1) * HEMI, x * 128 : (x + 1) * 128
                    ]

    @pl.when(slot == SLOTS - 1)
    def _():
        out[...] = stage[...].astype(BF16)


def homeward(place, counts, received, hot, grid, slots, stage):
    quarter = pl.program_id(0)
    south = place[0] >= HEMI
    where = jnp.where(south, QUADS - 1 - quarter, quarter)

    @pl.when(quarter == 0)
    def _():
        stage[...] = received[...].astype(F32)

    low = low_lanes(OWN)
    for pair in range(QUADS):
        for half in range(2):
            start = pair * QUADS + where
            left = stage[pl.ds(2 * half * CHUNK + start, OWN, stride=STRIDE), :]
            right = stage[pl.ds((2 * half + 1) * CHUNK + start, OWN, stride=STRIDE), :]
            lanes = slice(half * 128, (half + 1) * 128)
            slots[(2 * pair) * OWN : (2 * pair + 1) * OWN, lanes] = jnp.where(
                low, left, pltpu.roll(right, 64, 1)
            ).astype(BF16)
            slots[(2 * pair + 1) * OWN : (2 * pair + 2) * OWN, lanes] = jnp.where(
                low, pltpu.roll(left, 64, 1), right
            ).astype(BF16)
    values = jnp.dot(slots[...].T, hot[...], preferred_element_type=F32)
    lanes = 2 * lax.broadcasted_iota(jnp.int32, (LOCAL, WAVES), 1)
    for at in range(4):
        a = jnp.where(south, 3 - at, at)
        count = counts[place[0] * ROWS + quarter * 4 + a]
        for x in range(LEV):
            rows = slice((x * 4 + at) * LOCAL, (x * 4 + at + 1) * LOCAL)
            grid[a, x * LOCAL : (x + 1) * LOCAL, :] = jnp.where(lanes < count, values[rows], 0.0).astype(BF16)


def smem():
    return pl.BlockSpec(memory_space=pltpu.SMEM)


def fixed(*shape):
    return pl.BlockSpec(shape, lambda i: (0,) * len(shape))


def params(limit=VMEM):
    return pltpu.CompilerParams(vmem_limit_bytes=limit, dimension_semantics=("arbitrary",))


def call_outward(place, counts, quadrature, fourier, folded, vertical):
    return pl.pallas_call(
        outward,
        grid=(QUADS,),
        in_specs=[
            smem(),
            smem(),
            smem(),
            pl.BlockSpec((4, 64, WAVES), lambda i: (i, 0, 0)),
            fixed(WAVES),
            fixed(LOCAL, LEV * LOCAL),
        ],
        out_specs=[fixed(TOTAL, 128), fixed(WAVES, WAVES)],
        out_shape=[jax.ShapeDtypeStruct((TOTAL, 128), BF16), jax.ShapeDtypeStruct((WAVES, WAVES), BF16)],
        scratch_shapes=[
            pltpu.VMEM((256, WAVES), BF16),
            pltpu.VMEM((TOTAL, 128), F32),
            pltpu.VMEM((WAVES, 128), F32),
            pltpu.VMEM((LOCAL, LEV * LOCAL), F32),
        ],
        compiler_params=params(),
    )(place, counts, quadrature, fourier, folded, vertical)


def call_middle(place, folded, received, basis, damping):
    piece = pl.BlockSpec((1, LOCAL, WAVES), lambda i: (i, 0, 0))
    return pl.pallas_call(
        middle,
        grid=(SLOTS,),
        in_specs=[
            smem(),
            smem(),
            fixed(TOTAL, 128),
            pl.BlockSpec((1, HALF, WAVES), lambda i: (i, 0, 0)),
            fixed(512, 512),
            fixed(WAVES),
        ],
        out_specs=[piece] * LEV + [fixed(TOTAL, 128)],
        out_shape=[jax.ShapeDtypeStruct((SLOTS, LOCAL, WAVES), BF16)] * LEV
        + [jax.ShapeDtypeStruct((TOTAL, 128), BF16)],
        scratch_shapes=[
            pltpu.VMEM((TOTAL, 128), F32),
            pltpu.VMEM((2, GROUP, 512), BF16),
            pltpu.VMEM((2, HALF, 128), F32),
            pltpu.VMEM((2, 128, HALF), BF16),
            pltpu.VMEM((64, 128), F32),
        ],
        compiler_params=params(),
    )(place, folded, received, basis, jnp.asarray(lane_order(), BF16), damping)


def call_homeward(place, counts, received, hot):
    return pl.pallas_call(
        homeward,
        grid=(QUADS,),
        in_specs=[smem(), smem(), fixed(TOTAL, 128), fixed(WAVES, WAVES)],
        out_specs=pl.BlockSpec((4, 64, WAVES), lambda i: (i, 0, 0)),
        out_shape=jax.ShapeDtypeStruct((ROWS, 64, WAVES), BF16),
        scratch_shapes=[
            pltpu.VMEM((WAVES, 256), BF16),
            pltpu.VMEM((TOTAL, 128), F32),
        ],
        compiler_params=params(),
    )(place, counts, received, hot)


def exchange(blocks):
    blocks = blocks.reshape(TOTAL // 2, 2, 128).reshape(OWN * LEV, CHUNK // 2, 2, 128)
    blocks = lax.all_to_all(blocks, AXES, split_axis=0, concat_axis=0, tiled=True, axis_index_groups=GROUPS)
    return blocks.reshape(TOTAL // 2, 2, 128).reshape(TOTAL, 128)


def on_device(fourier, quadrature, counts, folded, basis, vertical, damping):
    lev = lax.axis_index("lev").astype(jnp.int32)
    place = jnp.stack([lax.axis_index("lat").astype(jnp.int32), lev])
    fourier = fourier.transpose(0, 1, 3, 2, 4).reshape(ROWS, 64, WAVES)
    sent, hot = call_outward(place, counts, quadrature, fourier, folded, vertical)
    *pieces, sent = call_middle(place, folded, exchange(sent), basis, damping)
    parts = pieces[:1] + [
        lax.ppermute(pieces[o], "lev", [(i, (i + o) % LEV) for i in range(LEV)]) for o in range(1, LEV)
    ]
    received = exchange(sent)
    parts = jnp.stack(parts)
    parts = jnp.stack([lax.dynamic_index_in_dim(parts, (lev - x) % LEV, 0, keepdims=False) for x in range(LEV)])
    spectral = parts.reshape(2, 2, SLOTS, LOCAL, WAVES).transpose(2, 0, 3, 1, 4)
    grid = call_homeward(place, counts, received, hot)
    return spectral, grid.reshape(ROWS, 2, 2, LOCAL, WAVES).transpose(0, 1, 3, 2, 4)


def solution(mesh):
    return jax.shard_map(
        on_device,
        mesh=mesh,
        in_specs=(
            P("lat", None, "lev", None, None),
            P("lat"),
            P(),
            P(),
            P("lat", None, None),
            P("lev", None),
            P(),
        ),
        out_specs=(P("lat", None, "lev", None, None), P("lat", None, "lev", None, None)),
        check_vma=False,
    )
```

time: 180 us -> 146 us (0.81)
  waiting for transfers between devices: 79.1 us -> 36.9 us
  blocking collectives: 25.6 us -> 60.4 us
  starting transfers between devices: 22.8 us -> 12 us
  local copies, waits for them, and re-layouts: 16.6 us -> 7.32 us
  Pallas kernels: 34.3 us -> 27 us
    all_to_all x2 -> x1, waiting for transfers between devices: 79.1 us -> 22.8 us  [exchange(): lax.all_to_all(blocks, AXES, split_axis=0, concat_axis=0, tiled=True, axi...]
    all_to_all x1, blocking collectives: 15 us -> 60.4 us  [exchange(): lax.all_to_all(blocks, AXES, split_axis=0, concat_axis=0, tiled=True, axi...]
    all_to_all x2 -> x1, starting transfers between devices: 22.8 us -> 6.95 us  [exchange(): lax.all_to_all(blocks, AXES, split_axis=0, concat_axis=0, tiled=True, axi...]
    ppermute x0 -> x3, waiting for transfers between devices: none -> 14.2 us  [on_device(): lax.ppermute(pieces[o], 'lev', [(i, (i + o) % LEV) for i in range(LEV)])]
    all_gather x1 -> x0, blocking collectives: 10.6 us -> none  [on_device(): whole_vertical = lax.all_gather(vertical, 'lev', axis=0, tiled=True)]
    reshape x5 -> x2, local copies, waits for them, and re-layouts: 12.8 us -> 4.31 us  [the longest x1 2.76 us: on_device(): grid.reshape(ROWS, 2, 2, LOCAL, WAVES).transpose(0, 1, 3, 2, 4)]
    pallas_call x3, Pallas kernels: 34.3 us -> 27 us  [the longest x1 17.3 us: call_middle(): pl.pallas_call(middle, grid=(SLOTS,), in_specs=[smem(), smem(), fixed(TOT...]
    ppermute x0 -> x3, starting transfers between devices: none -> 5.06 us  [on_device(): lax.ppermute(pieces[o], 'lev', [(i, (i + o) % LEV) for i in range(LEV)])]
  transfers between devices with their start and end apart: 2 -> 4, of which waited for: 2 -> 3; matrix products, arithmetic and copies ran while one was open for 2% -> 2% of each run, Pallas kernels for 0% -> 0%
where the time goes in v2:
time: 146 us
  blocking collectives  60.4 us (41%)
  waiting for transfers between devices  36.9 us (25%)
  Pallas kernels  27 us (18%)
  starting transfers between devices  12 us (8%)
  local copies, waits for them, and re-layouts  7.32 us (5%)
    all_to_all x1, blocking collectives, exchange(): lax.all_to_all(blocks, AXES, split_axis=0, concat_axis=0, tiled=True, axi...  60.4 us
    all_to_all x1, waiting for transfers between devices, exchange(): lax.all_to_all(blocks, AXES, split_axis=0, concat_axis=0, tiled=True, axi...  22.8 us
    pallas_call x1, Pallas kernels, call_middle(): pl.pallas_call(middle, grid=(SLOTS,), in_specs=[smem(), smem(), fixed(TOT...  17.3 us
    ppermute x3, waiting for transfers between devices, on_device(): lax.ppermute(pieces[o], 'lev', [(i, (i + o) % LEV) for i in range(LEV)])  14.2 us
    all_to_all x1, starting transfers between devices, exchange(): lax.all_to_all(blocks, AXES, split_axis=0, concat_axis=0, tiled=True, axi...  6.95 us
    pallas_call x1, Pallas kernels, call_outward(): pl.pallas_call(outward, grid=(QUADS,), in_specs=[smem(), smem(), smem(),...  5.34 us
    ppermute x3, starting transfers between devices, on_device(): lax.ppermute(pieces[o], 'lev', [(i, (i + o) % LEV) for i in range(LEV)])  5.06 us
    pallas_call x1, Pallas kernels, call_homeward(): pl.pallas_call(homeward, grid=(QUADS,), in_specs=[smem(), smem(), fixed(T...  4.44 us
  transfers between devices with their start and end apart: 4, of which 3 were waited for; matrix products, arithmetic and copies ran while one was open for 2% of the time, Pallas kernels for 0%

profile of v2, /device:TPU:1, one launch (start us, length us, event | category | flops | bytes accessed | tf_op | source)
XLA Modules:
  0.0 145.9 jit_solution(4159511489166322846)
XLA Ops:
  0.6 0.0 copy-start.2
  0.6 0.0 copy-start.3
  0.7 0.0 copy-start.4
  0.7 0.0 copy-start.6
  0.7 0.0 copy-start
  0.7 1.9 %copy.10 = bf16[20,2,2,16,640]{4,3,2,1,0:T(8,128)(2,1)S(1)} copy(bf16[20,2,2,16,640]{4,2,3,1,0:T(2,128)(2,1)} %bitcast.27) | data formatting | bytes 3276800 | tf_op jit(solution)/shard_map/transpose | solution.py:306
  2.6 0.1 pad_add_fusion.place
  2.6 0.0 copy-done.2
  2.6 0.0 copy-done.3
  2.6 0.0 copy-done.4
  2.6 0.0 copy-done.6
  2.7 5.3 %shard_map.95 = (bf16[6656,128]{1,0:T(8,128)(2,1)S(1)}, bf16[640,640]{1,0:T(8,128)(2,1)S(1)}) custom-call(s32[2]{0:T(128)S(1)} %pad_add_fusion.place, s32[1280]{0:T(1024)S(1)} %copy-done.2, f32[20]{0:T(128)S(1)} %copy-done.6, bf16[20,64,640]{2,1,0:T(8,128)(2,1)S(1)} %bitcast.22, s32[640]{0:T(1024)S(1)} %copy-done.3, bf16[16,64]{1,0:T(8,128)(2,1)S(1)} %copy-done.4), custom_call_target="tpu_custom_call" | custom-call | tf_op jit(solution)/shard_map/pallas_call | solution.py:232
  8.0 0.0 copy-start.5
  8.0 60.4 %all_to_all.10 = bf16[256,13,2,128]{3,2,1,0:T(2,128)(2,1)S(1)} all-to-all(bf16[256,13,2,128]{3,2,1,0:T(2,128)(2,1)S(1)} %bitcast.24), channel_id=1, replica_groups={{0,1,2,3,4,5,6,7,8,9,10,11,12,13,14,15,16,17,18,19,20,21,22,23,24,25,26..., dimensions={0} | all-to-all | bytes 3407872 | tf_op jit(solution)/shard_map/all_to_all | solution.py:299
  68.4 0.0 copy-done
  68.4 0.0 copy-done.5
  68.4 0.0 copy-start.1
  68.4 1.0 copy-done.1
  69.5 17.3 %shard_map.96 = (bf16[10,16,640]{2,1,0:T(8,128)(2,1)S(1)}, bf16[10,16,640]{2,1,0:T(8,128)(2,1)S(1)}, bf16[10,16,640]{2,1,0:T(8,128)(2,1)S(1)}, bf16[10,16,640]{2,1,0:T(8,128)(2,1)S(1)}, bf16[6656,128]{1,0:T(8,128)(2,1)}) custom-call(s32[2]{0:T(128)S(1)} %pad_add_fusion.place, s32[640]{0:T(1024)S(1)} %copy-done.3, bf16[6656,128]{1,0:T(8,128)(2,1)S(1)} %bitcast.21, ...), custom_call_target="tpu_custom_call" | custom-call | tf_op jit(solution)/shard_map/pallas_call | solution.py:257
  86.7 7.0 %all-to-all-start.1 = ((bf16[256,13,2,128]{3,2,1,0:T(2,128)(2,1)}), bf16[256,13,2,128]{3,2,1,0:T(2,128)(2,1)S(1)}, u32[]{:S(2)}, u32[]{:S(2)}) async-start(bf16[256,13,2,128]{3,2,1,0:T(2,128)(2,1)} %bitcast.12), calls=%async_computation.1 | async-start | bytes 3407872 | tf_op jit(solution)/shard_map/all_to_all | solution.py:299
  93.7 1.5 %collective-permute-start = (bf16[10,16,640]{2,1,0:T(8,128)(2,1)S(1)}, bf16[10,16,640]{2,1,0:T(8,128)(2,1)}, u32[]{:S(2)}, u32[]{:S(2)}) collective-permute-start(bf16[10,16,640]{2,1,0:T(8,128)(2,1)S(1)} %get-tuple-element.11), channel_id=1, source_target_pairs={{0,1},{1,2},{2,3},{3,0},{4,5},{5,6},{6,7},{7,4},{8,9},{9,10},{10,1... | collective-permute-start | bytes 614408 | tf_op jit(solution)/shard_map/ppermute | solution.py:310
  95.2 2.4 %collective-permute-start.1 = (bf16[10,16,640]{2,1,0:T(8,128)(2,1)S(1)}, bf16[10,16,640]{2,1,0:T(8,128)(2,1)}, u32[]{:S(2)}, u32[]{:S(2)}) collective-permute-start(bf16[10,16,640]{2,1,0:T(8,128)(2,1)S(1)} %get-tuple-element.12), channel_id=1, source_target_pairs={{0,2},{1,3},{2,0},{3,1},{4,6},{5,7},{6,4},{7,5},{8,10},{9,11},{10,... | collective-permute-start | bytes 614408 | tf_op jit(solution)/shard_map/ppermute | solution.py:310
  97.6 1.2 collective-permute-start.2
  98.8 3.8 %collective-permute-done = bf16[10,16,640]{2,1,0:T(8,128)(2,1)} collective-permute-done((bf16[10,16,640]{2,1,0:T(8,128)(2,1)S(1)}, bf16[10,16,640]{2,1,0:T(8,128)(2,1)}, u32[]{:S(2)}, u32[]{:S(2)}) %collective-permute-start) | collective-permute-done | bytes 204832 | tf_op jit(solution)/shard_map/ppermute | solution.py:310
  102.6 10.3 %collective-permute-done.1 = bf16[10,16,640]{2,1,0:T(8,128)(2,1)} collective-permute-done((bf16[10,16,640]{2,1,0:T(8,128)(2,1)S(1)}, bf16[10,16,640]{2,1,0:T(8,128)(2,1)}, u32[]{:S(2)}, u32[]{:S(2)}) %collective-permute-start.1) | collective-permute-done | bytes 204832 | tf_op jit(solution)/shard_map/ppermute | solution.py:310
  112.9 0.0 collective-permute-done.2
  112.9 1.2 pad_maximum_fusion
  114.2 0.1 constant_dynamic-slice_fusion.3
  114.3 0.1 pad_maximum_fusion.1
  114.4 1.5 %copy.16 = bf16[2,2,10,16,640]{4,1,3,0,2:T(2,128)(2,1)} copy(bf16[2,2,10,16,640]{4,3,2,1,0:T(8,128)(2,1)S(1)} %bitcast.26) | data formatting | bytes 1638400 | tf_op jit(solution)/shard_map/reshape | solution.py:315
  116.0 22.8 %all-to-all-done.1 = bf16[256,13,2,128]{3,2,1,0:T(2,128)(2,1)S(1)} async-done(((bf16[256,13,2,128]{3,2,1,0:T(2,128)(2,1)}), bf16[256,13,2,128]{3,2,1,0:T(2,128)(2,1)S(1)}, u32[]{:S(2)}, u32[]{:S(2)}) %all-to-all-start.1) | async-done | bytes 1703968 | tf_op jit(solution)/shard_map/all_to_all | solution.py:299
  138.7 4.4 %shard_map.97 = bf16[20,64,640]{2,1,0:T(8,128)(2,1)S(1)} custom-call(s32[2]{0:T(128)S(1)} %pad_add_fusion.place, s32[1280]{0:T(1024)S(1)} %copy-done.2, bf16[6656,128]{1,0:T(8,128)(2,1)S(1)} %bitcast.20, bf16[640,640]{1,0:T(8,128)(2,1)S(1)} %get-tuple-element.15.hot), custom_call_target="tpu_custom_call" | custom-call | tf_op jit(solution)/shard_map/pallas_call | solution.py:283
  143.2 2.8 %copy.15 = bf16[20,2,2,16,640]{4,2,3,1,0:T(2,128)(2,1)} copy(bf16[20,2,2,16,640]{4,3,2,1,0:T(8,128)(2,1)S(1)} %bitcast.23) | data formatting | bytes 3276800 | tf_op jit(solution)/shard_map/reshape | solution.py:317
Async XLA Ops:
  0.6 2.0 %copy-start.2 = (s32[1280]{0:T(1024)S(1)}, s32[1280]{0:T(1024)}, u32[]{:S(2)}) copy-start(s32[1280]{0:T(1024)} %counts.3) | copy-start | bytes 15364
  0.6 2.0 %copy-start.3 = (s32[640]{0:T(1024)S(1)}, s32[640]{0:T(1024)}, u32[]{:S(2)}) copy-start(s32[640]{0:T(1024)} %folded.3) | copy-start | bytes 7684
  0.7 2.0 %copy-start.4 = (bf16[16,64]{1,0:T(8,128)(2,1)S(1)}, bf16[16,64]{1,0:T(8,128)(2,1)}, u32[]{:S(2)}) copy-start(bf16[16,64]{1,0:T(8,128)(2,1)} %vertical.1) | copy-start | bytes 6148
  0.7 2.0 %copy-start.6 = (f32[20]{0:T(128)S(1)}, f32[20]{0:T(128)}, u32[]{:S(2)}) copy-start(f32[20]{0:T(128)} %quad.1) | copy-start | bytes 244
  0.7 67.7 %copy-start = (bf16[10,640,640]{2,1,0:T(8,128)(2,1)S(1)}, bf16[10,640,640]{2,1,0:T(8,128)(2,1)}, u32[]{:S(2)}) copy-start(bf16[10,640,640]{2,1,0:T(8,128)(2,1)} %basis.1) | copy-start | bytes 24576004
  8.0 60.4 %copy-start.5 = (f32[640]{0:T(1024)S(1)}, f32[640]{0:T(1024)}, u32[]{:S(2)}) copy-start(f32[640]{0:T(1024)} %damping.1) | copy-start | bytes 7684
  68.4 1.0 copy-start.1
  86.7 52.0 %all-to-all-start.1 = ((bf16[256,13,2,128]{3,2,1,0:T(2,128)(2,1)}), bf16[256,13,2,128]{3,2,1,0:T(2,128)(2,1)S(1)}, u32[]{:S(2)}, u32[]{:S(2)}) async-start(bf16[256,13,2,128]{3,2,1,0:T(2,128)(2,1)} %bitcast.12), calls=%async_computation.1 | async-start | bytes 3407872 | tf_op jit(solution)/shard_map/all_to_all | solution.py:299
  93.7 8.9 %collective-permute-start = (bf16[10,16,640]{2,1,0:T(8,128)(2,1)S(1)}, bf16[10,16,640]{2,1,0:T(8,128)(2,1)}, u32[]{:S(2)}, u32[]{:S(2)}) collective-permute-start(bf16[10,16,640]{2,1,0:T(8,128)(2,1)S(1)} %get-tuple-element.11), channel_id=1, source_target_pairs={{0,1},{1,2},{2,3},{3,0},{4,5},{5,6},{6,7},{7,4},{8,9},{9,10},{10,1... | collective-permute-start | bytes 614408 | tf_op jit(solution)/shard_map/ppermute | solution.py:310
  95.2 17.8 %collective-permute-start.1 = (bf16[10,16,640]{2,1,0:T(8,128)(2,1)S(1)}, bf16[10,16,640]{2,1,0:T(8,128)(2,1)}, u32[]{:S(2)}, u32[]{:S(2)}) collective-permute-start(bf16[10,16,640]{2,1,0:T(8,128)(2,1)S(1)} %get-tuple-element.12), channel_id=1, source_target_pairs={{0,2},{1,3},{2,0},{3,1},{4,6},{5,7},{6,4},{7,5},{8,10},{9,11},{10,... | collective-permute-start | bytes 614408 | tf_op jit(solution)/shard_map/ppermute | solution.py:310
  97.6 15.3 %collective-permute-start.2 = (bf16[10,16,640]{2,1,0:T(8,128)(2,1)S(1)}, bf16[10,16,640]{2,1,0:T(8,128)(2,1)}, u32[]{:S(2)}, u32[]{:S(2)}) collective-permute-start(bf16[10,16,640]{2,1,0:T(8,128)(2,1)S(1)} %get-tuple-element.13), channel_id=1, source_target_pairs={{0,3},{1,0},{2,1},{3,2},{4,7},{5,4},{6,5},{7,6},{8,11},{9,8},{10,9... | collective-permute-start | bytes 614408 | tf_op jit(solution)/shard_map/ppermute | solution.py:310

commit v3 on v0

v3 whole, which is shorter than its diff:
```python
import numpy as np
import jax
import jax.numpy as jnp
from jax import lax
from jax.experimental import pallas as pl
from jax.experimental.pallas import tpu as pltpu
from jax.sharding import PartitionSpec as P

F32, BF16 = jnp.float32, jnp.bfloat16
AXES = ("lat", "lev")
OWN = 64
HEMI = 32
LEV = 4
ROWS = 20
SLOTS = 10
LOCAL = 16
WAVES = 640
HALF = 640
QUADS = 5
GROUP = QUADS * HEMI
CHUNK = 26
STRIDE = LEV * CHUNK
TOTAL = OWN * STRIDE
VMEM = 24 * 1024 * 1024
UNROLL = True
ORDER = [d if d < HEMI else OWN - 1 + HEMI - d for d in range(OWN)]
GROUPS = [[d * LEV + x for d in ORDER for x in range(LEV)]]


def lane_order():
    x, a, k, l = np.meshgrid(np.arange(LEV), np.arange(4), np.arange(2), np.arange(LOCAL), indexing="ij")
    out = np.zeros((512, 512), np.float32)
    out[(((x * 4 + a) * 2 + k) * LOCAL + l).ravel(), (((a * LEV + x) * 2 + k) * LOCAL + l).ravel()] = 1
    return out


def row_order():
    t, j = np.meshgrid(np.arange(HEMI), np.arange(ROWS), indexing="ij")
    out = np.zeros((HALF, HALF), np.float32)
    out[(j * HEMI + t).ravel(), (t * ROWS + j).ravel()] = 1
    return out


def low_lanes(rows):
    return lax.broadcasted_iota(jnp.int32, (rows, 128), 1) < 64


def one_hot(folded, column, hot):
    row = folded[...].astype(F32).reshape(1, WAVES)
    for t in range(WAVES // 128):
        lanes = slice(t * 128, (t + 1) * 128)
        column[lanes, :] = jnp.broadcast_to(row[:, lanes], (128, 128)).T
    i = lax.broadcasted_iota(jnp.int32, (OWN, OWN), 0)
    d = lax.broadcasted_iota(jnp.int32, (OWN, OWN), 1)
    turn = jnp.where(d == jnp.where(i < HEMI, i, OWN - 1 + HEMI - i), 1.0, 0.0).astype(BF16)
    lanes = lax.broadcasted_iota(jnp.int32, (OWN, 128), 1)
    for k in range(SLOTS):
        waves = column[pl.ds(k, OWN, stride=SLOTS), :].astype(jnp.int32)
        plain = jnp.concatenate(
            [jnp.where(waves == lanes + t * 128, 1.0, 0.0).astype(BF16) for t in range(WAVES // 128)], axis=1
        )
        hot[k * OWN : (k + 1) * OWN, :] = jnp.dot(turn, plain, preferred_element_type=F32).astype(BF16)


def swap_halves(low, left, right):
    return jnp.where(low, left, pltpu.roll(right, 64, 1)), jnp.where(low, pltpu.roll(left, 64, 1), right)


def outward(place, counts, quad, fourier, folded, vertical, out, hot, weighted, stage, column, couple):
    south = place[0] >= HEMI
    one_hot(folded, column, hot)
    couple[...] = vertical[...].astype(F32)
    piece = 2 * lax.rem(place[0], 8)
    line = jnp.concatenate([couple[pl.ds(piece, 1), :], couple[pl.ds(piece + 1, 1), :]], axis=1)
    stage[pl.ds(CHUNK - 1, OWN * LEV, stride=CHUNK), :] = jnp.broadcast_to(line, (OWN * LEV, 128))
    lanes = 2 * lax.broadcasted_iota(jnp.int32, (LEV * LOCAL, WAVES), 1)
    low = low_lanes(LOCAL)
    slotted = hot[...].T

    @pl.loop(0, QUADS, unroll=UNROLL)
    def _(quarter):
        where = jnp.where(south, QUADS - 1 - quarter, quarter)
        for a in range(4):
            row = quarter * 4 + a
            count = counts[place[0] * ROWS + row]
            product = fourier[row].astype(F32) * quad[row]
            product = jnp.where(lanes < count, product, 0.0).astype(BF16)
            at = jnp.where(south, 3 - a, a)
            for x in range(LEV):
                weighted[quarter, pl.ds(pl.multiple_of((x * 4 + at) * LOCAL, LOCAL), LOCAL), :] = product[
                    x * LOCAL : (x + 1) * LOCAL
                ]
        spread = jnp.dot(weighted[quarter], slotted, preferred_element_type=F32)

        def part(x, a, tile):
            return spread[(x * 4 + a) * LOCAL : (x * 4 + a + 1) * LOCAL, tile * 128 : (tile + 1) * 128]

        def put(x, row, values):
            stage[pl.ds(x * CHUNK + row, OWN, stride=STRIDE), :] = values

        for x in range(LEV):
            for a in (0, 2):
                blocks = [block for tile in range(4) for block in swap_halves(low, part(x, a, tile), part(x, a + 1, tile))]
                across = jnp.concatenate(blocks, axis=0).T
                put(x, where * 4 + a, across[:OWN])
                put(x, where * 4 + a + 1, across[OWN:])
        for x in (0, 2):
            blocks = [block for a in range(4) for block in swap_halves(low, part(x, a, 4), part(x + 1, a, 4))]
            across = jnp.concatenate(blocks, axis=0).T
            put(x, ROWS + where, across[:OWN])
            put(x + 1, ROWS + where, across[OWN:])

    out[...] = stage[...].astype(BF16)


def prepare(basis, order, table, across):
    rows = jnp.dot(order[...], basis[0], preferred_element_type=F32)
    table[0] = rows.astype(BF16)
    across[0] = rows.T.astype(BF16)


def middle(
    place, folded, received, table, across, order, back, damping,
    own, first, second, third, out, stage, turned, couple, pieces, result, rest,
):
    stage[...] = received[...].astype(F32)
    for x in range(LEV):
        lines = stage[pl.ds(x * CHUNK + CHUNK - 1, 8, stride=STRIDE), :]
        couple[pl.ds(x * LOCAL, 8, stride=2), :] = lines
        couple[pl.ds(x * LOCAL + 1, 8, stride=2), :] = pltpu.roll(lines, 64, 1)
    mixing = couple[:, :64].astype(BF16)
    damp = damping[...].reshape(1, WAVES)
    degrees = lax.broadcasted_iota(jnp.int32, (64, WAVES), 1)

    def both(x, row):
        north = stage[pl.ds(x * CHUNK + row, HEMI, stride=STRIDE), :]
        south = stage[pl.ds((HEMI * LEV + x) * CHUNK + row, HEMI, stride=STRIDE), :]
        return north + south, north - south

    def split(side, x, k, values):
        turned[k, (side * LEV + x) * LOCAL : (side * LEV + x + 1) * LOCAL, :] = values.astype(BF16)

    for quarter in range(QUADS):
        rows = slice(quarter * HEMI, (quarter + 1) * HEMI)
        for x in range(LEV):
            for side, values in enumerate(both(x, ROWS + quarter)):
                rest[side * GROUP + quarter * HEMI : side * GROUP + (quarter + 1) * HEMI, x * 128 : (x + 1) * 128] = (
                    values.astype(BF16)
                )
    placed = jnp.dot(rest[...], order[...], preferred_element_type=F32)
    for side in range(2):
        values = jnp.concatenate(
            [
                placed[side * GROUP + quarter * HEMI : side * GROUP + (quarter + 1) * HEMI, a * 128 : (a + 1) * 128]
                for quarter in range(QUADS)
                for a in range(4)
            ],
            axis=0,
        ).T
        for x in range(LEV):
            for k in range(2):
                split(side, x, 8 + k, values[(x * 2 + k) * LOCAL : (x * 2 + k + 1) * LOCAL])
    for x in range(LEV):
        pairs = [both(x, row) for row in range(ROWS)]
        for side in range(2):
            values = jnp.concatenate([pair[side] for pair in pairs], axis=0).T
            for k in range(8):
                split(side, x, k, values[k * LOCAL : (k + 1) * LOCAL])

    def one_slot(slot):
        wave = folded[place[0] * SLOTS + slot]
        products = jnp.dot(turned[slot], table[slot], preferred_element_type=F32)
        matching = ((degrees ^ wave) & 1) == 0
        spectra = jnp.where(matching, products[:64], products[64:])
        spectra = jnp.where(degrees >= wave, spectra, 0.0).astype(BF16)
        pieces[slot] = spectra
        for o, ref in enumerate((own, first, second, third)):
            ahead = pl.multiple_of(lax.rem(place[1] + o, LEV) * LOCAL, LOCAL)
            ref[slot] = pieces[slot, pl.ds(ahead, LOCAL), :]
        filtered = jnp.dot(mixing, spectra, preferred_element_type=F32) * damp
        signed = jnp.where(matching, filtered, -filtered)
        stacked = jnp.concatenate([filtered, signed], axis=0).astype(BF16)
        values = jnp.dot(stacked, across[slot], preferred_element_type=F32)
        return [values[block * LOCAL : (block + 1) * LOCAL] for block in range(2 * LEV)]

    for slot in range(8):
        for block, values in enumerate(one_slot(slot)):
            result[block, slot * LOCAL : (slot + 1) * LOCAL, :] = values
    for slot in range(8, SLOTS):
        for block, values in enumerate(one_slot(slot)):
            side, x = divmod(block, LEV)
            at = (x * 2 + slot - 8) * LOCAL
            result[2 * LEV + side, at : at + LOCAL, :] = values

    for side in range(2):
        values = result[2 * LEV + side].T.astype(BF16)
        for quarter in range(QUADS):
            for a in range(4):
                row = quarter * 4 + a
                rest[side * GROUP + quarter * HEMI : side * GROUP + (quarter + 1) * HEMI, a * 128 : (a + 1) * 128] = (
                    values[row * HEMI : (row + 1) * HEMI]
                )
    placed = jnp.dot(rest[...], back[...], preferred_element_type=F32)
    for block in range(2 * LEV):
        side, x = divmod(block, LEV)
        values = result[block].T
        start = block * CHUNK if side == 0 else (HEMI * LEV + x) * CHUNK
        for row in range(ROWS):
            stage[pl.ds(start + row, HEMI, stride=STRIDE), :] = values[row * HEMI : (row + 1) * HEMI]
        for quarter in range(QUADS):
            stage[pl.ds(start + ROWS + quarter, HEMI, stride=STRIDE), :] = placed[
                side * GROUP + quarter * HEMI : side * GROUP + (quarter + 1) * HEMI, x * 128 : (x + 1) * 128
            ]
    out[...] = stage[...].astype(BF16)


def homeward(place, counts, received, hot, grid, slots, stage):
    south = place[0] >= HEMI
    stage[...] = received[...].astype(F32)
    low = low_lanes(LOCAL)
    lanes = 2 * lax.broadcasted_iota(jnp.int32, (LOCAL, WAVES), 1)

    @pl.loop(0, QUADS, unroll=UNROLL)
    def _(quarter):
        where = jnp.where(south, QUADS - 1 - quarter, quarter)

        def get(x, row):
            return stage[pl.ds(x * CHUNK + row, OWN, stride=STRIDE), :]

        def put(x, a, tile, values):
            slots[quarter, (x * 4 + a) * LOCAL : (x * 4 + a + 1) * LOCAL, tile * 128 : (tile + 1) * 128] = values.astype(BF16)

        for x in range(LEV):
            for a in (0, 2):
                values = jnp.concatenate([get(x, where * 4 + a), get(x, where * 4 + a + 1)], axis=0).T
                for tile in range(4):
                    even = values[2 * tile * LOCAL : (2 * tile + 1) * LOCAL]
                    odd = values[(2 * tile + 1) * LOCAL : (2 * tile + 2) * LOCAL]
                    left, right = swap_halves(low, even, odd)
                    put(x, a, tile, left)
                    put(x, a + 1, tile, right)
        for x in (0, 2):
            values = jnp.concatenate([get(x, ROWS + where), get(x + 1, ROWS + where)], axis=0).T
            for a in range(4):
                even = values[2 * a * LOCAL : (2 * a + 1) * LOCAL]
                odd = values[(2 * a + 1) * LOCAL : (2 * a + 2) * LOCAL]
                left, right = swap_halves(low, even, odd)
                put(x, a, 4, left)
                put(x + 1, a, 4, right)
        values = jnp.dot(slots[quarter], hot[...], preferred_element_type=F32)
        for at in range(4):
            row = quarter * 4 + jnp.where(south, 3 - at, at)
            count = counts[place[0] * ROWS + row]
            for x in range(LEV):
                part = values[(x * 4 + at) * LOCAL : (x * 4 + at + 1) * LOCAL]
                grid[row, x * LOCAL : (x + 1) * LOCAL, :] = jnp.where(lanes < count, part, 0.0).astype(BF16)


def smem():
    return pl.BlockSpec(memory_space=pltpu.SMEM)


def in_vmem():
    return pl.BlockSpec(memory_space=pltpu.VMEM)


def call(kernel, scalars, arrays, outs, scratch):
    outs = [jax.ShapeDtypeStruct(shape, BF16) for shape in outs]
    return pl.pallas_call(
        kernel,
        in_specs=[smem() for _ in scalars] + [in_vmem() for _ in arrays],
        out_specs=[in_vmem() for _ in outs],
        out_shape=outs,
        scratch_shapes=[pltpu.VMEM(shape, dtype) for shape, dtype in scratch],
        compiler_params=pltpu.CompilerParams(vmem_limit_bytes=VMEM),
    )(*scalars, *arrays)


def call_outward(place, counts, quadrature, fourier, folded, vertical):
    return call(
        outward,
        (place, counts, quadrature),
        (fourier, folded, vertical),
        [(TOTAL, 128), (WAVES, WAVES)],
        [((QUADS, 256, WAVES), BF16), ((TOTAL, 128), F32), ((WAVES, 128), F32), ((LOCAL, LEV * LOCAL), F32)],
    )


def call_prepare(basis):
    block = pl.BlockSpec((1, HALF, WAVES), lambda i: (i, 0, 0))
    shape = jax.ShapeDtypeStruct((SLOTS, HALF, WAVES), BF16)
    return pl.pallas_call(
        prepare,
        grid=(SLOTS,),
        in_specs=[block, pl.BlockSpec((HALF, HALF), lambda i: (0, 0))],
        out_specs=[block, block],
        out_shape=[shape, shape],
        cost_estimate=pl.CostEstimate(flops=SLOTS * HALF**3 * 2, bytes_accessed=SLOTS * HALF**2 * 6, transcendentals=0),
        compiler_params=pltpu.CompilerParams(vmem_limit_bytes=16 * 1024 * 1024),
    )(basis, jnp.asarray(row_order(), BF16))


def call_middle(place, folded, received, tables, damping):
    order = lane_order()
    return call(
        middle,
        (place, folded),
        (received, *tables, jnp.asarray(order, BF16), jnp.asarray(order.T, BF16), damping),
        [(SLOTS, LOCAL, WAVES)] * LEV + [(TOTAL, 128)],
        [
            ((TOTAL, 128), F32),
            ((SLOTS, 128, HALF), BF16),
            ((64, 128), F32),
            ((SLOTS, 64, WAVES), BF16),
            ((2 * LEV + 2, 128, HALF), F32),
            ((2 * GROUP, 512), BF16),
        ],
    )


def call_homeward(place, counts, received, hot):
    (grid,) = call(
        homeward, (place, counts), (received, hot), [(ROWS, 64, WAVES)], [((QUADS, 256, WAVES), BF16), ((TOTAL, 128), F32)]
    )
    return grid


def exchange(blocks):
    blocks = blocks.reshape(TOTAL // 2, 2, 128).reshape(OWN * LEV, CHUNK // 2, 2, 128)
    blocks = lax.all_to_all(blocks, AXES, split_axis=0, concat_axis=0, tiled=True, axis_index_groups=GROUPS)
    return blocks.reshape(TOTAL // 2, 2, 128).reshape(TOTAL, 128)


def on_device(fourier, quadrature, counts, folded, basis, vertical, damping):
    lev = lax.axis_index("lev").astype(jnp.int32)
    place = jnp.stack([lax.axis_index("lat").astype(jnp.int32), lev])
    fourier = fourier.transpose(0, 1, 3, 2, 4).reshape(ROWS, 64, WAVES)
    sent, hot = call_outward(place, counts, quadrature, fourier, folded, vertical)
    *pieces, sent = call_middle(place, folded, exchange(sent), call_prepare(basis), damping)
    parts = pieces[:1] + [
        lax.ppermute(pieces[o], "lev", [(i, (i + o) % LEV) for i in range(LEV)]) for o in range(1, LEV)
    ]
    received = exchange(sent)
    parts = jnp.stack(parts)
    parts = jnp.stack([lax.dynamic_index_in_dim(parts, (lev - x) % LEV, 0, keepdims=False) for x in range(LEV)])
    spectral = parts.reshape(2, 2, SLOTS, LOCAL, WAVES).transpose(2, 0, 3, 1, 4)
    grid = call_homeward(place, counts, received, hot)
    return spectral, grid.reshape(ROWS, 2, 2, LOCAL, WAVES).transpose(0, 1, 3, 2, 4)


def solution(mesh):
    return jax.shard_map(
        on_device,
        mesh=mesh,
        in_specs=(
            P("lat", None, "lev", None, None),
            P("lat"),
            P(),
            P(),
            P("lat", None, None),
            P("lev", None),
            P(),
        ),
        out_specs=(P("lat", None, "lev", None, None), P("lat", None, "lev", None, None)),
        check_vma=False,
    )
```

time: 287 us -> 143 us (0.50)
  local copies, waits for them, and re-layouts: 84.3 us -> 26.1 us
  waiting for transfers between devices: 117 us -> 62.3 us
  Pallas kernels: 0 us -> 25.3 us
  matrix products: 24.3 us -> 0 us
  other arithmetic: 21.3 us -> 1.45 us
  between operations: 14.3 us -> 0.79 us
    all_gather x1 -> x0, waiting for transfers between devices: 40 us -> none  [mix_levels(): lax.all_gather(spectral_out, 'lev', axis=2, tiled=True)]
    all_to_all x2, waiting for transfers between devices: 77.1 us -> 43.7 us  [exchange(): lax.all_to_all(blocks, AXES, split_axis=0, concat_axis=0, tiled=True, axi...]
    pallas_call x0 -> x4, Pallas kernels: none -> 25.3 us  [the longest x3 15.3 us: call(): pl.pallas_call(kernel, in_specs=[smem() for _ in scalars] + [in_vmem() fo...]
    dot_general x5 -> x0, matrix products: 24.3 us -> none  [the longest x1 6.07 us: transform_pair(): jnp.einsum('kjn,kbn->kjb', table, kept, preferred_element_type=jnp.float32)]
    ppermute x0 -> x3, waiting for transfers between devices: none -> 18.5 us  [on_device(): lax.ppermute(pieces[o], 'lev', [(i, (i + o) % LEV) for i in range(LEV)])]
    convert_element_type x4 -> x0, local copies, waits for them, and re-layouts: 13.7 us -> none  [the longest x3 13 us: transform_pair(): northern = received[:hemisphere].astype(jnp.float32)]
    select_n x5 -> x0, other arithmetic: 13.2 us -> none  [the longest x2 5.7 us: on_device(): jnp.take(weighted.reshape(lat_rows, batch, wave_count), folded, axis=2)]
    gather x2 -> x0, local copies, waits for them, and re-layouts: 11 us -> none  [the longest x1 5.49 us: on_device(): jnp.take(weighted.reshape(lat_rows, batch, wave_count), folded, axis=2)]
  transfers between devices with their start and end apart: 3 -> 5, of which waited for: 3 -> 5; matrix products, arithmetic and copies ran while one was open for 2% -> 2% of each run, Pallas kernels for 0% -> 7%
where the time goes in v3:
time: 143 us
  waiting for transfers between devices  62.3 us (44%)
  starting transfers between devices  26.8 us (19%)
  local copies, waits for them, and re-layouts  26.1 us (18%)
  Pallas kernels  25.3 us (18%)
  other arithmetic  1.45 us (1%)
    all_to_all x2, waiting for transfers between devices, exchange(): lax.all_to_all(blocks, AXES, split_axis=0, concat_axis=0, tiled=True, axi...  43.7 us
    all_to_all x2, starting transfers between devices, exchange(): lax.all_to_all(blocks, AXES, split_axis=0, concat_axis=0, tiled=True, axi...  22.9 us
    unnamed x34, local copies, waits for them, and re-layouts  20 us
    ppermute x3, waiting for transfers between devices, on_device(): lax.ppermute(pieces[o], 'lev', [(i, (i + o) % LEV) for i in range(LEV)])  18.5 us
    pallas_call x3, Pallas kernels, call(): pl.pallas_call(kernel, in_specs=[smem() for _ in scalars] + [in_vmem() fo...  15.3 us
    pallas_call x1, Pallas kernels, call_prepare(): pl.pallas_call(prepare, grid=(SLOTS,), in_specs=[block, pl.BlockSpec((HAL...  10 us
    ppermute x3, starting transfers between devices, on_device(): lax.ppermute(pieces[o], 'lev', [(i, (i + o) % LEV) for i in range(LEV)])  3.85 us
  transfers between devices with their start and end apart: 5, of which 5 were waited for; matrix products, arithmetic and copies ran while one was open for 2% of the time, Pallas kernels for 7%

profile of v3, /device:TPU:1, one launch (start us, length us, event | category | flops | bytes accessed | tf_op | source)
XLA Modules:
  0.0 142.7 jit_solution(13234828669436715180)
XLA Ops:
  0.6 0.0 copy-start.7
  0.6 0.0 copy-start.6
  0.7 0.0 copy-start.10
  0.7 0.0 copy-start.8
  0.7 1.7 %copy.12 = bf16[20,2,2,16,640]{4,3,2,1,0:T(8,128)(2,1)S(1)} copy(bf16[20,2,2,16,640]{4,2,3,1,0:T(2,128)(2,1)} %bitcast.27) | data formatting | bytes 3276800 | tf_op jit(solution)/shard_map/transpose | solution.py:337
  2.4 0.1 pad_add_fusion.place
  2.5 0.0 copy-done.7
  2.5 0.0 copy-done.6
  2.5 0.0 copy-done.10
  2.5 0.0 copy-done.8
  2.5 5.0 %shard_map.113 = (bf16[6656,128]{1,0:T(8,128)(2,1)}, bf16[640,640]{1,0:T(8,128)(2,1)S(1)}) custom-call(s32[2]{0:T(128)S(1)} %pad_add_fusion.place, s32[1280]{0:T(1024)S(1)} %copy-done.6, f32[20]{0:T(128)S(1)} %copy-done.10, bf16[20,64,640]{2,1,0:T(8,128)(2,1)S(1)} %bitcast.22, s32[640]{0:T(1024)S(1)} %copy-done.7, bf16[16,64]{1,0:T(8,128)(2,1)S(1)} %copy-done.8), custom_call_target="tpu_custom_call" | custom-call | tf_op jit(solution)/shard_map/pallas_call | solution.py:269
  7.5 15.6 %all-to-all-start = ((bf16[256,13,2,128]{3,2,1,0:T(2,128)(2,1)}), bf16[256,13,2,128]{3,2,1,0:T(2,128)(2,1)S(1)}, u32[]{:S(2)}, u32[]{:S(2)}) async-start(bf16[256,13,2,128]{3,2,1,0:T(2,128)(2,1)} %bitcast.4), calls=%async_computation | async-start | bytes 3407872 | tf_op jit(solution)/shard_map/all_to_all | solution.py:330
  23.2 0.0 copy-start.11
  23.2 3.3 %copy-done.11 = bf16[10,640,640]{2,1,0:T(8,128)(2,1)S(1)} copy-done((bf16[10,640,640]{2,1,0:T(8,128)(2,1)S(1)}, bf16[10,640,640]{2,1,0:T(8,128)(2,1)}, u32[]{:S(2)}) %copy-start.11) | copy-done | bytes 8192024
  26.5 0.0 copy-start.16
  26.5 1.1 copy-done.16
  27.7 0.0 copy-start.4
  27.7 0.0 copy-start.9
  27.7 10.0 %shard_map.114 = (bf16[10,640,640]{2,1,0:T(8,128)(2,1)S(1)}, bf16[10,640,640]{2,1,0:T(8,128)(2,1)S(1)}) custom-call(bf16[10,640,640]{2,1,0:T(8,128)(2,1)S(1)} %copy-done.11, bf16[640,640]{1,0:T(8,128)(2,1)S(1)} %copy-done.16), custom_call_target="tpu_custom_call" | custom-call | flops 5242880000 | bytes 24576000 | tf_op jit(solution)/shard_map/pallas_call | solution.py:292
  37.7 0.0 copy-start
  37.7 3.1 %copy-done = bf16[10,640,640]{2,1,0:T(8,128)(2,1)} copy-done((bf16[10,640,640]{2,1,0:T(8,128)(2,1)}, bf16[10,640,640]{2,1,0:T(8,128)(2,1)S(1)}, u32[]{:S(2)}) %copy-start) | copy-done | bytes 8192024
  40.9 3.2 %copy-done.2 = bf16[10,640,640]{2,1,0:T(8,128)(2,1)} copy-done((bf16[10,640,640]{2,1,0:T(8,128)(2,1)}, bf16[10,640,640]{2,1,0:T(8,128)(2,1)S(1)}, u32[]{:S(2)}) %copy-start.2) | copy-done | bytes 8192024
  44.0 24.1 %all-to-all-done = bf16[256,13,2,128]{3,2,1,0:T(2,128)(2,1)S(1)} async-done(((bf16[256,13,2,128]{3,2,1,0:T(2,128)(2,1)}), bf16[256,13,2,128]{3,2,1,0:T(2,128)(2,1)S(1)}, u32[]{:S(2)}, u32[]{:S(2)}) %all-to-all-start) | async-done | bytes 1703968 | tf_op jit(solution)/shard_map/all_to_all | solution.py:330
  68.2 0.0 copy-done.4
  68.2 0.0 copy-done.9
  68.2 3.3 %copy-done.1 = bf16[10,640,640]{2,1,0:T(8,128)(2,1)S(1)} copy-done((bf16[10,640,640]{2,1,0:T(8,128)(2,1)S(1)}, bf16[10,640,640]{2,1,0:T(8,128)(2,1)}, u32[]{:S(2)}) %copy-start.1) | copy-done | bytes 8192024
  71.5 3.3 %copy-done.3 = bf16[10,640,640]{2,1,0:T(8,128)(2,1)S(1)} copy-done((bf16[10,640,640]{2,1,0:T(8,128)(2,1)S(1)}, bf16[10,640,640]{2,1,0:T(8,128)(2,1)}, u32[]{:S(2)}) %copy-start.3) | copy-done | bytes 8192024
  74.8 7.3 %shard_map.115 = (bf16[10,16,640]{2,1,0:T(8,128)(2,1)S(1)}, bf16[10,16,640]{2,1,0:T(8,128)(2,1)S(1)}, bf16[10,16,640]{2,1,0:T(8,128)(2,1)S(1)}, bf16[10,16,640]{2,1,0:T(8,128)(2,1)S(1)}, bf16[6656,128]{1,0:T(8,128)(2,1)S(1)}) custom-call(s32[2]{0:T(128)S(1)} %pad_add_fusion.place, s32[640]{0:T(1024)S(1)} %copy-done.7, bf16[6656,128]{1,0:T(8,128)(2,1)S(1)} %bitcast.20, ...), custom_call_target="tpu_custom_call" | custom-call | tf_op jit(solution)/shard_map/pallas_call | solution.py:269
  82.1 0.0 copy-start.5
  82.2 1.2 copy-done.5
  83.4 0.7 copy-done.12
  84.0 0.7 copy-done.14
  84.7 7.3 %all-to-all-start.1 = ((bf16[256,13,2,128]{3,2,1,0:T(2,128)(2,1)}), bf16[256,13,2,128]{3,2,1,0:T(2,128)(2,1)S(1)}, u32[]{:S(2)}, u32[]{:S(2)}) async-start(bf16[256,13,2,128]{3,2,1,0:T(2,128)(2,1)} %bitcast.24), calls=%async_computation.1 | async-start | bytes 3407872 | tf_op jit(solution)/shard_map/all_to_all | solution.py:330
  92.0 0.0 copy-done.15
  92.0 2.7 %collective-permute-start.2 = (bf16[10,16,640]{2,1,0:T(8,128)(2,1)S(1)}, bf16[10,16,640]{2,1,0:T(8,128)(2,1)}, u32[]{:S(2)}, u32[]{:S(2)}) collective-permute-start(bf16[10,16,640]{2,1,0:T(8,128)(2,1)S(1)} %copy-done.15), channel_id=1, source_target_pairs={{0,3},{1,0},{2,1},{3,2},{4,7},{5,4},{6,5},{7,6},{8,11},{9,8},{10,9... | collective-permute-start | bytes 614408 | tf_op jit(solution)/shard_map/ppermute | solution.py:341
  94.7 0.0 copy-done.13
  94.7 0.5 collective-permute-start.1
  95.3 0.6 collective-permute-start
  95.9 7.2 %collective-permute-done.2 = bf16[10,16,640]{2,1,0:T(8,128)(2,1)} collective-permute-done((bf16[10,16,640]{2,1,0:T(8,128)(2,1)S(1)}, bf16[10,16,640]{2,1,0:T(8,128)(2,1)}, u32[]{:S(2)}, u32[]{:S(2)}) %collective-permute-start.2) | collective-permute-done | bytes 204832 | tf_op jit(solution)/shard_map/ppermute | solution.py:341
  103.1 2.6 %collective-permute-done.1 = bf16[10,16,640]{2,1,0:T(8,128)(2,1)} collective-permute-done((bf16[10,16,640]{2,1,0:T(8,128)(2,1)S(1)}, bf16[10,16,640]{2,1,0:T(8,128)(2,1)}, u32[]{:S(2)}, u32[]{:S(2)}) %collective-permute-start.1) | collective-permute-done | bytes 204832 | tf_op jit(solution)/shard_map/ppermute | solution.py:341
  105.7 8.7 %collective-permute-done = bf16[10,16,640]{2,1,0:T(8,128)(2,1)} collective-permute-done((bf16[10,16,640]{2,1,0:T(8,128)(2,1)S(1)}, bf16[10,16,640]{2,1,0:T(8,128)(2,1)}, u32[]{:S(2)}, u32[]{:S(2)}) %collective-permute-start) | collective-permute-done | bytes 204832 | tf_op jit(solution)/shard_map/ppermute | solution.py:341
  114.4 1.2 pad_maximum_fusion
  115.7 0.1 constant_dynamic-slice_fusion.3
  115.7 0.1 pad_maximum_fusion.1
  115.9 1.5 %copy.18 = bf16[2,2,10,16,640]{4,1,3,0,2:T(2,128)(2,1)} copy(bf16[2,2,10,16,640]{4,3,2,1,0:T(8,128)(2,1)S(1)} %bitcast.26) | data formatting | bytes 1638400 | tf_op jit(solution)/shard_map/reshape | solution.py:346
  117.4 19.6 %all-to-all-done.1 = bf16[256,13,2,128]{3,2,1,0:T(2,128)(2,1)S(1)} async-done(((bf16[256,13,2,128]{3,2,1,0:T(2,128)(2,1)}), bf16[256,13,2,128]{3,2,1,0:T(2,128)(2,1)S(1)}, u32[]{:S(2)}, u32[]{:S(2)}) %all-to-all-start.1) | async-done | bytes 1703968 | tf_op jit(solution)/shard_map/all_to_all | solution.py:330
  137.0 2.9 %shard_map.116 = bf16[20,64,640]{2,1,0:T(8,128)(2,1)S(1)} custom-call(s32[2]{0:T(128)S(1)} %pad_add_fusion.place, s32[1280]{0:T(1024)S(1)} %copy-done.6, bf16[6656,128]{1,0:T(8,128)(2,1)S(1)} %bitcast.21, bf16[640,640]{1,0:T(8,128)(2,1)S(1)} %get-tuple-element.19.hot), custom_call_target="tpu_custom_call" | custom-call | tf_op jit(solution)/shard_map/pallas_call | solution.py:269
  139.9 2.8 %copy.17 = bf16[20,2,2,16,640]{4,2,3,1,0:T(2,128)(2,1)} copy(bf16[20,2,2,16,640]{4,3,2,1,0:T(8,128)(2,1)S(1)} %bitcast.23) | data formatting | bytes 3276800 | tf_op jit(solution)/shard_map/reshape | solution.py:348
  (7 shorter events, 0.0 us)
Async XLA Ops:
  0.6 1.9 %copy-start.7 = (s32[640]{0:T(1024)S(1)}, s32[640]{0:T(1024)}, u32[]{:S(2)}) copy-start(s32[640]{0:T(1024)} %folded.3) | copy-start | bytes 7684
  0.6 1.9 %copy-start.6 = (s32[1280]{0:T(1024)S(1)}, s32[1280]{0:T(1024)}, u32[]{:S(2)}) copy-start(s32[1280]{0:T(1024)} %counts.3) | copy-start | bytes 15364
  0.7 1.9 %copy-start.10 = (f32[20]{0:T(128)S(1)}, f32[20]{0:T(128)}, u32[]{:S(2)}) copy-start(f32[20]{0:T(128)} %quad.1) | copy-start | bytes 244
  0.7 1.8 %copy-start.8 = (bf16[16,64]{1,0:T(8,128)(2,1)S(1)}, bf16[16,64]{1,0:T(8,128)(2,1)}, u32[]{:S(2)}) copy-start(bf16[16,64]{1,0:T(8,128)(2,1)} %vertical.1) | copy-start | bytes 6148
  7.5 60.6 %all-to-all-start = ((bf16[256,13,2,128]{3,2,1,0:T(2,128)(2,1)}), bf16[256,13,2,128]{3,2,1,0:T(2,128)(2,1)S(1)}, u32[]{:S(2)}, u32[]{:S(2)}) async-start(bf16[256,13,2,128]{3,2,1,0:T(2,128)(2,1)} %bitcast.4), calls=%async_computation | async-start | bytes 3407872 | tf_op jit(solution)/shard_map/all_to_all | solution.py:330
  23.2 3.3 %copy-start.11 = (bf16[10,640,640]{2,1,0:T(8,128)(2,1)S(1)}, bf16[10,640,640]{2,1,0:T(8,128)(2,1)}, u32[]{:S(2)}) copy-start(bf16[10,640,640]{2,1,0:T(8,128)(2,1)} %basis.1) | copy-start | bytes 24576004
  26.5 1.1 copy-start.16
  27.7 40.5 %copy-start.4 = (bf16[512,512]{1,0:T(8,128)(2,1)S(1)}, bf16[512,512]{1,0:T(8,128)(2,1)}, u32[]{:S(2)}) copy-start(bf16[512,512]{1,0:T(8,128)(2,1)} %constant.58.clone.order.back) | copy-start | bytes 1572868
  27.7 40.5 %copy-start.9 = (f32[640]{0:T(1024)S(1)}, f32[640]{0:T(1024)}, u32[]{:S(2)}) copy-start(f32[640]{0:T(1024)} %damping.1) | copy-start | bytes 7684
  37.7 3.2 %copy-start = (bf16[10,640,640]{2,1,0:T(8,128)(2,1)}, bf16[10,640,640]{2,1,0:T(8,128)(2,1)S(1)}, u32[]{:S(2)}) copy-start(bf16[10,640,640]{2,1,0:T(8,128)(2,1)S(1)} %get-tuple-element.12.table) | copy-start | bytes 24576004
  40.9 3.2 %copy-start.2 = (bf16[10,640,640]{2,1,0:T(8,128)(2,1)}, bf16[10,640,640]{2,1,0:T(8,128)(2,1)S(1)}, u32[]{:S(2)}) copy-start(bf16[10,640,640]{2,1,0:T(8,128)(2,1)S(1)} %get-tuple-element.13.across) | copy-start | bytes 24576004
  68.2 3.3 %copy-start.1 = (bf16[10,640,640]{2,1,0:T(8,128)(2,1)S(1)}, bf16[10,640,640]{2,1,0:T(8,128)(2,1)}, u32[]{:S(2)}) copy-start(bf16[10,640,640]{2,1,0:T(8,128)(2,1)} %copy-done) | copy-start | bytes 24576004
  71.5 3.3 %copy-start.3 = (bf16[10,640,640]{2,1,0:T(8,128)(2,1)S(1)}, bf16[10,640,640]{2,1,0:T(8,128)(2,1)}, u32[]{:S(2)}) copy-start(bf16[10,640,640]{2,1,0:T(8,128)(2,1)} %copy-done.2) | copy-start | bytes 24576004
  82.1 1.2 copy-start.5
  83.4 0.7 copy-start.12
  84.0 0.7 copy-start.14
  84.7 7.3 %copy-start.15 = (bf16[10,16,640]{2,1,0:T(8,128)(2,1)S(1)}, bf16[10,16,640]{2,1,0:T(8,128)(2,1)}, u32[]{:S(2)}) copy-start(bf16[10,16,640]{2,1,0:T(8,128)(2,1)} %copy-done.14) | copy-start | bytes 614404
  84.7 10.0 %copy-start.13 = (bf16[10,16,640]{2,1,0:T(8,128)(2,1)S(1)}, bf16[10,16,640]{2,1,0:T(8,128)(2,1)}, u32[]{:S(2)}) copy-start(bf16[10,16,640]{2,1,0:T(8,128)(2,1)} %copy-done.12) | copy-start | bytes 614404
  84.7 52.3 %all-to-all-start.1 = ((bf16[256,13,2,128]{3,2,1,0:T(2,128)(2,1)}), bf16[256,13,2,128]{3,2,1,0:T(2,128)(2,1)S(1)}, u32[]{:S(2)}, u32[]{:S(2)}) async-start(bf16[256,13,2,128]{3,2,1,0:T(2,128)(2,1)} %bitcast.24), calls=%async_computation.1 | async-start | bytes 3407872 | tf_op jit(solution)/shard_map/all_to_all | solution.py:330
  92.0 11.0 %collective-permute-start.2 = (bf16[10,16,640]{2,1,0:T(8,128)(2,1)S(1)}, bf16[10,16,640]{2,1,0:T(8,128)(2,1)}, u32[]{:S(2)}, u32[]{:S(2)}) collective-permute-start(bf16[10,16,640]{2,1,0:T(8,128)(2,1)S(1)} %copy-done.15), channel_id=1, source_target_pairs={{0,3},{1,0},{2,1},{3,2},{4,7},{5,4},{6,5},{7,6},{8,11},{9,8},{10,9... | collective-permute-start | bytes 614408 | tf_op jit(solution)/shard_map/ppermute | solution.py:341
  94.7 10.9 %collective-permute-start.1 = (bf16[10,16,640]{2,1,0:T(8,128)(2,1)S(1)}, bf16[10,16,640]{2,1,0:T(8,128)(2,1)}, u32[]{:S(2)}, u32[]{:S(2)}) collective-permute-start(bf16[10,16,640]{2,1,0:T(8,128)(2,1)S(1)} %copy-done.13), channel_id=1, source_target_pairs={{0,2},{1,3},{2,0},{3,1},{4,6},{5,7},{6,4},{7,5},{8,10},{9,11},{10,... | collective-permute-start | bytes 614408 | tf_op jit(solution)/shard_map/ppermute | solution.py:341
  95.3 19.1 %collective-permute-start = (bf16[10,16,640]{2,1,0:T(8,128)(2,1)S(1)}, bf16[10,16,640]{2,1,0:T(8,128)(2,1)}, u32[]{:S(2)}, u32[]{:S(2)}) collective-permute-start(bf16[10,16,640]{2,1,0:T(8,128)(2,1)S(1)} %get-tuple-element.15), channel_id=1, source_target_pairs={{0,1},{1,2},{2,3},{3,0},{4,5},{5,6},{6,7},{7,4},{8,9},{9,10},{10,1... | collective-permute-start | bytes 614408 | tf_op jit(solution)/shard_map/ppermute | solution.py:341

commit v4 on v3

--- a/solution.py
+++ b/solution.py
@@ -1,4 +1,3 @@
-import numpy as np
 import jax
 import jax.numpy as jnp
 from jax import lax
@@ -27,20 +26,6 @@
 GROUPS = [[d * LEV + x for d in ORDER for x in range(LEV)]]
 
 
-def lane_order():
-    x, a, k, l = np.meshgrid(np.arange(LEV), np.arange(4), np.arange(2), np.arange(LOCAL), indexing="ij")
-    out = np.zeros((512, 512), np.float32)
-    out[(((x * 4 + a) * 2 + k) * LOCAL + l).ravel(), (((a * LEV + x) * 2 + k) * LOCAL + l).ravel()] = 1
-    return out
-
-
-def row_order():
-    t, j = np.meshgrid(np.arange(HEMI), np.arange(ROWS), indexing="ij")
-    out = np.zeros((HALF, HALF), np.float32)
-    out[(j * HEMI + t).ravel(), (t * ROWS + j).ravel()] = 1
-    return out
-
-
 def low_lanes(rows):
     return lax.broadcasted_iota(jnp.int32, (rows, 128), 1) < 64
 
@@ -113,15 +98,9 @@
     out[...] = stage[...].astype(BF16)
 
 
-def prepare(basis, order, table, across):
-    rows = jnp.dot(order[...], basis[0], preferred_element_type=F32)
-    table[0] = rows.astype(BF16)
-    across[0] = rows.T.astype(BF16)
-
-
 def middle(
-    place, folded, received, table, across, order, back, damping,
-    own, first, second, third, out, stage, turned, couple, pieces, result, rest,
+    place, folded, received, damping, table,
+    own, first, second, third, out, stage, turned, couple, pieces, result, rest, order, natural, ready, leave, depart,
 ):
     stage[...] = received[...].astype(F32)
     for x in range(LEV):
@@ -131,6 +110,9 @@
     mixing = couple[:, :64].astype(BF16)
     damp = damping[...].reshape(1, WAVES)
     degrees = lax.broadcasted_iota(jnp.int32, (64, WAVES), 1)
+    lanes = lax.broadcasted_iota(jnp.int32, (512, 512), 1)
+    swapped = ((lanes >> 7) << 5) | (((lanes >> 5) & 3) << 7) | (lanes & 31)
+    order[...] = jnp.where(lax.broadcasted_iota(jnp.int32, (512, 512), 0) == swapped, 1.0, 0.0).astype(BF16)
 
     def both(x, row):
         north = stage[pl.ds(x * CHUNK + row, HEMI, stride=STRIDE), :]
@@ -149,23 +131,25 @@
                 )
     placed = jnp.dot(rest[...], order[...], preferred_element_type=F32)
     for side in range(2):
-        values = jnp.concatenate(
-            [
-                placed[side * GROUP + quarter * HEMI : side * GROUP + (quarter + 1) * HEMI, a * 128 : (a + 1) * 128]
-                for quarter in range(QUADS)
-                for a in range(4)
-            ],
-            axis=0,
-        ).T
+        for quarter in range(QUADS):
+            for a in range(4):
+                natural[2 * LEV + side, pl.ds(quarter * 4 + a, HEMI, stride=ROWS), :] = placed[
+                    side * GROUP + quarter * HEMI : side * GROUP + (quarter + 1) * HEMI, a * 128 : (a + 1) * 128
+                ]
+        values = natural[2 * LEV + side].T
         for x in range(LEV):
             for k in range(2):
                 split(side, x, 8 + k, values[(x * 2 + k) * LOCAL : (x * 2 + k + 1) * LOCAL])
     for x in range(LEV):
-        pairs = [both(x, row) for row in range(ROWS)]
+        for row in range(ROWS):
+            for side, values in enumerate(both(x, row)):
+                natural[side * LEV + x, pl.ds(row, HEMI, stride=ROWS), :] = values
         for side in range(2):
-            values = jnp.concatenate([pair[side] for pair in pairs], axis=0).T
+            values = natural[side * LEV + x].T
             for k in range(8):
                 split(side, x, k, values[k * LOCAL : (k + 1) * LOCAL])
+
+    stores = []
 
     def one_slot(slot):
         wave = folded[place[0] * SLOTS + slot]
@@ -176,11 +160,13 @@
         pieces[slot] = spectra
         for o, ref in enumerate((own, first, second, third)):
             ahead = pl.multiple_of(lax.rem(place[1] + o, LEV) * LOCAL, LOCAL)
-            ref[slot] = pieces[slot, pl.ds(ahead, LOCAL), :]
+            store = pltpu.make_async_copy(pieces.at[slot, pl.ds(ahead, LOCAL), :], ref.at[slot], leave.at[slot, o])
+            store.start()
+            stores.append(store)
         filtered = jnp.dot(mixing, spectra, preferred_element_type=F32) * damp
         signed = jnp.where(matching, filtered, -filtered)
         stacked = jnp.concatenate([filtered, signed], axis=0).astype(BF16)
-        values = jnp.dot(stacked, across[slot], preferred_element_type=F32)
+        values = lax.dot_general(stacked, table[slot], (((1,), (1,)), ((), ())), preferred_element_type=F32)
         return [values[block * LOCAL : (block + 1) * LOCAL] for block in range(2 * LEV)]
 
     for slot in range(8):
@@ -193,25 +179,32 @@
             result[2 * LEV + side, at : at + LOCAL, :] = values
 
     for side in range(2):
-        values = result[2 * LEV + side].T.astype(BF16)
+        natural[2 * LEV + side] = result[2 * LEV + side].T
         for quarter in range(QUADS):
             for a in range(4):
-                row = quarter * 4 + a
                 rest[side * GROUP + quarter * HEMI : side * GROUP + (quarter + 1) * HEMI, a * 128 : (a + 1) * 128] = (
-                    values[row * HEMI : (row + 1) * HEMI]
+                    natural[2 * LEV + side, pl.ds(quarter * 4 + a, HEMI, stride=ROWS), :].astype(BF16)
                 )
-    placed = jnp.dot(rest[...], back[...], preferred_element_type=F32)
-    for block in range(2 * LEV):
-        side, x = divmod(block, LEV)
-        values = result[block].T
-        start = block * CHUNK if side == 0 else (HEMI * LEV + x) * CHUNK
-        for row in range(ROWS):
-            stage[pl.ds(start + row, HEMI, stride=STRIDE), :] = values[row * HEMI : (row + 1) * HEMI]
-        for quarter in range(QUADS):
-            stage[pl.ds(start + ROWS + quarter, HEMI, stride=STRIDE), :] = placed[
-                side * GROUP + quarter * HEMI : side * GROUP + (quarter + 1) * HEMI, x * 128 : (x + 1) * 128
-            ]
-    out[...] = stage[...].astype(BF16)
+    placed = jnp.dot(rest[...], order[...], preferred_element_type=F32)
+    for side in range(2):
+        for x in range(LEV):
+            natural[side * LEV + x] = result[side * LEV + x].T
+            start = (side * HEMI * LEV + x) * CHUNK
+            for row in range(ROWS):
+                stage[pl.ds(start + row, HEMI, stride=STRIDE), :] = natural[
+                    side * LEV + x, pl.ds(row, HEMI, stride=ROWS), :
+                ]
+            for quarter in range(QUADS):
+                stage[pl.ds(start + ROWS + quarter, HEMI, stride=STRIDE), :] = placed[
+                    side * GROUP + quarter * HEMI : side * GROUP + (quarter + 1) * HEMI, x * 128 : (x + 1) * 128
+                ]
+        rows = pl.ds(side * HEMI * STRIDE, HEMI * STRIDE)
+        ready[rows, :] = stage[rows, :].astype(BF16)
+        store = pltpu.make_async_copy(ready.at[rows, :], out.at[rows, :], depart.at[side])
+        store.start()
+        stores.append(store)
+    for store in stores:
+        store.wait()
 
 
 def homeward(place, counts, received, hot, grid, slots, stage):
@@ -264,16 +257,27 @@
     return pl.BlockSpec(memory_space=pltpu.VMEM)
 
 
-def call(kernel, scalars, arrays, outs, scratch):
-    outs = [jax.ShapeDtypeStruct(shape, BF16) for shape in outs]
+def in_hbm():
+    return pl.BlockSpec(memory_space=pltpu.HBM)
+
+
+def call(kernel, scalars, arrays, outs, scratch, far_outs=(), limit=VMEM):
+    shapes = [jax.ShapeDtypeStruct(shape, BF16) for shape in (*far_outs, *outs)]
     return pl.pallas_call(
         kernel,
         in_specs=[smem() for _ in scalars] + [in_vmem() for _ in arrays],
-        out_specs=[in_vmem() for _ in outs],
-        out_shape=outs,
-        scratch_shapes=[pltpu.VMEM(shape, dtype) for shape, dtype in scratch],
-        compiler_params=pltpu.CompilerParams(vmem_limit_bytes=VMEM),
+        out_specs=[in_hbm() for _ in far_outs] + [in_vmem() for _ in outs],
+        out_shape=shapes,
+        scratch_shapes=[
+            kind(shape, dtype) if dtype is not None else kind(shape)
+            for kind, shape, dtype in ((pltpu.VMEM, *s) if len(s) == 2 else s for s in scratch)
+        ],
+        compiler_params=pltpu.CompilerParams(vmem_limit_bytes=limit),
     )(*scalars, *arrays)
+
+
+def copies(*shape):
+    return (pltpu.SemaphoreType.DMA, shape, None)
 
 
 def call_outward(place, counts, quadrature, fourier, folded, vertical):
@@ -286,27 +290,12 @@
     )
 
 
-def call_prepare(basis):
-    block = pl.BlockSpec((1, HALF, WAVES), lambda i: (i, 0, 0))
-    shape = jax.ShapeDtypeStruct((SLOTS, HALF, WAVES), BF16)
-    return pl.pallas_call(
-        prepare,
-        grid=(SLOTS,),
-        in_specs=[block, pl.BlockSpec((HALF, HALF), lambda i: (0, 0))],
-        out_specs=[block, block],
-        out_shape=[shape, shape],
-        cost_estimate=pl.CostEstimate(flops=SLOTS * HALF**3 * 2, bytes_accessed=SLOTS * HALF**2 * 6, transcendentals=0),
-        compiler_params=pltpu.CompilerParams(vmem_limit_bytes=16 * 1024 * 1024),
-    )(basis, jnp.asarray(row_order(), BF16))
-
-
-def call_middle(place, folded, received, tables, damping):
-    order = lane_order()
+def call_middle(place, folded, received, table, damping):
     return call(
         middle,
         (place, folded),
-        (received, *tables, jnp.asarray(order, BF16), jnp.asarray(order.T, BF16), damping),
-        [(SLOTS, LOCAL, WAVES)] * LEV + [(TOTAL, 128)],
+        (received, damping, table),
+        [],
         [
             ((TOTAL, 128), F32),
             ((SLOTS, 128, HALF), BF16),
@@ -314,13 +303,24 @@
             ((SLOTS, 64, WAVES), BF16),
             ((2 * LEV + 2, 128, HALF), F32),
             ((2 * GROUP, 512), BF16),
+            ((512, 512), BF16),
+            ((2 * LEV + 2, HALF, 128), F32),
+            ((TOTAL, 128), BF16),
+            copies(SLOTS, LEV),
+            copies(2),
         ],
+        far_outs=[(SLOTS, LOCAL, WAVES)] * LEV + [(TOTAL, 128)],
+        limit=28 * 1024 * 1024,
     )
 
 
 def call_homeward(place, counts, received, hot):
     (grid,) = call(
-        homeward, (place, counts), (received, hot), [(ROWS, 64, WAVES)], [((QUADS, 256, WAVES), BF16), ((TOTAL, 128), F32)]
+        homeward,
+        (place, counts),
+        (received, hot),
+        [(ROWS, 64, WAVES)],
+        [((QUADS, 256, WAVES), BF16), ((TOTAL, 128), F32)],
     )
     return grid
 
@@ -336,7 +336,7 @@
     place = jnp.stack([lax.axis_index("lat").astype(jnp.int32), lev])
     fourier = fourier.transpose(0, 1, 3, 2, 4).reshape(ROWS, 64, WAVES)
     sent, hot = call_outward(place, counts, quadrature, fourier, folded, vertical)
-    *pieces, sent = call_middle(place, folded, exchange(sent), call_prepare(basis), damping)
+    *pieces, sent = call_middle(place, folded, exchange(sent), basis, damping)
     parts = pieces[:1] + [
         lax.ppermute(pieces[o], "lev", [(i, (i + o) % LEV) for i in range(LEV)]) for o in range(1, LEV)
     ]

time: 143 us -> 137 us (0.958)
  blocking collectives: 0 us -> 60.4 us
  waiting for transfers between devices: 62.3 us -> 36.9 us
  local copies, waits for them, and re-layouts: 26.1 us -> 6.28 us
  starting transfers between devices: 26.8 us -> 12.2 us
  Pallas kernels: 25.3 us -> 18.7 us
    all_to_all x0 -> x1, blocking collectives: none -> 60.4 us  [exchange(): lax.all_to_all(blocks, AXES, split_axis=0, concat_axis=0, tiled=True, axi...]
    all_to_all x2 -> x1, waiting for transfers between devices: 43.7 us -> 22.8 us  [exchange(): lax.all_to_all(blocks, AXES, split_axis=0, concat_axis=0, tiled=True, axi...]
    unnamed x34 -> x12, local copies, waits for them, and re-layouts: 20 us -> 0.03 us
    all_to_all x2 -> x1, starting transfers between devices: 22.9 us -> 7.11 us  [exchange(): lax.all_to_all(blocks, AXES, split_axis=0, concat_axis=0, tiled=True, axi...]
    pallas_call x1 -> x0, Pallas kernels: 10 us -> none  [call_prepare(): pl.pallas_call(prepare, grid=(SLOTS,), in_specs=[block, pl.BlockSpec((HAL...]
    ppermute x3, waiting for transfers between devices: 18.5 us -> 14.2 us  [on_device(): lax.ppermute(pieces[o], 'lev', [(i, (i + o) % LEV) for i in range(LEV)])]
    pallas_call x3, Pallas kernels: 15.3 us -> 18.7 us  [call(): pl.pallas_call(kernel, in_specs=[smem() for _ in scalars] + [in_vmem() fo...]
  transfers between devices with their start and end apart: 5 -> 4, of which waited for: 5 -> 3; matrix products, arithmetic and copies ran while one was open for 2% -> 2% of each run, Pallas kernels for 7% -> 0%
where the time goes in v4:
time: 137 us
  blocking collectives  60.4 us (44%)
  waiting for transfers between devices  36.9 us (27%)
  Pallas kernels  18.7 us (14%)
  starting transfers between devices  12.2 us (9%)
  local copies, waits for them, and re-layouts  6.28 us (5%)
  other arithmetic  1.45 us (1%)
    all_to_all x1, blocking collectives, exchange(): lax.all_to_all(blocks, AXES, split_axis=0, concat_axis=0, tiled=True, axi...  60.4 us
    all_to_all x1, waiting for transfers between devices, exchange(): lax.all_to_all(blocks, AXES, split_axis=0, concat_axis=0, tiled=True, axi...  22.8 us
    pallas_call x3, Pallas kernels, call(): pl.pallas_call(kernel, in_specs=[smem() for _ in scalars] + [in_vmem() fo...  18.7 us
    ppermute x3, waiting for transfers between devices, on_device(): lax.ppermute(pieces[o], 'lev', [(i, (i + o) % LEV) for i in range(LEV)])  14.2 us
    all_to_all x1, starting transfers between devices, exchange(): lax.all_to_all(blocks, AXES, split_axis=0, concat_axis=0, tiled=True, axi...  7.11 us
    ppermute x3, starting transfers between devices, on_device(): lax.ppermute(pieces[o], 'lev', [(i, (i + o) % LEV) for i in range(LEV)])  5.06 us
    reshape x1, local copies, waits for them, and re-layouts, on_device(): grid.reshape(ROWS, 2, 2, LOCAL, WAVES).transpose(0, 1, 3, 2, 4)  2.76 us
  transfers between devices with their start and end apart: 4, of which 3 were waited for; matrix products, arithmetic and copies ran while one was open for 2% of the time, Pallas kernels for 0%

profile of v4, /device:TPU:1, one launch (start us, length us, event | category | flops | bytes accessed | tf_op | source)
XLA Modules:
  0.0 136.7 jit_solution(4527932368413895595)
XLA Ops:
  0.6 0.0 copy-start.2
  0.6 0.0 copy-start.3
  0.7 0.0 copy-start.5
  0.7 0.0 copy-start.1
  0.7 0.0 copy-start
  0.7 1.9 %copy.9 = bf16[20,2,2,16,640]{4,3,2,1,0:T(8,128)(2,1)S(1)} copy(bf16[20,2,2,16,640]{4,2,3,1,0:T(2,128)(2,1)} %bitcast.27) | data formatting | bytes 3276800 | tf_op jit(solution)/shard_map/transpose | solution.py:337
  2.6 0.1 pad_add_fusion.place
  2.6 0.0 copy-done.2
  2.6 0.0 copy-done.3
  2.6 0.0 copy-done.5
  2.6 0.0 copy-done.1
  2.7 3.8 %shard_map.86 = (bf16[6656,128]{1,0:T(8,128)(2,1)S(1)}, bf16[640,640]{1,0:T(8,128)(2,1)S(1)}) custom-call(s32[2]{0:T(128)S(1)} %pad_add_fusion.place, s32[1280]{0:T(1024)S(1)} %copy-done.1, f32[20]{0:T(128)S(1)} %copy-done.5, bf16[20,64,640]{2,1,0:T(8,128)(2,1)S(1)} %bitcast.22, s32[640]{0:T(1024)S(1)} %copy-done.2, bf16[16,64]{1,0:T(8,128)(2,1)S(1)} %copy-done.3), custom_call_target="tpu_custom_call" | custom-call | tf_op jit(solution)/shard_map/pallas_call | solution.py:266
  6.5 0.0 copy-start.4
  6.5 60.4 %all_to_all.10 = bf16[256,13,2,128]{3,2,1,0:T(2,128)(2,1)S(1)} all-to-all(bf16[256,13,2,128]{3,2,1,0:T(2,128)(2,1)S(1)} %bitcast.24), channel_id=1, replica_groups={{0,1,2,3,4,5,6,7,8,9,10,11,12,13,14,15,16,17,18,19,20,21,22,23,24,25,26..., dimensions={0} | all-to-all | bytes 3407872 | tf_op jit(solution)/shard_map/all_to_all | solution.py:330
  66.9 0.0 copy-done
  66.9 0.0 copy-done.4
  66.9 12.0 %shard_map.87 = (bf16[10,16,640]{2,1,0:T(8,128)(2,1)S(1)}, bf16[10,16,640]{2,1,0:T(8,128)(2,1)S(1)}, bf16[10,16,640]{2,1,0:T(8,128)(2,1)S(1)}, bf16[10,16,640]{2,1,0:T(8,128)(2,1)S(1)}, bf16[6656,128]{1,0:T(8,128)(2,1)}) custom-call(s32[2]{0:T(128)S(1)} %pad_add_fusion.place, s32[640]{0:T(1024)S(1)} %copy-done.2, bf16[6656,128]{1,0:T(8,128)(2,1)S(1)} %bitcast.21, ...), custom_call_target="tpu_custom_call" | custom-call | tf_op jit(solution)/shard_map/pallas_call | solution.py:266
  78.9 7.1 %all-to-all-start.1 = ((bf16[256,13,2,128]{3,2,1,0:T(2,128)(2,1)}), bf16[256,13,2,128]{3,2,1,0:T(2,128)(2,1)S(1)}, u32[]{:S(2)}, u32[]{:S(2)}) async-start(bf16[256,13,2,128]{3,2,1,0:T(2,128)(2,1)} %bitcast.12), calls=%async_computation.1 | async-start | bytes 3407872 | tf_op jit(solution)/shard_map/all_to_all | solution.py:330
  86.0 1.5 %collective-permute-start = (bf16[10,16,640]{2,1,0:T(8,128)(2,1)S(1)}, bf16[10,16,640]{2,1,0:T(8,128)(2,1)}, u32[]{:S(2)}, u32[]{:S(2)}) collective-permute-start(bf16[10,16,640]{2,1,0:T(8,128)(2,1)S(1)} %get-tuple-element.11), channel_id=1, source_target_pairs={{0,1},{1,2},{2,3},{3,0},{4,5},{5,6},{6,7},{7,4},{8,9},{9,10},{10,1... | collective-permute-start | bytes 614408 | tf_op jit(solution)/shard_map/ppermute | solution.py:341
  87.5 2.4 %collective-permute-start.1 = (bf16[10,16,640]{2,1,0:T(8,128)(2,1)S(1)}, bf16[10,16,640]{2,1,0:T(8,128)(2,1)}, u32[]{:S(2)}, u32[]{:S(2)}) collective-permute-start(bf16[10,16,640]{2,1,0:T(8,128)(2,1)S(1)} %get-tuple-element.12), channel_id=1, source_target_pairs={{0,2},{1,3},{2,0},{3,1},{4,6},{5,7},{6,4},{7,5},{8,10},{9,11},{10,... | collective-permute-start | bytes 614408 | tf_op jit(solution)/shard_map/ppermute | solution.py:341
  89.9 1.2 collective-permute-start.2
  91.1 3.8 %collective-permute-done = bf16[10,16,640]{2,1,0:T(8,128)(2,1)} collective-permute-done((bf16[10,16,640]{2,1,0:T(8,128)(2,1)S(1)}, bf16[10,16,640]{2,1,0:T(8,128)(2,1)}, u32[]{:S(2)}, u32[]{:S(2)}) %collective-permute-start) | collective-permute-done | bytes 204832 | tf_op jit(solution)/shard_map/ppermute | solution.py:341
  94.9 10.3 %collective-permute-done.1 = bf16[10,16,640]{2,1,0:T(8,128)(2,1)} collective-permute-done((bf16[10,16,640]{2,1,0:T(8,128)(2,1)S(1)}, bf16[10,16,640]{2,1,0:T(8,128)(2,1)}, u32[]{:S(2)}, u32[]{:S(2)}) %collective-permute-start.1) | collective-permute-done | bytes 204832 | tf_op jit(solution)/shard_map/ppermute | solution.py:341
  105.3 0.0 collective-permute-done.2
  105.3 1.2 pad_maximum_fusion
  106.5 0.1 constant_dynamic-slice_fusion.3
  106.6 0.1 pad_maximum_fusion.1
  106.7 1.5 %copy.15 = bf16[2,2,10,16,640]{4,1,3,0,2:T(2,128)(2,1)} copy(bf16[2,2,10,16,640]{4,3,2,1,0:T(8,128)(2,1)S(1)} %bitcast.26) | data formatting | bytes 1638400 | tf_op jit(solution)/shard_map/reshape | solution.py:346
  108.3 22.8 %all-to-all-done.1 = bf16[256,13,2,128]{3,2,1,0:T(2,128)(2,1)S(1)} async-done(((bf16[256,13,2,128]{3,2,1,0:T(2,128)(2,1)}), bf16[256,13,2,128]{3,2,1,0:T(2,128)(2,1)S(1)}, u32[]{:S(2)}, u32[]{:S(2)}) %all-to-all-start.1) | async-done | bytes 1703968 | tf_op jit(solution)/shard_map/all_to_all | solution.py:330
  131.0 2.9 %shard_map.88 = bf16[20,64,640]{2,1,0:T(8,128)(2,1)S(1)} custom-call(s32[2]{0:T(128)S(1)} %pad_add_fusion.place, s32[1280]{0:T(1024)S(1)} %copy-done.1, bf16[6656,128]{1,0:T(8,128)(2,1)S(1)} %bitcast.20, bf16[640,640]{1,0:T(8,128)(2,1)S(1)} %get-tuple-element.15.hot), custom_call_target="tpu_custom_call" | custom-call | tf_op jit(solution)/shard_map/pallas_call | solution.py:266
  134.0 2.8 %copy.14 = bf16[20,2,2,16,640]{4,2,3,1,0:T(2,128)(2,1)} copy(bf16[20,2,2,16,640]{4,3,2,1,0:T(8,128)(2,1)S(1)} %bitcast.23) | data formatting | bytes 3276800 | tf_op jit(solution)/shard_map/reshape | solution.py:348
Async XLA Ops:
  0.6 2.0 %copy-start.2 = (s32[640]{0:T(1024)S(1)}, s32[640]{0:T(1024)}, u32[]{:S(2)}) copy-start(s32[640]{0:T(1024)} %folded.3) | copy-start | bytes 7684
  0.6 2.0 %copy-start.3 = (bf16[16,64]{1,0:T(8,128)(2,1)S(1)}, bf16[16,64]{1,0:T(8,128)(2,1)}, u32[]{:S(2)}) copy-start(bf16[16,64]{1,0:T(8,128)(2,1)} %vertical.1) | copy-start | bytes 6148
  0.7 2.0 %copy-start.5 = (f32[20]{0:T(128)S(1)}, f32[20]{0:T(128)}, u32[]{:S(2)}) copy-start(f32[20]{0:T(128)} %quad.1) | copy-start | bytes 244
  0.7 2.0 %copy-start.1 = (s32[1280]{0:T(1024)S(1)}, s32[1280]{0:T(1024)}, u32[]{:S(2)}) copy-start(s32[1280]{0:T(1024)} %counts.3) | copy-start | bytes 15364
  0.7 66.2 %copy-start = (bf16[10,640,640]{2,1,0:T(8,128)(2,1)S(1)}, bf16[10,640,640]{2,1,0:T(8,128)(2,1)}, u32[]{:S(2)}) copy-start(bf16[10,640,640]{2,1,0:T(8,128)(2,1)} %table.1) | copy-start | bytes 24576004
  6.5 60.4 %copy-start.4 = (f32[640]{0:T(1024)S(1)}, f32[640]{0:T(1024)}, u32[]{:S(2)}) copy-start(f32[640]{0:T(1024)} %damping.1) | copy-start | bytes 7684
  78.9 52.1 %all-to-all-start.1 = ((bf16[256,13,2,128]{3,2,1,0:T(2,128)(2,1)}), bf16[256,13,2,128]{3,2,1,0:T(2,128)(2,1)S(1)}, u32[]{:S(2)}, u32[]{:S(2)}) async-start(bf16[256,13,2,128]{3,2,1,0:T(2,128)(2,1)} %bitcast.12), calls=%async_computation.1 | async-start | bytes 3407872 | tf_op jit(solution)/shard_map/all_to_all | solution.py:330
  86.0 8.9 %collective-permute-start = (bf16[10,16,640]{2,1,0:T(8,128)(2,1)S(1)}, bf16[10,16,640]{2,1,0:T(8,128)(2,1)}, u32[]{:S(2)}, u32[]{:S(2)}) collective-permute-start(bf16[10,16,640]{2,1,0:T(8,128)(2,1)S(1)} %get-tuple-element.11), channel_id=1, source_target_pairs={{0,1},{1,2},{2,3},{3,0},{4,5},{5,6},{6,7},{7,4},{8,9},{9,10},{10,1... | collective-permute-start | bytes 614408 | tf_op jit(solution)/shard_map/ppermute | solution.py:341
  87.5 17.8 %collective-permute-start.1 = (bf16[10,16,640]{2,1,0:T(8,128)(2,1)S(1)}, bf16[10,16,640]{2,1,0:T(8,128)(2,1)}, u32[]{:S(2)}, u32[]{:S(2)}) collective-permute-start(bf16[10,16,640]{2,1,0:T(8,128)(2,1)S(1)} %get-tuple-element.12), channel_id=1, source_target_pairs={{0,2},{1,3},{2,0},{3,1},{4,6},{5,7},{6,4},{7,5},{8,10},{9,11},{10,... | collective-permute-start | bytes 614408 | tf_op jit(solution)/shard_map/ppermute | solution.py:341
  89.9 15.3 %collective-permute-start.2 = (bf16[10,16,640]{2,1,0:T(8,128)(2,1)S(1)}, bf16[10,16,640]{2,1,0:T(8,128)(2,1)}, u32[]{:S(2)}, u32[]{:S(2)}) collective-permute-start(bf16[10,16,640]{2,1,0:T(8,128)(2,1)S(1)} %get-tuple-element.13), channel_id=1, source_target_pairs={{0,3},{1,0},{2,1},{3,2},{4,7},{5,4},{6,5},{7,6},{8,11},{9,8},{10,9... | collective-permute-start | bytes 614408 | tf_op jit(solution)/shard_map/ppermute | solution.py:341

commit v5 on v4

--- a/solution.py
+++ b/solution.py
@@ -15,6 +15,7 @@
 LOCAL = 16
 WAVES = 640
 HALF = 640
+TILES = WAVES // 128
 QUADS = 5
 GROUP = QUADS * HEMI
 CHUNK = 26
@@ -109,7 +110,6 @@
         couple[pl.ds(x * LOCAL + 1, 8, stride=2), :] = pltpu.roll(lines, 64, 1)
     mixing = couple[:, :64].astype(BF16)
     damp = damping[...].reshape(1, WAVES)
-    degrees = lax.broadcasted_iota(jnp.int32, (64, WAVES), 1)
     lanes = lax.broadcasted_iota(jnp.int32, (512, 512), 1)
     swapped = ((lanes >> 7) << 5) | (((lanes >> 5) & 3) << 7) | (lanes & 31)
     order[...] = jnp.where(lax.broadcasted_iota(jnp.int32, (512, 512), 0) == swapped, 1.0, 0.0).astype(BF16)
@@ -149,37 +149,39 @@
             for k in range(8):
                 split(side, x, k, values[k * LOCAL : (k + 1) * LOCAL])
 
+    degrees = lax.broadcasted_iota(jnp.int32, (64, WAVES), 1)
+
+    def matching(slot):
+        return ((degrees ^ folded[place[0] * SLOTS + slot]) & 1) == 0
+
+    for slot in range(SLOTS):
+        products = jnp.dot(turned[slot], table[slot], preferred_element_type=F32)
+        spectra = jnp.where(matching(slot), products[:64], products[64:])
+        spectra = jnp.where(degrees >= folded[place[0] * SLOTS + slot], spectra, 0.0)
+        pieces[slot] = spectra.astype(BF16)
     stores = []
-
-    def one_slot(slot):
-        wave = folded[place[0] * SLOTS + slot]
-        products = jnp.dot(turned[slot], table[slot], preferred_element_type=F32)
-        matching = ((degrees ^ wave) & 1) == 0
-        spectra = jnp.where(matching, products[:64], products[64:])
-        spectra = jnp.where(degrees >= wave, spectra, 0.0).astype(BF16)
-        pieces[slot] = spectra
-        for o, ref in enumerate((own, first, second, third)):
-            ahead = pl.multiple_of(lax.rem(place[1] + o, LEV) * LOCAL, LOCAL)
-            store = pltpu.make_async_copy(pieces.at[slot, pl.ds(ahead, LOCAL), :], ref.at[slot], leave.at[slot, o])
-            store.start()
-            stores.append(store)
-        filtered = jnp.dot(mixing, spectra, preferred_element_type=F32) * damp
-        signed = jnp.where(matching, filtered, -filtered)
-        stacked = jnp.concatenate([filtered, signed], axis=0).astype(BF16)
-        values = lax.dot_general(stacked, table[slot], (((1,), (1,)), ((), ())), preferred_element_type=F32)
-        return [values[block * LOCAL : (block + 1) * LOCAL] for block in range(2 * LEV)]
-
-    for slot in range(8):
-        for block, values in enumerate(one_slot(slot)):
-            result[block, slot * LOCAL : (slot + 1) * LOCAL, :] = values
-    for slot in range(8, SLOTS):
-        for block, values in enumerate(one_slot(slot)):
-            side, x = divmod(block, LEV)
-            at = (x * 2 + slot - 8) * LOCAL
-            result[2 * LEV + side, at : at + LOCAL, :] = values
+    for o, ref in enumerate((own, first, second, third)):
+        ahead = pl.multiple_of(lax.rem(place[1] + o, LEV) * LOCAL, LOCAL)
+        store = pltpu.make_async_copy(pieces.at[:, pl.ds(ahead, LOCAL), :], ref, leave.at[o])
+        store.start()
+        stores.append(store)
+
+    for slot in range(SLOTS):
+        filtered = jnp.dot(mixing, pieces[slot], preferred_element_type=F32) * damp
+        signed = jnp.where(matching(slot), filtered, -filtered)
+        turned[slot] = jnp.concatenate([filtered, signed], axis=0).astype(BF16)
+    for slot in range(SLOTS):
+        result[slot] = lax.dot_general(
+            turned[slot], table[slot], (((1,), (1,)), ((), ())), preferred_element_type=F32
+        )
+
+    def gather(block, slots):
+        return [result[slot, block * LOCAL : (block + 1) * LOCAL, :] for slot in slots]
 
     for side in range(2):
-        natural[2 * LEV + side] = result[2 * LEV + side].T
+        natural[2 * LEV + side] = jnp.concatenate(
+            [part for x in range(LEV) for part in gather(side * LEV + x, (8, 9))], axis=0
+        ).T
         for quarter in range(QUADS):
             for a in range(4):
                 rest[side * GROUP + quarter * HEMI : side * GROUP + (quarter + 1) * HEMI, a * 128 : (a + 1) * 128] = (
@@ -188,7 +190,7 @@
     placed = jnp.dot(rest[...], order[...], preferred_element_type=F32)
     for side in range(2):
         for x in range(LEV):
-            natural[side * LEV + x] = result[side * LEV + x].T
+            natural[side * LEV + x] = jnp.concatenate(gather(side * LEV + x, range(8)), axis=0).T
             start = (side * HEMI * LEV + x) * CHUNK
             for row in range(ROWS):
                 stage[pl.ds(start + row, HEMI, stride=STRIDE), :] = natural[
@@ -198,30 +200,32 @@
                 stage[pl.ds(start + ROWS + quarter, HEMI, stride=STRIDE), :] = placed[
                     side * GROUP + quarter * HEMI : side * GROUP + (quarter + 1) * HEMI, x * 128 : (x + 1) * 128
                 ]
-        rows = pl.ds(side * HEMI * STRIDE, HEMI * STRIDE)
-        ready[rows, :] = stage[rows, :].astype(BF16)
-        store = pltpu.make_async_copy(ready.at[rows, :], out.at[rows, :], depart.at[side])
-        store.start()
-        stores.append(store)
+        for part in range(2):
+            rows = pl.ds((2 * side + part) * (TOTAL // 4), TOTAL // 4)
+            ready[rows, :] = stage[rows, :].astype(BF16)
+            store = pltpu.make_async_copy(ready.at[rows, :], out.at[rows, :], depart.at[2 * side + part])
+            store.start()
+            stores.append(store)
     for store in stores:
         store.wait()
 
 
-def homeward(place, counts, received, hot, grid, slots, stage):
+def homeward(place, counts, received, hot, out, grid, slots, stage, depart):
+    stores = []
     south = place[0] >= HEMI
     stage[...] = received[...].astype(F32)
     low = low_lanes(LOCAL)
-    lanes = 2 * lax.broadcasted_iota(jnp.int32, (LOCAL, WAVES), 1)
-
-    @pl.loop(0, QUADS, unroll=UNROLL)
-    def _(quarter):
+    lanes = 2 * lax.broadcasted_iota(jnp.int32, (LEV * LOCAL, WAVES), 1)
+
+    def one_quarter(quarter):
         where = jnp.where(south, QUADS - 1 - quarter, quarter)
 
         def get(x, row):
             return stage[pl.ds(x * CHUNK + row, OWN, stride=STRIDE), :]
 
         def put(x, a, tile, values):
-            slots[quarter, (x * 4 + a) * LOCAL : (x * 4 + a + 1) * LOCAL, tile * 128 : (tile + 1) * 128] = values.astype(BF16)
+            f, c = divmod(x, 2)
+            slots[quarter, tile, pl.ds(a * 64 + f * 32 + c, LOCAL, stride=2), :] = values
 
         for x in range(LEV):
             for a in (0, 2):
@@ -240,13 +244,21 @@
                 left, right = swap_halves(low, even, odd)
                 put(x, a, 4, left)
                 put(x + 1, a, 4, right)
-        values = jnp.dot(slots[quarter], hot[...], preferred_element_type=F32)
+        mixed = jnp.concatenate([slots[quarter, tile].astype(BF16) for tile in range(TILES)], axis=1)
+        values = jnp.dot(mixed, hot[...], preferred_element_type=F32)
         for at in range(4):
             row = quarter * 4 + jnp.where(south, 3 - at, at)
             count = counts[place[0] * ROWS + row]
-            for x in range(LEV):
-                part = values[(x * 4 + at) * LOCAL : (x * 4 + at + 1) * LOCAL]
-                grid[row, x * LOCAL : (x + 1) * LOCAL, :] = jnp.where(lanes < count, part, 0.0).astype(BF16)
+            part = jnp.where(lanes < count, values[at * 64 : (at + 1) * 64], 0.0).astype(BF16)
+            grid[row] = part.reshape(2, LOCAL, 2, WAVES)
+        rows = pl.ds(quarter * 4, 4)
+        stores.append(pltpu.make_async_copy(grid.at[rows], out.at[rows], depart.at[quarter]))
+        stores[-1].start()
+
+    for quarter in range(QUADS):
+        one_quarter(quarter)
+    for store in stores:
+        store.wait()
 
 
 def smem():
@@ -301,13 +313,13 @@
             ((SLOTS, 128, HALF), BF16),
             ((64, 128), F32),
             ((SLOTS, 64, WAVES), BF16),
-            ((2 * LEV + 2, 128, HALF), F32),
+            ((SLOTS, 128, HALF), F32),
             ((2 * GROUP, 512), BF16),
             ((512, 512), BF16),
             ((2 * LEV + 2, HALF, 128), F32),
             ((TOTAL, 128), BF16),
-            copies(SLOTS, LEV),
-            copies(2),
+            copies(LEV),
+            copies(4),
         ],
         far_outs=[(SLOTS, LOCAL, WAVES)] * LEV + [(TOTAL, 128)],
         limit=28 * 1024 * 1024,
@@ -315,12 +327,14 @@
 
 
 def call_homeward(place, counts, received, hot):
+    shape = (ROWS, 2, LOCAL, 2, WAVES)
     (grid,) = call(
         homeward,
         (place, counts),
         (received, hot),
-        [(ROWS, 64, WAVES)],
-        [((QUADS, 256, WAVES), BF16), ((TOTAL, 128), F32)],
+        [],
+        [(shape, BF16), ((QUADS, TILES, 256, 128), F32), ((TOTAL, 128), F32), copies(QUADS)],
+        far_outs=[shape],
     )
     return grid
 
@@ -345,7 +359,7 @@
     parts = jnp.stack([lax.dynamic_index_in_dim(parts, (lev - x) % LEV, 0, keepdims=False) for x in range(LEV)])
     spectral = parts.reshape(2, 2, SLOTS, LOCAL, WAVES).transpose(2, 0, 3, 1, 4)
     grid = call_homeward(place, counts, received, hot)
-    return spectral, grid.reshape(ROWS, 2, 2, LOCAL, WAVES).transpose(0, 1, 3, 2, 4)
+    return spectral, grid
 
 
 def solution(mesh):

time: 137 us -> 133 us (0.971)
  local copies, waits for them, and re-layouts: 6.28 us -> 3.52 us
  Pallas kernels: 18.7 us -> 17 us
    reshape x1 -> x0, local copies, waits for them, and re-layouts: 2.76 us -> none  [on_device(): grid.reshape(ROWS, 2, 2, LOCAL, WAVES).transpose(0, 1, 3, 2, 4)]
    pallas_call x3, Pallas kernels: 18.7 us -> 17 us  [call(): pl.pallas_call(kernel, in_specs=[smem() for _ in scalars] + [in_vmem() fo...]
where the time goes in v5:
time: 133 us; the launch traced here: 132 us
  blocking collectives  60.4 us (45%)
  waiting for transfers between devices  36.9 us (28%)
  Pallas kernels  17 us (13%)
  starting transfers between devices  12.2 us (9%)
  local copies, waits for them, and re-layouts  3.52 us (3%)
  other arithmetic  1.45 us (1%)
    all_to_all x1, blocking collectives, exchange(): lax.all_to_all(blocks, AXES, split_axis=0, concat_axis=0, tiled=True, axi...  60.4 us
    all_to_all x1, waiting for transfers between devices, exchange(): lax.all_to_all(blocks, AXES, split_axis=0, concat_axis=0, tiled=True, axi...  22.8 us
    pallas_call x3, Pallas kernels, call(): pl.pallas_call(kernel, in_specs=[smem() for _ in scalars] + [in_vmem() fo...  17 us
    ppermute x3, waiting for transfers between devices, on_device(): lax.ppermute(pieces[o], 'lev', [(i, (i + o) % LEV) for i in range(LEV)])  14.2 us
    all_to_all x1, starting transfers between devices, exchange(): lax.all_to_all(blocks, AXES, split_axis=0, concat_axis=0, tiled=True, axi...  7.16 us
    ppermute x3, starting transfers between devices, on_device(): lax.ppermute(pieces[o], 'lev', [(i, (i + o) % LEV) for i in range(LEV)])  5.06 us
  transfers between devices with their start and end apart: 4, of which 3 were waited for; matrix products, arithmetic and copies ran while one was open for 2% of the time, Pallas kernels for 0%

profile of v5, /device:TPU:1, one launch (start us, length us, event | category | flops | bytes accessed | tf_op | source)
XLA Modules:
  0.0 132.5 jit_solution(6053465930055083431)
XLA Ops:
  0.6 0.0 copy-start.2
  0.6 0.0 copy-start.3
  0.7 0.0 copy-start.5
  0.7 0.0 copy-start.1
  0.7 0.0 copy-start
  0.7 1.9 %copy.9 = bf16[20,2,2,16,640]{4,3,2,1,0:T(8,128)(2,1)S(1)} copy(bf16[20,2,2,16,640]{4,2,3,1,0:T(2,128)(2,1)} %bitcast.22) | data formatting | bytes 3276800 | tf_op jit(solution)/shard_map/transpose | solution.py:351
  2.6 0.1 pad_add_fusion.place
  2.6 0.0 copy-done.2
  2.6 0.0 copy-done.3
  2.6 0.0 copy-done.5
  2.6 0.0 copy-done.1
  2.7 3.8 %shard_map.86 = (bf16[6656,128]{1,0:T(8,128)(2,1)S(1)}, bf16[640,640]{1,0:T(8,128)(2,1)S(1)}) custom-call(s32[2]{0:T(128)S(1)} %pad_add_fusion.place, s32[1280]{0:T(1024)S(1)} %copy-done.1, f32[20]{0:T(128)S(1)} %copy-done.5, bf16[20,64,640]{2,1,0:T(8,128)(2,1)S(1)} %bitcast.18, s32[640]{0:T(1024)S(1)} %copy-done.2, bf16[16,64]{1,0:T(8,128)(2,1)S(1)} %copy-done.3), custom_call_target="tpu_custom_call" | custom-call | tf_op jit(solution)/shard_map/pallas_call | solution.py:278
  6.5 0.0 copy-start.4
  6.5 60.4 %all_to_all.10 = bf16[256,13,2,128]{3,2,1,0:T(2,128)(2,1)S(1)} all-to-all(bf16[256,13,2,128]{3,2,1,0:T(2,128)(2,1)S(1)} %bitcast.19), channel_id=1, replica_groups={{0,1,2,3,4,5,6,7,8,9,10,11,12,13,14,15,16,17,18,19,20,21,22,23,24,25,26..., dimensions={0} | all-to-all | bytes 3407872 | tf_op jit(solution)/shard_map/all_to_all | solution.py:344
  66.9 0.0 copy-done
  66.9 0.0 copy-done.4
  66.9 8.9 %shard_map.87 = (bf16[10,16,640]{2,1,0:T(8,128)(2,1)S(1)}, bf16[10,16,640]{2,1,0:T(8,128)(2,1)S(1)}, bf16[10,16,640]{2,1,0:T(8,128)(2,1)S(1)}, bf16[10,16,640]{2,1,0:T(8,128)(2,1)S(1)}, bf16[6656,128]{1,0:T(8,128)(2,1)}) custom-call(s32[2]{0:T(128)S(1)} %pad_add_fusion.place, s32[640]{0:T(1024)S(1)} %copy-done.2, bf16[6656,128]{1,0:T(8,128)(2,1)S(1)} %bitcast.17, ...), custom_call_target="tpu_custom_call" | custom-call | tf_op jit(solution)/shard_map/pallas_call | solution.py:278
  75.8 7.2 %all-to-all-start.1 = ((bf16[256,13,2,128]{3,2,1,0:T(2,128)(2,1)}), bf16[256,13,2,128]{3,2,1,0:T(2,128)(2,1)S(1)}, u32[]{:S(2)}, u32[]{:S(2)}) async-start(bf16[256,13,2,128]{3,2,1,0:T(2,128)(2,1)} %bitcast.12), calls=%async_computation.1 | async-start | bytes 3407872 | tf_op jit(solution)/shard_map/all_to_all | solution.py:344
  83.0 1.5 %collective-permute-start = (bf16[10,16,640]{2,1,0:T(8,128)(2,1)S(1)}, bf16[10,16,640]{2,1,0:T(8,128)(2,1)}, u32[]{:S(2)}, u32[]{:S(2)}) collective-permute-start(bf16[10,16,640]{2,1,0:T(8,128)(2,1)S(1)} %get-tuple-element.11), channel_id=1, source_target_pairs={{0,1},{1,2},{2,3},{3,0},{4,5},{5,6},{6,7},{7,4},{8,9},{9,10},{10,1... | collective-permute-start | bytes 614408 | tf_op jit(solution)/shard_map/ppermute | solution.py:355
  84.4 2.4 %collective-permute-start.1 = (bf16[10,16,640]{2,1,0:T(8,128)(2,1)S(1)}, bf16[10,16,640]{2,1,0:T(8,128)(2,1)}, u32[]{:S(2)}, u32[]{:S(2)}) collective-permute-start(bf16[10,16,640]{2,1,0:T(8,128)(2,1)S(1)} %get-tuple-element.12), channel_id=1, source_target_pairs={{0,2},{1,3},{2,0},{3,1},{4,6},{5,7},{6,4},{7,5},{8,10},{9,11},{10,... | collective-permute-start | bytes 614408 | tf_op jit(solution)/shard_map/ppermute | solution.py:355
  86.9 1.2 collective-permute-start.2
  88.0 3.8 %collective-permute-done = bf16[10,16,640]{2,1,0:T(8,128)(2,1)} collective-permute-done((bf16[10,16,640]{2,1,0:T(8,128)(2,1)S(1)}, bf16[10,16,640]{2,1,0:T(8,128)(2,1)}, u32[]{:S(2)}, u32[]{:S(2)}) %collective-permute-start) | collective-permute-done | bytes 204832 | tf_op jit(solution)/shard_map/ppermute | solution.py:355
  91.9 10.3 %collective-permute-done.1 = bf16[10,16,640]{2,1,0:T(8,128)(2,1)} collective-permute-done((bf16[10,16,640]{2,1,0:T(8,128)(2,1)S(1)}, bf16[10,16,640]{2,1,0:T(8,128)(2,1)}, u32[]{:S(2)}, u32[]{:S(2)}) %collective-permute-start.1) | collective-permute-done | bytes 204832 | tf_op jit(solution)/shard_map/ppermute | solution.py:355
  102.2 0.0 collective-permute-done.2
  102.2 1.2 pad_maximum_fusion
  103.4 0.1 constant_dynamic-slice_fusion.3
  103.5 0.1 pad_maximum_fusion.1
  103.7 1.5 %copy.12 = bf16[2,2,10,16,640]{4,1,3,0,2:T(2,128)(2,1)} copy(bf16[2,2,10,16,640]{4,3,2,1,0:T(8,128)(2,1)S(1)} %bitcast.21) | data formatting | bytes 1638400 | tf_op jit(solution)/shard_map/reshape | solution.py:360
  105.2 22.8 %all-to-all-done.1 = bf16[256,13,2,128]{3,2,1,0:T(2,128)(2,1)S(1)} async-done(((bf16[256,13,2,128]{3,2,1,0:T(2,128)(2,1)}), bf16[256,13,2,128]{3,2,1,0:T(2,128)(2,1)S(1)}, u32[]{:S(2)}, u32[]{:S(2)}) %all-to-all-start.1) | async-done | bytes 1703968 | tf_op jit(solution)/shard_map/all_to_all | solution.py:344
  128.0 4.4 %shard_map.88 = bf16[20,2,16,2,640]{4,3,2,1,0:T(2,128)(2,1)} custom-call(s32[2]{0:T(128)S(1)} %pad_add_fusion.place, s32[1280]{0:T(1024)S(1)} %copy-done.1, bf16[6656,128]{1,0:T(8,128)(2,1)S(1)} %bitcast.16, bf16[640,640]{1,0:T(8,128)(2,1)S(1)} %get-tuple-element.15.hot), custom_call_target="tpu_custom_call" | custom-call | tf_op jit(solution)/shard_map/pallas_call | solution.py:278
Async XLA Ops:
  0.6 2.0 %copy-start.2 = (s32[640]{0:T(1024)S(1)}, s32[640]{0:T(1024)}, u32[]{:S(2)}) copy-start(s32[640]{0:T(1024)} %folded.3) | copy-start | bytes 7684
  0.6 2.0 %copy-start.3 = (bf16[16,64]{1,0:T(8,128)(2,1)S(1)}, bf16[16,64]{1,0:T(8,128)(2,1)}, u32[]{:S(2)}) copy-start(bf16[16,64]{1,0:T(8,128)(2,1)} %vertical.1) | copy-start | bytes 6148
  0.7 2.0 %copy-start.5 = (f32[20]{0:T(128)S(1)}, f32[20]{0:T(128)}, u32[]{:S(2)}) copy-start(f32[20]{0:T(128)} %quad.1) | copy-start | bytes 244
  0.7 2.0 %copy-start.1 = (s32[1280]{0:T(1024)S(1)}, s32[1280]{0:T(1024)}, u32[]{:S(2)}) copy-start(s32[1280]{0:T(1024)} %counts.3) | copy-start | bytes 15364
  0.7 66.2 %copy-start = (bf16[10,640,640]{2,1,0:T(8,128)(2,1)S(1)}, bf16[10,640,640]{2,1,0:T(8,128)(2,1)}, u32[]{:S(2)}) copy-start(bf16[10,640,640]{2,1,0:T(8,128)(2,1)} %table.1) | copy-start | bytes 24576004
  6.5 60.4 %copy-start.4 = (f32[640]{0:T(1024)S(1)}, f32[640]{0:T(1024)}, u32[]{:S(2)}) copy-start(f32[640]{0:T(1024)} %damping.1) | copy-start | bytes 7684
  75.8 52.2 %all-to-all-start.1 = ((bf16[256,13,2,128]{3,2,1,0:T(2,128)(2,1)}), bf16[256,13,2,128]{3,2,1,0:T(2,128)(2,1)S(1)}, u32[]{:S(2)}, u32[]{:S(2)}) async-start(bf16[256,13,2,128]{3,2,1,0:T(2,128)(2,1)} %bitcast.12), calls=%async_computation.1 | async-start | bytes 3407872 | tf_op jit(solution)/shard_map/all_to_all | solution.py:344
  83.0 8.9 %collective-permute-start = (bf16[10,16,640]{2,1,0:T(8,128)(2,1)S(1)}, bf16[10,16,640]{2,1,0:T(8,128)(2,1)}, u32[]{:S(2)}, u32[]{:S(2)}) collective-permute-start(bf16[10,16,640]{2,1,0:T(8,128)(2,1)S(1)} %get-tuple-element.11), channel_id=1, source_target_pairs={{0,1},{1,2},{2,3},{3,0},{4,5},{5,6},{6,7},{7,4},{8,9},{9,10},{10,1... | collective-permute-start | bytes 614408 | tf_op jit(solution)/shard_map/ppermute | solution.py:355
  84.4 17.8 %collective-permute-start.1 = (bf16[10,16,640]{2,1,0:T(8,128)(2,1)S(1)}, bf16[10,16,640]{2,1,0:T(8,128)(2,1)}, u32[]{:S(2)}, u32[]{:S(2)}) collective-permute-start(bf16[10,16,640]{2,1,0:T(8,128)(2,1)S(1)} %get-tuple-element.12), channel_id=1, source_target_pairs={{0,2},{1,3},{2,0},{3,1},{4,6},{5,7},{6,4},{7,5},{8,10},{9,11},{10,... | collective-permute-start | bytes 614408 | tf_op jit(solution)/shard_map/ppermute | solution.py:355
  86.9 15.3 %collective-permute-start.2 = (bf16[10,16,640]{2,1,0:T(8,128)(2,1)S(1)}, bf16[10,16,640]{2,1,0:T(8,128)(2,1)}, u32[]{:S(2)}, u32[]{:S(2)}) collective-permute-start(bf16[10,16,640]{2,1,0:T(8,128)(2,1)S(1)} %get-tuple-element.13), channel_id=1, source_target_pairs={{0,3},{1,0},{2,1},{3,2},{4,7},{5,4},{6,5},{7,6},{8,11},{9,8},{10,9... | collective-permute-start | bytes 614408 | tf_op jit(solution)/shard_map/ppermute | solution.py:355

commit v6 on v5

v6 whole, which is shorter than its diff:
```python
import jax
import jax.numpy as jnp
from jax import lax
from jax.experimental import pallas as pl
from jax.experimental.pallas import tpu as pltpu
from jax.sharding import PartitionSpec as P

F32, BF16 = jnp.float32, jnp.bfloat16
AXES = ("lat", "lev")
OWN = 64
HEMI = 32
LEV = 4
ROWS = 20
SLOTS = 10
LOCAL = 16
PART = 2 * LOCAL
WIDE = LEV * PART
TAKEN = 5
KEPT = (0, 1, 2, 3, 5, 6, 7, 8, 4, 9)
WAVES = 640
HALF = 640
QUADS = 5
GROUP = QUADS * HEMI
CHUNK = 26
STRIDE = LEV * CHUNK
TOTAL = OWN * STRIDE
VMEM = 24 * 1024 * 1024
ORDER = [d if d < HEMI else OWN - 1 + HEMI - d for d in range(OWN)]
GROUPS = [[d * LEV + x for d in ORDER for x in range(LEV)]]


def low_lanes(rows):
    return lax.broadcasted_iota(jnp.int32, (rows, 128), 1) < 64


def one_hot(folded, column, hot):
    row = folded[...].astype(F32).reshape(1, WAVES)
    for t in range(WAVES // 128):
        lanes = slice(t * 128, (t + 1) * 128)
        column[lanes, :] = jnp.broadcast_to(row[:, lanes], (128, 128)).T
    i = lax.broadcasted_iota(jnp.int32, (OWN, OWN), 0)
    d = lax.broadcasted_iota(jnp.int32, (OWN, OWN), 1)
    turn = jnp.where(d == jnp.where(i < HEMI, i, OWN - 1 + HEMI - i), 1.0, 0.0).astype(BF16)
    lanes = lax.broadcasted_iota(jnp.int32, (OWN, 128), 1)
    for k in range(SLOTS):
        waves = column[pl.ds(KEPT[k], OWN, stride=SLOTS), :].astype(jnp.int32)
        plain = jnp.concatenate(
            [jnp.where(waves == lanes + t * 128, 1.0, 0.0).astype(BF16) for t in range(WAVES // 128)], axis=1
        )
        hot[k * OWN : (k + 1) * OWN, :] = jnp.dot(turn, plain, preferred_element_type=F32).astype(BF16)


def swap_halves(low, left, right):
    return jnp.where(low, left, pltpu.roll(right, 64, 1)), jnp.where(low, pltpu.roll(left, 64, 1), right)


def outward(place, counts, quad, fourier, folded, vertical, out, hot, weighted, stage, column, couple):
    south = place[0] >= HEMI
    one_hot(folded, column, hot)
    couple[...] = vertical[...].astype(F32)
    piece = 2 * lax.rem(place[0], 8)
    line = jnp.concatenate([couple[pl.ds(piece, 1), :], couple[pl.ds(piece + 1, 1), :]], axis=1)
    stage[pl.ds(CHUNK - 1, OWN * LEV, stride=CHUNK), :] = jnp.broadcast_to(line, (OWN * LEV, 128))
    lanes = 2 * lax.broadcasted_iota(jnp.int32, (2 * PART, WAVES), 1)
    low = low_lanes(PART)
    slotted = hot[...].T

    def one_quarter(quarter):
        where = jnp.where(south, QUADS - 1 - quarter, quarter)
        for a in range(4):
            row = quarter * 4 + a
            count = counts[place[0] * ROWS + row]
            product = fourier[row].astype(F32) * quad[row]
            at = pl.multiple_of(jnp.where(south, 3 - a, a) * 2 * PART, 2 * PART)
            weighted[quarter, pl.ds(at, 2 * PART), :] = jnp.where(lanes < count, product, 0.0).astype(BF16)
        spread = jnp.dot(weighted[quarter], slotted, preferred_element_type=F32)

        def part(f, a, tile):
            return spread[(a * 2 + f) * PART : (a * 2 + f + 1) * PART, tile * 128 : (tile + 1) * 128]

        def put(x, row, values):
            stage[pl.ds(x * CHUNK + row, OWN, stride=STRIDE), :] = values

        for f in range(2):
            for half in range(2):
                for a in (0, 2):
                    blocks = [
                        block
                        for tile in (2 * half, 2 * half + 1)
                        for block in swap_halves(low, part(f, a, tile), part(f, a + 1, tile))
                    ]
                    across = jnp.concatenate(blocks, axis=0).T
                    put(2 * f + half, where * 4 + a, across[:OWN])
                    put(2 * f + half, where * 4 + a + 1, across[OWN:])
            across = jnp.concatenate([part(f, a, 4) for a in range(4)], axis=0).T
            put(2 * f, ROWS + where, across[:OWN])
            put(2 * f + 1, ROWS + where, across[OWN:])

    for quarter in range(QUADS):
        one_quarter(quarter)
    out[...] = stage[...].astype(BF16)


def middle(
    place, folded, received, damping, table,
    own, first, second, third, out, stage, turned, couple, pieces, result, rest, order, natural, ready, leave, depart,
):
    stage[...] = received[...].astype(F32)
    for x in range(LEV):
        lines = stage[pl.ds(x * CHUNK + CHUNK - 1, 8, stride=STRIDE), :]
        couple[pl.ds(x * LOCAL, 8, stride=2), :] = lines
        couple[pl.ds(x * LOCAL + 1, 8, stride=2), :] = pltpu.roll(lines, 64, 1)
    target = lax.broadcasted_iota(jnp.int32, (WIDE, 64), 0)
    level = lax.broadcasted_iota(jnp.int32, (WIDE, 64), 1)
    after = jnp.where(target >> 1 == level, 1.0, 0.0).astype(BF16)
    before = jnp.where(((target >> 5) << 4) | (target & 15) == level, 1.0, 0.0).astype(BF16)
    mixing = jnp.dot(after, couple[:, :64].astype(BF16), preferred_element_type=F32).astype(BF16)
    mixing = lax.dot_general(mixing, before, (((1,), (1,)), ((), ())), preferred_element_type=F32)
    target = lax.broadcasted_iota(jnp.int32, (WIDE, WIDE), 0)
    source = lax.broadcasted_iota(jnp.int32, (WIDE, WIDE), 1)
    mixing = jnp.where((target & 1) == ((source >> 4) & 1), mixing, 0.0).astype(BF16)
    damp = damping[...].reshape(1, WAVES)
    lanes = lax.broadcasted_iota(jnp.int32, (512, 512), 1)
    swapped = ((lanes >> 7) << 5) | (((lanes >> 5) & 3) << 7) | (lanes & 31)
    order[...] = jnp.where(lax.broadcasted_iota(jnp.int32, (512, 512), 0) == swapped, 1.0, 0.0).astype(BF16)

    def both(x, row):
        north = stage[pl.ds(x * CHUNK + row, HEMI, stride=STRIDE), :]
        south = stage[pl.ds((HEMI * LEV + x) * CHUNK + row, HEMI, stride=STRIDE), :]
        return north + south, north - south

    for quarter in range(QUADS):
        rows = slice(quarter * HEMI, (quarter + 1) * HEMI)
        for x in range(LEV):
            for side, values in enumerate(both(x, ROWS + quarter)):
                rest[side * GROUP + quarter * HEMI : side * GROUP + (quarter + 1) * HEMI, x * 128 : (x + 1) * 128] = (
                    values.astype(BF16)
                )
    placed = jnp.dot(rest[...], order[...], preferred_element_type=F32)
    for side in range(2):
        for quarter in range(QUADS):
            for a in range(4):
                natural[2 * LEV + side, pl.ds(quarter * 4 + a, HEMI, stride=ROWS), :] = placed[
                    side * GROUP + quarter * HEMI : side * GROUP + (quarter + 1) * HEMI, a * 128 : (a + 1) * 128
                ]
        turned[TAKEN - 1, side * WIDE : (side + 1) * WIDE, :] = natural[2 * LEV + side].T.astype(BF16)
    for x in range(LEV):
        for row in range(ROWS):
            for side, values in enumerate(both(x, row)):
                natural[side * LEV + x, pl.ds(row, HEMI, stride=ROWS), :] = values
        for side in range(2):
            values = natural[side * LEV + x].T
            at = side * WIDE + x * PART
            for k in range(4):
                turned[k, at : at + PART, :] = values[k * PART : (k + 1) * PART].astype(BF16)

    degrees = lax.broadcasted_iota(jnp.int32, (WIDE, WAVES), 1)
    begin = lax.rem(place[1], 2) * TAKEN
    waves = [folded[place[0] * SLOTS + begin + slot] for slot in range(TAKEN)]

    def matching(slot):
        return ((degrees ^ waves[slot]) & 1) == 0

    for slot in range(TAKEN):
        products = jnp.dot(turned[slot], table[begin + slot], preferred_element_type=F32)
        spectra = jnp.where(matching(slot), products[:WIDE], products[WIDE:])
        pieces[slot] = jnp.where(degrees >= waves[slot], spectra, 0.0).astype(BF16)
    stores = []
    for o, ref in enumerate((own, first, second, third)):
        ahead = pl.multiple_of(lax.rem(place[1] + o, LEV) * PART, PART)
        store = pltpu.make_async_copy(pieces.at[:, pl.ds(ahead, PART), :], ref, leave.at[o])
        store.start()
        stores.append(store)

    for slot in range(TAKEN):
        filtered = jnp.dot(mixing, pieces[slot], preferred_element_type=F32) * damp
        signed = jnp.where(matching(slot), filtered, -filtered)
        turned[slot] = jnp.concatenate([filtered, signed], axis=0).astype(BF16)
    for slot in range(TAKEN):
        result[slot] = lax.dot_general(
            turned[slot], table[begin + slot], (((1,), (1,)), ((), ())), preferred_element_type=F32
        )

    for side in range(2):
        natural[2 * LEV + side] = result[TAKEN - 1, side * WIDE : (side + 1) * WIDE, :].T
        for quarter in range(QUADS):
            for a in range(4):
                rest[side * GROUP + quarter * HEMI : side * GROUP + (quarter + 1) * HEMI, a * 128 : (a + 1) * 128] = (
                    natural[2 * LEV + side, pl.ds(quarter * 4 + a, HEMI, stride=ROWS), :].astype(BF16)
                )
    placed = jnp.dot(rest[...], order[...], preferred_element_type=F32)
    for side in range(2):
        for x in range(LEV):
            at = side * WIDE + x * PART
            natural[side * LEV + x] = jnp.concatenate([result[k, at : at + PART, :] for k in range(4)], axis=0).T
            start = (side * HEMI * LEV + x) * CHUNK
            for row in range(ROWS):
                stage[pl.ds(start + row, HEMI, stride=STRIDE), :] = natural[
                    side * LEV + x, pl.ds(row, HEMI, stride=ROWS), :
                ]
            for quarter in range(QUADS):
                stage[pl.ds(start + ROWS + quarter, HEMI, stride=STRIDE), :] = placed[
                    side * GROUP + quarter * HEMI : side * GROUP + (quarter + 1) * HEMI, x * 128 : (x + 1) * 128
                ]
        for part in range(2):
            rows = pl.ds((2 * side + part) * (TOTAL // 4), TOTAL // 4)
            ready[rows, :] = stage[rows, :].astype(BF16)
            store = pltpu.make_async_copy(ready.at[rows, :], out.at[rows, :], depart.at[2 * side + part])
            store.start()
            stores.append(store)
    for store in stores:
        store.wait()


def homeward(place, counts, received, hot, out, grid, slots, stage, depart):
    stores = []
    south = place[0] >= HEMI
    stage[...] = received[...].astype(F32)
    low = low_lanes(PART)
    lanes = 2 * lax.broadcasted_iota(jnp.int32, (LEV * LOCAL, WAVES), 1)

    def collect(quarter):
        where = jnp.where(south, QUADS - 1 - quarter, quarter)

        def get(x, row):
            return stage[pl.ds(x * CHUNK + row, OWN, stride=STRIDE), :]

        def put(f, a, tile, values):
            rows = slice((a * 2 + f) * PART, (a * 2 + f + 1) * PART)
            slots[quarter, rows, tile * 128 : (tile + 1) * 128] = values

        for f in range(2):
            for half in range(2):
                for a in (0, 2):
                    x = 2 * f + half
                    values = jnp.concatenate([get(x, where * 4 + a), get(x, where * 4 + a + 1)], axis=0).T
                    for tile in range(2):
                        even = values[2 * tile * PART : (2 * tile + 1) * PART]
                        odd = values[(2 * tile + 1) * PART : (2 * tile + 2) * PART]
                        left, right = swap_halves(low, even, odd)
                        put(f, a, 2 * half + tile, left)
                        put(f, a + 1, 2 * half + tile, right)
            values = jnp.concatenate([get(2 * f, ROWS + where), get(2 * f + 1, ROWS + where)], axis=0).T
            for a in range(4):
                put(f, a, 4, values[a * PART : (a + 1) * PART])

    def finish(quarter):
        values = jnp.dot(slots[quarter].astype(BF16), hot[...], preferred_element_type=F32)
        for at in range(4):
            row = quarter * 4 + jnp.where(south, 3 - at, at)
            count = counts[place[0] * ROWS + row]
            part = jnp.where(lanes < count, values[at * 64 : (at + 1) * 64], 0.0).astype(BF16)
            grid[row] = part.reshape(2, LOCAL, 2, WAVES)
        rows = pl.ds(quarter * 4, 4)
        stores.append(pltpu.make_async_copy(grid.at[rows], out.at[rows], depart.at[quarter]))
        stores[-1].start()

    for quarter in range(QUADS):
        collect(quarter)
    for quarter in range(QUADS):
        finish(quarter)
    for store in stores:
        store.wait()


def smem():
    return pl.BlockSpec(memory_space=pltpu.SMEM)


def in_vmem():
    return pl.BlockSpec(memory_space=pltpu.VMEM)


def in_hbm():
    return pl.BlockSpec(memory_space=pltpu.HBM)


def call(kernel, scalars, arrays, outs, scratch, far_outs=(), limit=VMEM):
    shapes = [jax.ShapeDtypeStruct(shape, BF16) for shape in (*far_outs, *outs)]
    return pl.pallas_call(
        kernel,
        in_specs=[smem() for _ in scalars] + [in_vmem() for _ in arrays],
        out_specs=[in_hbm() for _ in far_outs] + [in_vmem() for _ in outs],
        out_shape=shapes,
        scratch_shapes=[
            kind(shape, dtype) if dtype is not None else kind(shape)
            for kind, shape, dtype in ((pltpu.VMEM, *s) if len(s) == 2 else s for s in scratch)
        ],
        compiler_params=pltpu.CompilerParams(vmem_limit_bytes=limit),
    )(*scalars, *arrays)


def copies(*shape):
    return (pltpu.SemaphoreType.DMA, shape, None)


def call_outward(place, counts, quadrature, fourier, folded, vertical):
    return call(
        outward,
        (place, counts, quadrature),
        (fourier, folded, vertical),
        [(TOTAL, 128), (WAVES, WAVES)],
        [
            ((QUADS, 256, WAVES), BF16),
            ((TOTAL, 128), F32),
            ((WAVES, 128), F32),
            ((LOCAL, LEV * LOCAL), F32),
        ],
    )


def call_middle(place, folded, received, table, damping):
    return call(
        middle,
        (place, folded),
        (received, damping, table),
        [],
        [
            ((TOTAL, 128), F32),
            ((TAKEN, 2 * WIDE, HALF), BF16),
            ((64, 128), F32),
            ((TAKEN, WIDE, WAVES), BF16),
            ((TAKEN, 2 * WIDE, HALF), F32),
            ((2 * GROUP, 512), BF16),
            ((512, 512), BF16),
            ((2 * LEV + 2, HALF, 128), F32),
            ((TOTAL, 128), BF16),
            copies(LEV),
            copies(4),
        ],
        far_outs=[(TAKEN, PART, WAVES)] * LEV + [(TOTAL, 128)],
        limit=28 * 1024 * 1024,
    )


def call_homeward(place, counts, received, hot):
    shape = (ROWS, 2, LOCAL, 2, WAVES)
    (grid,) = call(
        homeward,
        (place, counts),
        (received, hot),
        [],
        [(shape, BF16), ((QUADS, 256, WAVES), F32), ((TOTAL, 128), F32), copies(QUADS)],
        far_outs=[shape],
    )
    return grid


def exchange(blocks):
    blocks = blocks.reshape(TOTAL // 2, 2, 128).reshape(OWN * LEV, CHUNK // 2, 2, 128)
    blocks = lax.all_to_all(blocks, AXES, split_axis=0, concat_axis=0, tiled=True, axis_index_groups=GROUPS)
    return blocks.reshape(TOTAL // 2, 2, 128).reshape(TOTAL, 128)


def on_device(fourier, quadrature, counts, folded, basis, vertical, damping):
    lev = lax.axis_index("lev").astype(jnp.int32)
    place = jnp.stack([lax.axis_index("lat").astype(jnp.int32), lev])
    fourier = fourier.transpose(0, 1, 3, 2, 4).reshape(ROWS, 2 * PART, WAVES)
    sent, hot = call_outward(place, counts, quadrature, fourier, folded, vertical)
    *pieces, sent = call_middle(place, folded, exchange(sent), basis, damping)
    parts = pieces[:1] + [
        lax.ppermute(pieces[o], "lev", [(i, (i + o) % LEV) for i in range(LEV)]) for o in range(1, LEV)
    ]
    received = exchange(sent)
    parts = jnp.stack(parts)
    parts = jnp.stack([lax.dynamic_index_in_dim(parts, (lev - x) % LEV, 0, keepdims=False) for x in range(LEV)])
    parts = parts.reshape(2, 2, TAKEN, 2, LOCAL, WAVES).transpose(1, 2, 0, 4, 3, 5)
    spectral = parts.reshape(SLOTS, 2, LOCAL, 2, WAVES)
    grid = call_homeward(place, counts, received, hot)
    return spectral, grid


def solution(mesh):
    return jax.shard_map(
        on_device,
        mesh=mesh,
        in_specs=(
            P("lat", None, "lev", None, None),
            P("lat"),
            P(),
            P(),
            P("lat", None, None),
            P("lev", None),
            P(),
        ),
        out_specs=(P("lat", None, "lev", None, None), P("lat", None, "lev", None, None)),
        check_vma=False,
    )
```

time: 133 us -> 132 us (level)
    reshape x1 -> x0, local copies, waits for them, and re-layouts: 1.55 us -> none  [on_device(): spectral = parts.reshape(2, 2, SLOTS, LOCAL, WAVES).transpose(2, 0, 3, 1, 4)]
    transpose x1 -> x2, local copies, waits for them, and re-layouts: 1.86 us -> 3.41 us  [the longest x1 1.86 us: on_device(): fourier = fourier.transpose(0, 1, 3, 2, 4).reshape(ROWS, 2 * PART, WAVES)]
where the time goes in v6:
time: 132 us
  blocking collectives  60.4 us (46%)
  waiting for transfers between devices  36.7 us (28%)
  Pallas kernels  16.4 us (12%)
  starting transfers between devices  12.2 us (9%)
  local copies, waits for them, and re-layouts  3.56 us (3%)
  other arithmetic  1.45 us (1%)
    all_to_all x1, blocking collectives, exchange(): lax.all_to_all(blocks, AXES, split_axis=0, concat_axis=0, tiled=True, axi...  60.4 us
    all_to_all x1, waiting for transfers between devices, exchange(): lax.all_to_all(blocks, AXES, split_axis=0, concat_axis=0, tiled=True, axi...  22.5 us
    pallas_call x3, Pallas kernels, call(): pl.pallas_call(kernel, in_specs=[smem() for _ in scalars] + [in_vmem() fo...  16.4 us
    ppermute x3, waiting for transfers between devices, on_device(): lax.ppermute(pieces[o], 'lev', [(i, (i + o) % LEV) for i in range(LEV)])  14.2 us
    all_to_all x1, starting transfers between devices, exchange(): lax.all_to_all(blocks, AXES, split_axis=0, concat_axis=0, tiled=True, axi...  6.98 us
    ppermute x3, starting transfers between devices, on_device(): lax.ppermute(pieces[o], 'lev', [(i, (i + o) % LEV) for i in range(LEV)])  5.24 us
  transfers between devices with their start and end apart: 4, of which 3 were waited for; matrix products, arithmetic and copies ran while one was open for 2% of the time, Pallas kernels for 0%

profile of v6, /device:TPU:1, one launch (start us, length us, event | category | flops | bytes accessed | tf_op | source)
XLA Modules:
  0.0 131.7 jit_solution(2304501426109129721)
XLA Ops:
  0.6 0.0 copy-start.2
  0.6 0.0 copy-start.3
  0.7 0.0 copy-start.5
  0.7 0.0 copy-start.1
  0.7 0.0 copy-start
  0.7 1.9 %copy.9 = bf16[20,2,2,16,640]{4,3,2,1,0:T(8,128)(2,1)S(1)} copy(bf16[20,2,2,16,640]{4,2,3,1,0:T(2,128)(2,1)} %bitcast.22) | data formatting | bytes 3276800 | tf_op jit(solution)/shard_map/transpose | solution.py:358
  2.6 0.1 pad_add_fusion.place
  2.6 0.0 copy-done.2
  2.6 0.0 copy-done.3
  2.6 0.0 copy-done.5
  2.6 0.0 copy-done.1
  2.7 4.0 %shard_map.86 = (bf16[6656,128]{1,0:T(8,128)(2,1)S(1)}, bf16[640,640]{1,0:T(8,128)(2,1)S(1)}) custom-call(s32[2]{0:T(128)S(1)} %pad_add_fusion.place, s32[1280]{0:T(1024)S(1)} %copy-done.1, f32[20]{0:T(128)S(1)} %copy-done.5, bf16[20,64,640]{2,1,0:T(8,128)(2,1)S(1)} %bitcast.18, s32[640]{0:T(1024)S(1)} %copy-done.2, bf16[16,64]{1,0:T(8,128)(2,1)S(1)} %copy-done.3), custom_call_target="tpu_custom_call" | custom-call | tf_op jit(solution)/shard_map/pallas_call | solution.py:280
  6.7 0.0 copy-start.4
  6.7 60.4 %all_to_all.10 = bf16[256,13,2,128]{3,2,1,0:T(2,128)(2,1)S(1)} all-to-all(bf16[256,13,2,128]{3,2,1,0:T(2,128)(2,1)S(1)} %bitcast.19), channel_id=1, replica_groups={{0,1,2,3,4,5,6,7,8,9,10,11,12,13,14,15,16,17,18,19,20,21,22,23,24,25,26..., dimensions={0} | all-to-all | bytes 3407872 | tf_op jit(solution)/shard_map/all_to_all | solution.py:351
  67.1 0.0 copy-done
  67.1 0.0 copy-done.4
  67.1 7.8 %shard_map.87 = (bf16[5,32,640]{2,1,0:T(8,128)(2,1)S(1)}, bf16[5,32,640]{2,1,0:T(8,128)(2,1)S(1)}, bf16[5,32,640]{2,1,0:T(8,128)(2,1)S(1)}, bf16[5,32,640]{2,1,0:T(8,128)(2,1)S(1)}, bf16[6656,128]{1,0:T(8,128)(2,1)}) custom-call(s32[2]{0:T(128)S(1)} %pad_add_fusion.place, s32[640]{0:T(1024)S(1)} %copy-done.2, bf16[6656,128]{1,0:T(8,128)(2,1)S(1)} %bitcast.17, ...), custom_call_target="tpu_custom_call" | custom-call | tf_op jit(solution)/shard_map/pallas_call | solution.py:280
  75.0 7.0 %all-to-all-start.1 = ((bf16[256,13,2,128]{3,2,1,0:T(2,128)(2,1)}), bf16[256,13,2,128]{3,2,1,0:T(2,128)(2,1)S(1)}, u32[]{:S(2)}, u32[]{:S(2)}) async-start(bf16[256,13,2,128]{3,2,1,0:T(2,128)(2,1)} %bitcast.13), calls=%async_computation.1 | async-start | bytes 3407872 | tf_op jit(solution)/shard_map/all_to_all | solution.py:351
  81.9 1.7 %collective-permute-start = (bf16[5,32,640]{2,1,0:T(8,128)(2,1)S(1)}, bf16[5,32,640]{2,1,0:T(8,128)(2,1)}, u32[]{:S(2)}, u32[]{:S(2)}) collective-permute-start(bf16[5,32,640]{2,1,0:T(8,128)(2,1)S(1)} %get-tuple-element.11), channel_id=1, source_target_pairs={{0,1},{1,2},{2,3},{3,0},{4,5},{5,6},{6,7},{7,4},{8,9},{9,10},{10,1... | collective-permute-start | bytes 614408 | tf_op jit(solution)/shard_map/ppermute | solution.py:362
  83.6 2.4 %collective-permute-start.1 = (bf16[5,32,640]{2,1,0:T(8,128)(2,1)S(1)}, bf16[5,32,640]{2,1,0:T(8,128)(2,1)}, u32[]{:S(2)}, u32[]{:S(2)}) collective-permute-start(bf16[5,32,640]{2,1,0:T(8,128)(2,1)S(1)} %get-tuple-element.12), channel_id=1, source_target_pairs={{0,2},{1,3},{2,0},{3,1},{4,6},{5,7},{6,4},{7,5},{8,10},{9,11},{10,... | collective-permute-start | bytes 614408 | tf_op jit(solution)/shard_map/ppermute | solution.py:362
  86.0 1.2 collective-permute-start.2
  87.2 3.5 %collective-permute-done = bf16[5,32,640]{2,1,0:T(8,128)(2,1)} collective-permute-done((bf16[5,32,640]{2,1,0:T(8,128)(2,1)S(1)}, bf16[5,32,640]{2,1,0:T(8,128)(2,1)}, u32[]{:S(2)}, u32[]{:S(2)}) %collective-permute-start) | collective-permute-done | bytes 204832 | tf_op jit(solution)/shard_map/ppermute | solution.py:362
  90.7 10.7 %collective-permute-done.1 = bf16[5,32,640]{2,1,0:T(8,128)(2,1)} collective-permute-done((bf16[5,32,640]{2,1,0:T(8,128)(2,1)S(1)}, bf16[5,32,640]{2,1,0:T(8,128)(2,1)}, u32[]{:S(2)}, u32[]{:S(2)}) %collective-permute-start.1) | collective-permute-done | bytes 204832 | tf_op jit(solution)/shard_map/ppermute | solution.py:362
  101.4 0.0 collective-permute-done.2
  101.4 1.2 pad_maximum_fusion
  102.7 0.1 constant_dynamic-slice_fusion.3
  102.8 0.1 pad_maximum_fusion.1
  102.9 1.5 %copy.10 = bf16[2,5,2,16,2,640]{5,4,3,2,1,0:T(2,128)(2,1)} copy(bf16[2,5,2,16,2,640]{5,3,4,1,0,2:T(8,128)(2,1)S(1)} %bitcast.21) | data formatting | bytes 1638400 | tf_op jit(solution)/shard_map/transpose | solution.py:367
  104.5 22.5 %all-to-all-done.1 = bf16[256,13,2,128]{3,2,1,0:T(2,128)(2,1)S(1)} async-done(((bf16[256,13,2,128]{3,2,1,0:T(2,128)(2,1)}), bf16[256,13,2,128]{3,2,1,0:T(2,128)(2,1)S(1)}, u32[]{:S(2)}, u32[]{:S(2)}) %all-to-all-start.1) | async-done | bytes 1703968 | tf_op jit(solution)/shard_map/all_to_all | solution.py:351
  127.0 4.5 %shard_map.88 = bf16[20,2,16,2,640]{4,3,2,1,0:T(2,128)(2,1)} custom-call(s32[2]{0:T(128)S(1)} %pad_add_fusion.place, s32[1280]{0:T(1024)S(1)} %copy-done.1, bf16[6656,128]{1,0:T(8,128)(2,1)S(1)} %bitcast.16, bf16[640,640]{1,0:T(8,128)(2,1)S(1)} %get-tuple-element.15.hot), custom_call_target="tpu_custom_call" | custom-call | tf_op jit(solution)/shard_map/pallas_call | solution.py:280
Async XLA Ops:
  0.6 2.0 %copy-start.2 = (s32[640]{0:T(1024)S(1)}, s32[640]{0:T(1024)}, u32[]{:S(2)}) copy-start(s32[640]{0:T(1024)} %folded.3) | copy-start | bytes 7684
  0.6 2.0 %copy-start.3 = (bf16[16,64]{1,0:T(8,128)(2,1)S(1)}, bf16[16,64]{1,0:T(8,128)(2,1)}, u32[]{:S(2)}) copy-start(bf16[16,64]{1,0:T(8,128)(2,1)} %vertical.1) | copy-start | bytes 6148
  0.7 2.0 %copy-start.5 = (f32[20]{0:T(128)S(1)}, f32[20]{0:T(128)}, u32[]{:S(2)}) copy-start(f32[20]{0:T(128)} %quad.1) | copy-start | bytes 244
  0.7 2.0 %copy-start.1 = (s32[1280]{0:T(1024)S(1)}, s32[1280]{0:T(1024)}, u32[]{:S(2)}) copy-start(s32[1280]{0:T(1024)} %counts.3) | copy-start | bytes 15364
  0.7 66.5 %copy-start = (bf16[10,640,640]{2,1,0:T(8,128)(2,1)S(1)}, bf16[10,640,640]{2,1,0:T(8,128)(2,1)}, u32[]{:S(2)}) copy-start(bf16[10,640,640]{2,1,0:T(8,128)(2,1)} %table.1) | copy-start | bytes 24576004
  6.7 60.4 %copy-start.4 = (f32[640]{0:T(1024)S(1)}, f32[640]{0:T(1024)}, u32[]{:S(2)}) copy-start(f32[640]{0:T(1024)} %damping.1) | copy-start | bytes 7684
  75.0 52.0 %all-to-all-start.1 = ((bf16[256,13,2,128]{3,2,1,0:T(2,128)(2,1)}), bf16[256,13,2,128]{3,2,1,0:T(2,128)(2,1)S(1)}, u32[]{:S(2)}, u32[]{:S(2)}) async-start(bf16[256,13,2,128]{3,2,1,0:T(2,128)(2,1)} %bitcast.13), calls=%async_computation.1 | async-start | bytes 3407872 | tf_op jit(solution)/shard_map/all_to_all | solution.py:351
  81.9 8.7 %collective-permute-start = (bf16[5,32,640]{2,1,0:T(8,128)(2,1)S(1)}, bf16[5,32,640]{2,1,0:T(8,128)(2,1)}, u32[]{:S(2)}, u32[]{:S(2)}) collective-permute-start(bf16[5,32,640]{2,1,0:T(8,128)(2,1)S(1)} %get-tuple-element.11), channel_id=1, source_target_pairs={{0,1},{1,2},{2,3},{3,0},{4,5},{5,6},{6,7},{7,4},{8,9},{9,10},{10,1... | collective-permute-start | bytes 614408 | tf_op jit(solution)/shard_map/ppermute | solution.py:362
  83.6 17.8 %collective-permute-start.1 = (bf16[5,32,640]{2,1,0:T(8,128)(2,1)S(1)}, bf16[5,32,640]{2,1,0:T(8,128)(2,1)}, u32[]{:S(2)}, u32[]{:S(2)}) collective-permute-start(bf16[5,32,640]{2,1,0:T(8,128)(2,1)S(1)} %get-tuple-element.12), channel_id=1, source_target_pairs={{0,2},{1,3},{2,0},{3,1},{4,6},{5,7},{6,4},{7,5},{8,10},{9,11},{10,... | collective-permute-start | bytes 614408 | tf_op jit(solution)/shard_map/ppermute | solution.py:362
  86.0 15.4 %collective-permute-start.2 = (bf16[5,32,640]{2,1,0:T(8,128)(2,1)S(1)}, bf16[5,32,640]{2,1,0:T(8,128)(2,1)}, u32[]{:S(2)}, u32[]{:S(2)}) collective-permute-start(bf16[5,32,640]{2,1,0:T(8,128)(2,1)S(1)} %get-tuple-element.13), channel_id=1, source_target_pairs={{0,3},{1,0},{2,1},{3,2},{4,7},{5,4},{6,5},{7,6},{8,11},{9,8},{10,9... | collective-permute-start | bytes 614408 | tf_op jit(solution)/shard_map/ppermute | solution.py:362

commit v7 on v6

--- a/solution.py
+++ b/solution.py
@@ -165,13 +165,6 @@
         products = jnp.dot(turned[slot], table[begin + slot], preferred_element_type=F32)
         spectra = jnp.where(matching(slot), products[:WIDE], products[WIDE:])
         pieces[slot] = jnp.where(degrees >= waves[slot], spectra, 0.0).astype(BF16)
-    stores = []
-    for o, ref in enumerate((own, first, second, third)):
-        ahead = pl.multiple_of(lax.rem(place[1] + o, LEV) * PART, PART)
-        store = pltpu.make_async_copy(pieces.at[:, pl.ds(ahead, PART), :], ref, leave.at[o])
-        store.start()
-        stores.append(store)
-
     for slot in range(TAKEN):
         filtered = jnp.dot(mixing, pieces[slot], preferred_element_type=F32) * damp
         signed = jnp.where(matching(slot), filtered, -filtered)
@@ -180,6 +173,13 @@
         result[slot] = lax.dot_general(
             turned[slot], table[begin + slot], (((1,), (1,)), ((), ())), preferred_element_type=F32
         )
+
+    stores = []
+    for o, ref in enumerate((own, first, second, third)):
+        ahead = pl.multiple_of(lax.rem(place[1] + o, LEV) * PART, PART)
+        store = pltpu.make_async_copy(pieces.at[:, pl.ds(ahead, PART), :], ref, leave.at[o])
+        store.start()
+        stores.append(store)
 
     for side in range(2):
         natural[2 * LEV + side] = result[TAKEN - 1, side * WIDE : (side + 1) * WIDE, :].T

time: 132 us -> 132 us (level)
  no operation moved by 1% of the time
where the time goes in v7:
time: 132 us
  blocking collectives  60.4 us (46%)
  waiting for transfers between devices  36.7 us (28%)
  Pallas kernels  16.4 us (12%)
  starting transfers between devices  12.2 us (9%)
  local copies, waits for them, and re-layouts  3.56 us (3%)
  other arithmetic  1.45 us (1%)
    all_to_all x1, blocking collectives, exchange(): lax.all_to_all(blocks, AXES, split_axis=0, concat_axis=0, tiled=True, axi...  60.4 us
    all_to_all x1, waiting for transfers between devices, exchange(): lax.all_to_all(blocks, AXES, split_axis=0, concat_axis=0, tiled=True, axi...  22.5 us
    pallas_call x3, Pallas kernels, call(): pl.pallas_call(kernel, in_specs=[smem() for _ in scalars] + [in_vmem() fo...  16.4 us
    ppermute x3, waiting for transfers between devices, on_device(): lax.ppermute(pieces[o], 'lev', [(i, (i + o) % LEV) for i in range(LEV)])  14.2 us
    all_to_all x1, starting transfers between devices, exchange(): lax.all_to_all(blocks, AXES, split_axis=0, concat_axis=0, tiled=True, axi...  6.98 us
    ppermute x3, starting transfers between devices, on_device(): lax.ppermute(pieces[o], 'lev', [(i, (i + o) % LEV) for i in range(LEV)])  5.24 us
  transfers between devices with their start and end apart: 4, of which 3 were waited for; matrix products, arithmetic and copies ran while one was open for 2% of the time, Pallas kernels for 0%

profile of v7, /device:TPU:1, one launch (start us, length us, event | category | flops | bytes accessed | tf_op | source)
XLA Modules:
  0.0 131.7 jit_solution(12021946401800225322)
XLA Ops:
  0.6 0.0 copy-start.2
  0.6 0.0 copy-start.3
  0.7 0.0 copy-start.5
  0.7 0.0 copy-start.1
  0.7 0.0 copy-start
  0.7 1.9 %copy.9 = bf16[20,2,2,16,640]{4,3,2,1,0:T(8,128)(2,1)S(1)} copy(bf16[20,2,2,16,640]{4,2,3,1,0:T(2,128)(2,1)} %bitcast.22) | data formatting | bytes 3276800 | tf_op jit(solution)/shard_map/transpose | solution.py:358
  2.6 0.1 pad_add_fusion.place
  2.6 0.0 copy-done.2
  2.6 0.0 copy-done.3
  2.6 0.0 copy-done.5
  2.6 0.0 copy-done.1
  2.7 4.0 %shard_map.86 = (bf16[6656,128]{1,0:T(8,128)(2,1)S(1)}, bf16[640,640]{1,0:T(8,128)(2,1)S(1)}) custom-call(s32[2]{0:T(128)S(1)} %pad_add_fusion.place, s32[1280]{0:T(1024)S(1)} %copy-done.1, f32[20]{0:T(128)S(1)} %copy-done.5, bf16[20,64,640]{2,1,0:T(8,128)(2,1)S(1)} %bitcast.18, s32[640]{0:T(1024)S(1)} %copy-done.2, bf16[16,64]{1,0:T(8,128)(2,1)S(1)} %copy-done.3), custom_call_target="tpu_custom_call" | custom-call | tf_op jit(solution)/shard_map/pallas_call | solution.py:280
  6.7 0.0 copy-start.4
  6.7 60.4 %all_to_all.10 = bf16[256,13,2,128]{3,2,1,0:T(2,128)(2,1)S(1)} all-to-all(bf16[256,13,2,128]{3,2,1,0:T(2,128)(2,1)S(1)} %bitcast.19), channel_id=1, replica_groups={{0,1,2,3,4,5,6,7,8,9,10,11,12,13,14,15,16,17,18,19,20,21,22,23,24,25,26..., dimensions={0} | all-to-all | bytes 3407872 | tf_op jit(solution)/shard_map/all_to_all | solution.py:351
  67.1 0.0 copy-done
  67.1 0.0 copy-done.4
  67.1 7.8 %shard_map.87 = (bf16[5,32,640]{2,1,0:T(8,128)(2,1)S(1)}, bf16[5,32,640]{2,1,0:T(8,128)(2,1)S(1)}, bf16[5,32,640]{2,1,0:T(8,128)(2,1)S(1)}, bf16[5,32,640]{2,1,0:T(8,128)(2,1)S(1)}, bf16[6656,128]{1,0:T(8,128)(2,1)}) custom-call(s32[2]{0:T(128)S(1)} %pad_add_fusion.place, s32[640]{0:T(1024)S(1)} %copy-done.2, bf16[6656,128]{1,0:T(8,128)(2,1)S(1)} %bitcast.17, ...), custom_call_target="tpu_custom_call" | custom-call | tf_op jit(solution)/shard_map/pallas_call | solution.py:280
  75.0 7.0 %all-to-all-start.1 = ((bf16[256,13,2,128]{3,2,1,0:T(2,128)(2,1)}), bf16[256,13,2,128]{3,2,1,0:T(2,128)(2,1)S(1)}, u32[]{:S(2)}, u32[]{:S(2)}) async-start(bf16[256,13,2,128]{3,2,1,0:T(2,128)(2,1)} %bitcast.13), calls=%async_computation.1 | async-start | bytes 3407872 | tf_op jit(solution)/shard_map/all_to_all | solution.py:351
  82.0 1.7 %collective-permute-start = (bf16[5,32,640]{2,1,0:T(8,128)(2,1)S(1)}, bf16[5,32,640]{2,1,0:T(8,128)(2,1)}, u32[]{:S(2)}, u32[]{:S(2)}) collective-permute-start(bf16[5,32,640]{2,1,0:T(8,128)(2,1)S(1)} %get-tuple-element.11), channel_id=1, source_target_pairs={{0,1},{1,2},{2,3},{3,0},{4,5},{5,6},{6,7},{7,4},{8,9},{9,10},{10,1... | collective-permute-start | bytes 614408 | tf_op jit(solution)/shard_map/ppermute | solution.py:362
  83.6 2.4 %collective-permute-start.1 = (bf16[5,32,640]{2,1,0:T(8,128)(2,1)S(1)}, bf16[5,32,640]{2,1,0:T(8,128)(2,1)}, u32[]{:S(2)}, u32[]{:S(2)}) collective-permute-start(bf16[5,32,640]{2,1,0:T(8,128)(2,1)S(1)} %get-tuple-element.12), channel_id=1, source_target_pairs={{0,2},{1,3},{2,0},{3,1},{4,6},{5,7},{6,4},{7,5},{8,10},{9,11},{10,... | collective-permute-start | bytes 614408 | tf_op jit(solution)/shard_map/ppermute | solution.py:362
  86.0 1.2 collective-permute-start.2
  87.2 3.5 %collective-permute-done = bf16[5,32,640]{2,1,0:T(8,128)(2,1)} collective-permute-done((bf16[5,32,640]{2,1,0:T(8,128)(2,1)S(1)}, bf16[5,32,640]{2,1,0:T(8,128)(2,1)}, u32[]{:S(2)}, u32[]{:S(2)}) %collective-permute-start) | collective-permute-done | bytes 204832 | tf_op jit(solution)/shard_map/ppermute | solution.py:362
  90.7 10.7 %collective-permute-done.1 = bf16[5,32,640]{2,1,0:T(8,128)(2,1)} collective-permute-done((bf16[5,32,640]{2,1,0:T(8,128)(2,1)S(1)}, bf16[5,32,640]{2,1,0:T(8,128)(2,1)}, u32[]{:S(2)}, u32[]{:S(2)}) %collective-permute-start.1) | collective-permute-done | bytes 204832 | tf_op jit(solution)/shard_map/ppermute | solution.py:362
  101.4 0.0 collective-permute-done.2
  101.4 1.2 pad_maximum_fusion
  102.7 0.1 constant_dynamic-slice_fusion.3
  102.8 0.1 pad_maximum_fusion.1
  102.9 1.5 %copy.10 = bf16[2,5,2,16,2,640]{5,4,3,2,1,0:T(2,128)(2,1)} copy(bf16[2,5,2,16,2,640]{5,3,4,1,0,2:T(8,128)(2,1)S(1)} %bitcast.21) | data formatting | bytes 1638400 | tf_op jit(solution)/shard_map/transpose | solution.py:367
  104.5 22.5 %all-to-all-done.1 = bf16[256,13,2,128]{3,2,1,0:T(2,128)(2,1)S(1)} async-done(((bf16[256,13,2,128]{3,2,1,0:T(2,128)(2,1)}), bf16[256,13,2,128]{3,2,1,0:T(2,128)(2,1)S(1)}, u32[]{:S(2)}, u32[]{:S(2)}) %all-to-all-start.1) | async-done | bytes 1703968 | tf_op jit(solution)/shard_map/all_to_all | solution.py:351
  127.0 4.5 %shard_map.88 = bf16[20,2,16,2,640]{4,3,2,1,0:T(2,128)(2,1)} custom-call(s32[2]{0:T(128)S(1)} %pad_add_fusion.place, s32[1280]{0:T(1024)S(1)} %copy-done.1, bf16[6656,128]{1,0:T(8,128)(2,1)S(1)} %bitcast.16, bf16[640,640]{1,0:T(8,128)(2,1)S(1)} %get-tuple-element.15.hot), custom_call_target="tpu_custom_call" | custom-call | tf_op jit(solution)/shard_map/pallas_call | solution.py:280
Async XLA Ops:
  0.6 2.0 %copy-start.2 = (s32[640]{0:T(1024)S(1)}, s32[640]{0:T(1024)}, u32[]{:S(2)}) copy-start(s32[640]{0:T(1024)} %folded.3) | copy-start | bytes 7684
  0.6 2.0 %copy-start.3 = (bf16[16,64]{1,0:T(8,128)(2,1)S(1)}, bf16[16,64]{1,0:T(8,128)(2,1)}, u32[]{:S(2)}) copy-start(bf16[16,64]{1,0:T(8,128)(2,1)} %vertical.1) | copy-start | bytes 6148
  0.7 2.0 %copy-start.5 = (f32[20]{0:T(128)S(1)}, f32[20]{0:T(128)}, u32[]{:S(2)}) copy-start(f32[20]{0:T(128)} %quad.1) | copy-start | bytes 244
  0.7 2.0 %copy-start.1 = (s32[1280]{0:T(1024)S(1)}, s32[1280]{0:T(1024)}, u32[]{:S(2)}) copy-start(s32[1280]{0:T(1024)} %counts.3) | copy-start | bytes 15364
  0.7 66.5 %copy-start = (bf16[10,640,640]{2,1,0:T(8,128)(2,1)S(1)}, bf16[10,640,640]{2,1,0:T(8,128)(2,1)}, u32[]{:S(2)}) copy-start(bf16[10,640,640]{2,1,0:T(8,128)(2,1)} %table.1) | copy-start | bytes 24576004
  6.7 60.4 %copy-start.4 = (f32[640]{0:T(1024)S(1)}, f32[640]{0:T(1024)}, u32[]{:S(2)}) copy-start(f32[640]{0:T(1024)} %damping.1) | copy-start | bytes 7684
  75.0 52.0 %all-to-all-start.1 = ((bf16[256,13,2,128]{3,2,1,0:T(2,128)(2,1)}), bf16[256,13,2,128]{3,2,1,0:T(2,128)(2,1)S(1)}, u32[]{:S(2)}, u32[]{:S(2)}) async-start(bf16[256,13,2,128]{3,2,1,0:T(2,128)(2,1)} %bitcast.13), calls=%async_computation.1 | async-start | bytes 3407872 | tf_op jit(solution)/shard_map/all_to_all | solution.py:351
  82.0 8.7 %collective-permute-start = (bf16[5,32,640]{2,1,0:T(8,128)(2,1)S(1)}, bf16[5,32,640]{2,1,0:T(8,128)(2,1)}, u32[]{:S(2)}, u32[]{:S(2)}) collective-permute-start(bf16[5,32,640]{2,1,0:T(8,128)(2,1)S(1)} %get-tuple-element.11), channel_id=1, source_target_pairs={{0,1},{1,2},{2,3},{3,0},{4,5},{5,6},{6,7},{7,4},{8,9},{9,10},{10,1... | collective-permute-start | bytes 614408 | tf_op jit(solution)/shard_map/ppermute | solution.py:362
  83.6 17.8 %collective-permute-start.1 = (bf16[5,32,640]{2,1,0:T(8,128)(2,1)S(1)}, bf16[5,32,640]{2,1,0:T(8,128)(2,1)}, u32[]{:S(2)}, u32[]{:S(2)}) collective-permute-start(bf16[5,32,640]{2,1,0:T(8,128)(2,1)S(1)} %get-tuple-element.12), channel_id=1, source_target_pairs={{0,2},{1,3},{2,0},{3,1},{4,6},{5,7},{6,4},{7,5},{8,10},{9,11},{10,... | collective-permute-start | bytes 614408 | tf_op jit(solution)/shard_map/ppermute | solution.py:362
  86.0 15.4 %collective-permute-start.2 = (bf16[5,32,640]{2,1,0:T(8,128)(2,1)S(1)}, bf16[5,32,640]{2,1,0:T(8,128)(2,1)}, u32[]{:S(2)}, u32[]{:S(2)}) collective-permute-start(bf16[5,32,640]{2,1,0:T(8,128)(2,1)S(1)} %get-tuple-element.13), channel_id=1, source_target_pairs={{0,3},{1,0},{2,1},{3,2},{4,7},{5,4},{6,5},{7,6},{8,11},{9,8},{10,9... | collective-permute-start | bytes 614408 | tf_op jit(solution)/shard_map/ppermute | solution.py:362
